TPU v7x, 32 devices: a whole 2x2x4 slice. The times are simulated.
32 devices in a mesh: runs: 2 (over y), slab: 4 (over z), pencil: 2 (over x), sub: 2 (over core).
Axes of the slice: x: 2, y: 2, z: 4, core: 2. Of those that a mesh axis runs over, the one named last changes fastest.
Arguments:
- masses: bfloat16 [262144], P(('runs', 'slab', 'pencil', 'sub')), parts along dimension 0, may hold values from 0.5 to 2
- velocity: float32 [3, 262144], P(None, ('runs', 'slab', 'pencil', 'sub')), parts along dimension 1, may hold values from -6 to 6
- dest_slab: int32 [262144, 1], P(('runs', 'slab', 'pencil', 'sub')), parts along dimension 0, may hold values from 0 to 3; in each aligned block of 8192 rows (0 to 8191, 8192 to 16383, ...) at most 4096 rows name the same one
- dest_cell: int32 [262144], P(('runs', 'slab', 'pencil', 'sub')), parts along dimension 0, may hold values from 0 to 8191
- w_first: bfloat16 [8, 27], replicated, may hold values from -1.25 to 1.25
- w_middle: bfloat16 [8, 216], replicated, may hold values from -0.4375 to 0.4375
- w_last: bfloat16 [3, 216], replicated, may hold values from -0.4375 to 0.4375
- step_size: float32 [1], replicated, may hold values from 0.5 to 2
- cotangent: float32 [3, 262144], P(None, ('runs', 'slab', 'pencil', 'sub')), parts along dimension 1, may hold values from -6 to 6
Outputs:
- velocity_new: float32 [3, 262144], P(None, ('runs', 'slab', 'pencil', 'sub')), parts along dimension 1
- grad_mass: bfloat16 [262144], P(('runs', 'slab', 'pencil', 'sub')), parts along dimension 0
- grad_first: float32 [16, 27], P('runs'), parts along dimension 0
- grad_middle: float32 [16, 216], P('runs'), parts along dimension 0
- grad_last: float32 [6, 216], P('runs'), parts along dimension 0
There are 2 independent parts, one for each index of `runs`. A program takes and returns all parts, laid end to end along the dimension named above; an argument that names none is the same for every part. Nothing has to cross between parts.
Inputs may be any that keep to these rules, and one draw needn't show every extreme that they name: `dest_slab`: among the rows of one device, at most 4096 name the same slab.
All inputs are finite; a program needn't handle non-finite values.
Results may differ from a plain program's by a relative error of at most 0.011.
Values may be sent and summed in bfloat16 or wider, within the bound.
No kernel may reach another device: no remote copies, remote signals or barrier semaphores. Data moves between devices by JAX's collectives and lax.ppermute only.
A program may use at most 64 MiB of HBM per device.

v0:
```python
import math

import jax
import jax.numpy as jnp
from jax import lax
from jax.sharding import PartitionSpec as P

ZL = 4
YL = 8
XL = 256


def with_halo(shard, sides, width):
    for axis, dim in sides:
        devices, length = (lax.axis_size(axis), shard.shape[dim])
        up = [(i, (i + 1) % devices) for i in range(devices)]
        down = [(j, i) for i, j in up]
        last = lax.slice_in_dim(shard, length - width, length, axis=dim)
        initial = lax.slice_in_dim(shard, 0, width, axis=dim)
        before = lax.ppermute(last, axis, up)
        after = lax.ppermute(initial, axis, down)
        shard = jnp.concatenate([before, shard, after], axis=dim)
    return shard


def silu_slope(pre):
    sigma = jax.nn.sigmoid(pre)
    return sigma * (1.0 + pre * (1.0 - sigma))


def plane_patches(padded, shift_z):
    depth_in = padded.shape[1]
    rows_in = padded.shape[2]
    pieces = []
    for shift_y in (-1, 0, 1):
        for shift_x in (-1, 0, 1):
            window = padded[
                :, 1 + shift_z : depth_in - 1 + shift_z, 1 + shift_y : rows_in - 1 + shift_y, :
            ]
            if shift_x != 0:
                window = jnp.roll(window, -shift_x, axis=3)
            pieces.append(window)
    return jnp.stack(pieces, axis=0).reshape(9 * padded.shape[0], -1)


def conv_apply(padded, weight):
    in_channels = padded.shape[0]
    result = None
    for shift_z in (-1, 0, 1):
        first_col = (shift_z + 1) * 9 * in_channels
        weight_cols = weight[:, first_col : first_col + 9 * in_channels]
        term = jnp.dot(
            weight_cols, plane_patches(padded, shift_z), preferred_element_type=jnp.float32
        )
        result = term if result is None else result + term
    return result


def weight_grad(padded, delta):
    pieces = []
    for shift_z in (-1, 0, 1):
        pieces.append(
            lax.dot_general(
                delta,
                plane_patches(padded, shift_z),
                (((1,), (1,)), ((), ())),
                preferred_element_type=jnp.float32,
            )
        )
    return jnp.concatenate(pieces, axis=1)


def back_input(padded_grad, weight):
    out_channels = weight.shape[0]
    in_channels = weight.shape[1] // 27
    flipped = (
        weight.reshape(out_channels, 27, in_channels)[:, ::-1, :]
        .transpose(2, 1, 0)
        .reshape(in_channels, 27 * out_channels)
    )
    return conv_apply(padded_grad, flipped)


def slot_tables(owner_cells, offset, block_rows):
    piece_cells = lax.dynamic_slice_in_dim(owner_cells, offset, block_rows, 0)
    tile_hot = (piece_cells[:, None] // XL == jnp.arange(ZL * YL, dtype=jnp.int32)[None, :]).astype(
        jnp.bfloat16
    )
    lane_hot = (piece_cells[:, None] % XL == jnp.arange(XL, dtype=jnp.int32)[None, :]).astype(
        jnp.bfloat16
    )
    return (tile_hot, lane_hot)


def paint_slots(values, owner_cells):
    slot_total = values.shape[1]
    block_rows = math.gcd(slot_total, 1024)

    def add_block(running, turn_index):
        offset = turn_index * block_rows
        tile_hot, lane_hot = slot_tables(owner_cells, offset, block_rows)
        values_part = lax.dynamic_slice_in_dim(values, offset, block_rows, 1)
        weighted = values_part[:, :, None] * tile_hot[None, :, :]
        return (
            running
            + jnp.einsum("kst,sl->ktl", weighted, lane_hot, preferred_element_type=jnp.float32),
            None,
        )

    initial = jnp.zeros((values.shape[0], ZL * YL, XL), jnp.float32)
    painted, unused = lax.scan(
        add_block, initial, jnp.arange(slot_total // block_rows, dtype=jnp.int32)
    )
    return painted


def readout(mesh_field, owner_cells):
    valid = owner_cells >= 0
    safe_cells = jnp.where(valid, owner_cells, 0)
    picked = jnp.take(mesh_field, safe_cells, axis=1)
    return jnp.where(valid[None, :], picked, jnp.zeros_like(picked))


def planes(field):
    return with_halo(field, (("slab", 1), (("pencil", "sub"), 2)), 1)


def grad_planes(field):
    return with_halo(field, (("slab", 1), (("pencil", "sub"), 2)), 1)


def activate(pre, channels, depth_in, rows_in):
    return jax.nn.silu(pre).astype(jnp.bfloat16).reshape(channels, depth_in, rows_in, XL)


def local(masses, velocity, dest_slab, dest_cell, w_first, w_middle, w_last, step_size, cotangent):
    particles_here = masses.shape[0]
    slab_count = lax.axis_size("slab")
    slot_count = 2 * particles_here // slab_count
    buffer_len = slab_count * slot_count
    channels = w_first.shape[0]
    target = dest_slab[:, 0]
    member = (target[:, None] == jnp.arange(slab_count, dtype=jnp.int32)[None, :]).astype(jnp.int32)
    before = jnp.cumsum(member, axis=0) - member
    placed = target * slot_count + jnp.sum(before * member, axis=1)
    mass_rows = jnp.zeros((1, buffer_len), jnp.bfloat16).at[0, placed].set(masses)
    cell_rows = jnp.full((1, buffer_len), -1, jnp.int32).at[0, placed].set(dest_cell)
    pushed = (step_size[0] * cotangent).astype(jnp.bfloat16)
    push_rows = jnp.zeros((3, buffer_len), jnp.bfloat16).at[:, placed].set(pushed)
    arrived_mass, arrived_cell = (
        lax.all_to_all(mass_rows, "slab", split_axis=1, concat_axis=1, tiled=True),
        lax.all_to_all(cell_rows, "slab", split_axis=1, concat_axis=1, tiled=True),
    )
    owner_cells = arrived_cell[0]
    density = paint_slots(arrived_mass, owner_cells).astype(jnp.bfloat16).reshape(1, ZL, YL, XL)
    padded_zero = planes(density)
    pre_one = conv_apply(padded_zero, w_first)
    padded_one = planes(activate(pre_one, channels, ZL, YL))
    pre_two = conv_apply(padded_one, w_middle)
    padded_two = planes(activate(pre_two, channels, ZL, YL))
    force_mesh = conv_apply(padded_two, w_last).astype(jnp.bfloat16)
    slot_force = readout(force_mesh, owner_cells)
    returned = lax.all_to_all(slot_force, "slab", split_axis=1, concat_axis=1, tiled=True)
    arrived_push = lax.all_to_all(push_rows, "slab", split_axis=1, concat_axis=1, tiled=True)
    grad_force = paint_slots(arrived_push, owner_cells).astype(jnp.bfloat16).reshape(3, -1)
    grad_last = weight_grad(padded_two, grad_force)
    back_two = back_input(grad_planes(grad_force.reshape(3, ZL, YL, XL)), w_last)
    delta_two = (back_two * silu_slope(pre_two)).astype(jnp.bfloat16)
    grad_middle = weight_grad(padded_one, delta_two)
    back_one = back_input(grad_planes(delta_two.reshape(channels, ZL, YL, XL)), w_middle)
    delta_one = (back_one * silu_slope(pre_one)).astype(jnp.bfloat16)
    grad_first = weight_grad(padded_zero, delta_one)
    density_grad = back_input(grad_planes(delta_one.reshape(channels, ZL, YL, XL)), w_first).astype(
        jnp.bfloat16
    )
    slot_grad = readout(density_grad, owner_cells)
    grad_back = lax.all_to_all(slot_grad, "slab", split_axis=1, concat_axis=1, tiled=True)
    velocity_new = velocity + step_size[0] * returned[:, placed].astype(jnp.float32)
    grad_mass = grad_back[0, placed]
    cell_total = ZL * YL * XL * slab_count * lax.axis_size("pencil") * lax.axis_size("sub")
    summed = lax.psum((grad_first, grad_middle, grad_last), ("slab", "pencil", "sub"))
    scale = 1.0 / math.sqrt(cell_total)
    return (velocity_new, grad_mass, summed[0] * scale, summed[1] * scale, summed[2] * scale)


def solution(mesh):
    placed = (
        P(("runs", "slab", "pencil", "sub")),
        P(None, ("runs", "slab", "pencil", "sub")),
        P(("runs", "slab", "pencil", "sub"), None),
        P(("runs", "slab", "pencil", "sub")),
        P(),
        P(),
        P(),
        P(),
        P(None, ("runs", "slab", "pencil", "sub")),
    )
    return jax.shard_map(
        local,
        mesh=mesh,
        in_specs=placed,
        out_specs=(
            P(None, ("runs", "slab", "pencil", "sub")),
            P(("runs", "slab", "pencil", "sub")),
            P("runs", None),
            P("runs", None),
            P("runs", None),
        ),
        check_vma=False,
    )
```

profile of v0, /device:TPU:0, one launch (start us, length us, event | category | flops | bytes accessed | tf_op | source)
XLA Modules:
  0.0 662.3 jit_solution(6886009132037439011)
XLA Ops:
  5.4 56.8 %scatter_custom_fusion.2 = bf16[16384]{0:T(1024)(128)(2,1)S(1)} fusion(s32[8192]{0:T(1024)S(1)} %broadcast_select_fusion, bf16[8192]{0:T(1024)(128)(2,1)} %param.13, bf16[]{:T(256)} %constant.181.clone.1), kind=kCustom, calls=%fused_computation.587 | custom fusion | bytes 33280
  64.2 6.3 all-to-all-start.1
  71.3 31.2 %scatter_custom_fusion.1 = s32[16384]{0:T(1024)} fusion(s32[8192]{0:T(1024)S(1)} %broadcast_select_fusion, s32[8192]{0:T(1024)} %param.16, s32[]{:T(128)} %constant.174.clone.1), kind=kCustom, calls=%fused_computation.522 | custom fusion | bytes 66048
  102.5 5.1 all-to-all-start
  109.3 23.8 %scatter_custom_fusion = bf16[3,16384]{0,1:T(8,128)(2,1)} fusion(s32[8192]{0:T(1024)S(1)} %bitcast.879, bf16[8192,3]{1,0:T(8,128)(2,1)S(1)} %copy.44, bf16[]{:T(256)} %constant.181.clone.1), kind=kCustom, calls=%fused_computation.65 | custom fusion | bytes 98306 | tf_op jit(solution)/shard_map/scatter | solution.py:149
  133.0 4.4 copy.45
  143.0 5.3 all-to-all-start.3
  148.3 33.0 %while.26 = (s32[]{:T(128)}, f32[1,32,256]{2,1,0:T(8,128)S(1)}, s32[16]{0:T(128)S(1)}, s32[16384]{0:T(1024)S(1)}, bf16[1,16384]{1,0:T(2,128)(2,1)S(1)}, /*index=5*/s32[]{:T(128)}, s32[1]{0:T(128)}, s32[]{:T(128)}, s32[]{:T(128)}) while((s32[]{:T(128)}, f32[1,32,256]{2,1,0:T(8,128)S(1)}, s32[16]{0:T(128)S(1)}, s32[16384]{0:T(1024)S(1)}, ...), condition=%wide.region_6.7_spmd.clone, body=%wide.region_5.6_spmd.clone.sunk | while | flops 17146888 | bytes 98477 | solution.py:111
  203.3 28.3 %while.27 = (s32[]{:T(128)}, f32[3,32,256]{2,1,0:T(8,128)S(1)}, s32[16]{0:T(128)S(1)}, bf16[3,16384]{1,0:T(4,128)(2,1)S(1)}, s32[16384]{0:T(1024)S(1)}, /*index=5*/s32[]{:T(128)}, s32[1]{0:T(128)}, s32[]{:T(128)}, s32[]{:T(128)}) while((s32[]{:T(128)}, f32[3,32,256]{2,1,0:T(8,128)S(1)}, s32[16]{0:T(128)S(1)}, ...), condition=%wide.region_9.10_spmd.clone, body=%wide.region_8.9_spmd.clone.sunk | while | flops 50832392 | bytes 372909 | solution.py:111
  246.4 2.7 collective-permute-start.9
  271.5 4.0 collective-permute-start.17
  289.1 57.4 %gather_fusion = bf16[16384,3]{1,0:T(8,128)(2,1)} fusion(bf16[3,8192]{0,1:T(8,128)(2,1)S(1)} %copy.38, s32[16384]{0:T(1024)S(1)} %broadcast_clamp_fusion), kind=kCustom, calls=%fused_computation | custom fusion | bytes 262144 | tf_op jit(solution)/shard_map/jit(_take)/gather | solution.py:120
  346.5 3.8 copy.39
  357.8 3.8 collective-permute-start.21
  361.7 58.2 %all-reduce.1 = (f32[8,27]{1,0:T(8,128)S(1)}, f32[8,216]{1,0:T(8,128)S(1)}, f32[3,216]{1,0:T(4,128)S(1)}) all-reduce(f32[8,27]{1,0:T(8,128)S(1)} %pad_maximum_fusion.37, f32[8,216]{1,0:T(8,128)S(1)} %pad_maximum_fusion.33, ...), channel_id=1, replica_groups=mesh['runs'=2,'slab'=4,'pencil'=2,'sub'=2] {'slab','pencil','sub'}, use_global_device_ids=true, to_apply=%region_10.11 | all-reduce | flops 2592 | bytes 20736 | tf_op jit(solution)/shard_map/psum | solution.py:181
  427.9 100.9 %gather_fusion.2 = bf16[16384]{0:T(1024)(128)(2,1)S(1)} fusion(bf16[8192]{0:T(1024)(128)(2,1)S(1)} %add_convert_fusion, s32[16384]{0:T(1024)S(1)} %broadcast_clamp_fusion), kind=kCustom, calls=%fused_computation.2 | custom fusion | bytes 131072 | tf_op jit(solution)/shard_map/jit(_take)/gather | solution.py:120
  530.4 3.3 all-to-all-start.4
  534.3 5.0 all-to-all-done.4
  539.3 3.3 all-to-all-start.2
  543.3 82.5 %gather_fusion.3 = bf16[8192]{0:T(1024)(128)(2,1)} fusion(bf16[1,16384]{1,0:T(2,128)(2,1)S(1)} %bitcast.813, s32[8192]{0:T(1024)S(1)} %bitcast.814), kind=kCustom, calls=%fused_computation.3 | custom fusion | bytes 98304 | tf_op jit(solution)/shard_map/gather | solution.py:179
  625.8 3.4 copy.40
  629.2 24.6 %gather_fusion.1 = bf16[8192,3]{1,0:T(8,128)(2,1)S(1)} fusion(bf16[3,16384]{0,1:T(8,128)(2,1)} %bitcast.852, s32[8192]{0:T(1024)S(1)} %copy-done.21), kind=kCustom, calls=%fused_computation.1 | custom fusion | bytes 131072 | tf_op jit(solution)/shard_map/gather | solution.py:178
  653.8 4.6 bitcast_add_fusion
  658.4 3.5 copy.50
  (594 shorter events, 142.6 us)
Async XLA Ops:
  64.2 38.3 %all-to-all-start.1 = ((bf16[4,2,2048]{2,1,0:T(2,128)(2,1)}), bf16[4,2,2048]{2,1,0:T(2,128)(2,1)S(1)}, u32[]{:S(2)}, u32[]{:S(2)}) async-start(bf16[4,2,2048]{2,1,0:T(2,128)(2,1)} %reshape.471), calls=%async_computation.1 | async-start | bytes 65536 | tf_op jit(solution)/shard_map/all_to_all | solution.py:151
  102.5 40.5 %all-to-all-start = ((s32[1,4,4096]{2,0,1:T(1,128)}), s32[1,4,4096]{2,0,1:T(1,128)S(1)}, u32[]{:S(2)}, u32[]{:S(2)}) async-start(s32[1,4,4096]{2,0,1:T(1,128)} %bitcast.5), calls=%async_computation | async-start | bytes 131072 | tf_op jit(solution)/shard_map/all_to_all | solution.py:152
  143.0 60.3 %all-to-all-start.3 = ((bf16[3,4,4096]{2,0,1:T(4,128)(2,1)}), bf16[3,4,4096]{2,0,1:T(4,128)(2,1)S(1)}, u32[]{:S(2)}, u32[]{:S(2)}) async-start(bf16[3,4,4096]{2,0,1:T(4,128)(2,1)} %copy.45), calls=%async_computation.3 | async-start | bytes 262144 | tf_op jit(solution)/shard_map/all_to_all | solution.py:164
  181.3 5.5 collective-permute-start
  194.6 5.9 collective-permute-start.4
  196.1 4.4 collective-permute-start.5
  200.5 38.7 %collective-permute-start.6 = (bf16[8,6,1,256]{3,0,2,1:T(8,128)(2,1)S(1)}, bf16[8,6,1,256]{3,0,2,1:T(8,128)(2,1)S(1)}, u32[]{:S(2)}, u32[]{:S(2)}) collective-permute-start(bf16[8,6,1,256]{3,0,2,1:T(8,128)(2,1)S(1)} %get-tuple-element.363), channel_id=1, source_target_pairs={{0,1},{1,2},{2,3},{3,0},{4,5},{5,6},{6,7},{7,4},{8,9},{9,10},{10,1... | collective-permute-start | bytes 73736 | tf_op jit(solution)/shard_map/ppermute | solution.py:20
  201.1 38.1 %collective-permute-start.7 = (bf16[8,6,1,256]{3,0,2,1:T(8,128)(2,1)S(1)}, bf16[8,6,1,256]{3,0,2,1:T(8,128)(2,1)S(1)}, u32[]{:S(2)}, u32[]{:S(2)}) collective-permute-start(bf16[8,6,1,256]{3,0,2,1:T(8,128)(2,1)S(1)} %get-tuple-element.362), channel_id=1, source_target_pairs={{1,0},{2,1},{3,2},{0,3},{5,4},{6,5},{7,6},{4,7},{9,8},{10,9},{11,1... | collective-permute-start | bytes 73736 | tf_op jit(solution)/shard_map/ppermute | solution.py:21
  231.6 5.5 collective-permute-start.12
  233.1 4.0 collective-permute-start.13
  237.2 12.0 %collective-permute-start.14 = (bf16[3,6,1,256]{3,2,1,0:T(2,128)(2,1)S(1)}, bf16[3,6,1,256]{3,2,1,0:T(2,128)(2,1)S(1)}, u32[]{:S(2)}, u32[]{:S(2)}) collective-permute-start(bf16[3,6,1,256]{3,2,1,0:T(2,128)(2,1)S(1)} %get-tuple-element.465), channel_id=1, source_target_pairs={{0,1},{1,2},{2,3},{3,0},{4,5},{5,6},{6,7},{7,4},{8,9},{9,10},{10,1... | collective-permute-start | bytes 27656 | tf_op jit(solution)/shard_map/ppermute | solution.py:20
  237.2 11.9 %collective-permute-start.15 = (bf16[3,6,1,256]{3,2,1,0:T(2,128)(2,1)S(1)}, bf16[3,6,1,256]{3,2,1,0:T(2,128)(2,1)S(1)}, u32[]{:S(2)}, u32[]{:S(2)}) collective-permute-start(bf16[3,6,1,256]{3,2,1,0:T(2,128)(2,1)S(1)} %get-tuple-element.464), channel_id=1, source_target_pairs={{1,0},{2,1},{3,2},{0,3},{5,4},{6,5},{7,6},{4,7},{9,8},{10,9},{11,1... | collective-permute-start | bytes 27656 | tf_op jit(solution)/shard_map/ppermute | solution.py:21
  245.3 30.3 %collective-permute-start.8 = (bf16[8,1,8,256]{3,0,2,1:T(8,128)(2,1)}, bf16[8,1,8,256]{3,0,2,1:T(8,128)(2,1)S(1)}, u32[]{:S(2)}, u32[]{:S(2)}) collective-permute-start(bf16[8,1,8,256]{3,0,2,1:T(8,128)(2,1)} %get-tuple-element.446), channel_id=1, source_target_pairs={{0,4},{4,8},{8,12},{12,0},{1,5},{5,9},{9,13},{13,1},{2,6},{6,10},{... | collective-permute-start | bytes 98312 | tf_op jit(solution)/shard_map/ppermute | solution.py:20
  246.4 29.2 %collective-permute-start.9 = (bf16[8,1,8,256]{3,0,2,1:T(8,128)(2,1)}, bf16[8,1,8,256]{3,0,2,1:T(8,128)(2,1)S(1)}, u32[]{:S(2)}, u32[]{:S(2)}) collective-permute-start(bf16[8,1,8,256]{3,0,2,1:T(8,128)(2,1)} %get-tuple-element.447), channel_id=1, source_target_pairs={{4,0},{8,4},{12,8},{0,12},{5,1},{9,5},{13,9},{1,13},{6,2},{10,6},{... | collective-permute-start | bytes 98312 | tf_op jit(solution)/shard_map/ppermute | solution.py:21
  271.5 6.3 collective-permute-start.16
  271.5 6.3 collective-permute-start.17
  275.6 6.2 collective-permute-start.10
  275.7 6.2 collective-permute-start.11
  278.4 72.8 %collective-permute-start.18 = (bf16[8,6,1,256]{3,0,2,1:T(8,128)(2,1)}, bf16[8,6,1,256]{3,0,2,1:T(8,128)(2,1)}, u32[]{:S(2)}, u32[]{:S(2)}) collective-permute-start(bf16[8,6,1,256]{3,0,2,1:T(8,128)(2,1)} %get-tuple-element.355), channel_id=1, source_target_pairs={{0,1},{1,2},{2,3},{3,0},{4,5},{5,6},{6,7},{7,4},{8,9},{9,10},{10,1... | collective-permute-start | bytes 73736 | tf_op jit(solution)/shard_map/ppermute | solution.py:20
  278.6 72.7 %collective-permute-start.19 = (bf16[8,6,1,256]{3,0,2,1:T(8,128)(2,1)}, bf16[8,6,1,256]{3,0,2,1:T(8,128)(2,1)}, u32[]{:S(2)}, u32[]{:S(2)}) collective-permute-start(bf16[8,6,1,256]{3,0,2,1:T(8,128)(2,1)} %get-tuple-element.354), channel_id=1, source_target_pairs={{1,0},{2,1},{3,2},{0,3},{5,4},{6,5},{7,6},{4,7},{9,8},{10,9},{11,1... | collective-permute-start | bytes 73736 | tf_op jit(solution)/shard_map/ppermute | solution.py:21
  357.8 62.7 %collective-permute-start.20 = (bf16[8,1,8,256]{3,0,2,1:T(8,128)(2,1)S(1)}, bf16[8,1,8,256]{3,0,2,1:T(8,128)(2,1)S(1)}, u32[]{:S(2)}, u32[]{:S(2)}) collective-permute-start(bf16[8,1,8,256]{3,0,2,1:T(8,128)(2,1)S(1)} %get-tuple-element.422), channel_id=1, source_target_pairs={{0,4},{4,8},{8,12},{12,0},{1,5},{5,9},{9,13},{13,1},{2,6},{6,10},{... | collective-permute-start | bytes 98312 | tf_op jit(solution)/shard_map/ppermute | solution.py:20
  357.8 62.7 %collective-permute-start.21 = (bf16[8,1,8,256]{3,0,2,1:T(8,128)(2,1)S(1)}, bf16[8,1,8,256]{3,0,2,1:T(8,128)(2,1)S(1)}, u32[]{:S(2)}, u32[]{:S(2)}) collective-permute-start(bf16[8,1,8,256]{3,0,2,1:T(8,128)(2,1)S(1)} %get-tuple-element.423), channel_id=1, source_target_pairs={{4,0},{8,4},{12,8},{0,12},{5,1},{9,5},{13,9},{1,13},{6,2},{10,6},{... | collective-permute-start | bytes 98312 | tf_op jit(solution)/shard_map/ppermute | solution.py:21
  530.4 8.9 %all-to-all-start.4 = ((bf16[4,2,2048]{2,1,0:T(2,128)(2,1)}), bf16[4,2,2048]{2,1,0:T(2,128)(2,1)S(1)}, u32[]{:S(2)}, u32[]{:S(2)}) async-start(bf16[4,2,2048]{2,1,0:T(2,128)(2,1)} %reshape.473), calls=%async_computation.4 | async-start | bytes 65536 | tf_op jit(solution)/shard_map/all_to_all | solution.py:177
  539.3 86.4 %all-to-all-start.2 = ((bf16[3,4,4096]{2,0,1:T(4,128)(2,1)}), bf16[3,4,4096]{2,0,1:T(4,128)(2,1)S(1)}, u32[]{:S(2)}, u32[]{:S(2)}) async-start(bf16[3,4,4096]{2,0,1:T(4,128)(2,1)} %select_select_fusion), calls=%async_computation.2 | async-start | bytes 262144 | tf_op jit(solution)/shard_map/all_to_all | solution.py:163
  (44 other events, 180.7 us)
where the time goes:
time: 672 us; the launch traced here: 662 us
  local copies, waits for them, and re-layouts  441 us (66%)
  blocking collectives  58.2 us (9%)
  starting transfers between devices  57.6 us (9%)
  other arithmetic  37.6 us (6%)
  matrix products  31 us (5%)
  loops' own time  22.5 us (3%)
  waiting for transfers between devices  11.3 us (2%)
    gather x4, local copies, waits for them, and re-layouts, readout(): picked = jnp.take(mesh_field, safe_cells, axis=1)  162 us
    unnamed x130, local copies, waits for them, and re-layouts  104 us
    gather x1, local copies, waits for them, and re-layouts, local(): grad_mass = grad_back[0, placed]  82.5 us
    psum x1, blocking collectives, local(): lax.psum((grad_first, grad_middle, grad_last), ('slab', 'pencil', 'sub'))  58.2 us
    ppermute x12, starting transfers between devices, with_halo(): after = lax.ppermute(initial, axis, down)  27.1 us
    gather x1, local copies, waits for them, and re-layouts, local(): returned[:, placed].astype(jnp.float32)  24.6 us
    scatter x1, local copies, waits for them, and re-layouts, local(): jnp.zeros((3, buffer_len), jnp.bfloat16).at[:, placed].set(pushed)  23.8 us
    another operation x2, loops' own time, paint_slots(): lax.scan(add_block, initial, jnp.arange(slot_total // block_rows, dtype=j...  22.5 us
  transfers between devices with their start and end apart: 29, of which 8 were waited for; matrix products, arithmetic and copies ran while one was open for 44% of the time, Pallas kernels for 0%

commit v1 on v0

v1 whole, which is shorter than its diff:
```python
import functools
import math

import jax
import jax.numpy as jnp
import numpy as np
from jax import lax
from jax.experimental import pallas as pl
from jax.experimental.pallas import tpu as pltpu
from jax.sharding import PartitionSpec as P

ZL = 4
YL = 8
XL = 256
ROWS = ZL * YL
FIELDS = 4
BLOCK = FIELDS * ROWS
POS = 16
DEPTH = 3 * ZL
BF16 = jnp.bfloat16
F32 = jnp.float32
NT = (((1,), (1,)), ((), ()))
VMEM_LIMIT = 56 * 1024 * 1024


def dot(a, b):
    return jnp.dot(a, b, preferred_element_type=F32)


def dot_nt(a, b):
    return lax.dot_general(a, b, NT, preferred_element_type=F32)


def row_iota(shape, dim):
    return lax.broadcasted_iota(jnp.int32, shape, dim)


def paint_kernel(slabs, step_ref, mass_ref, slab_ref, cell_ref, cot_ref, *rest):
    outs, (hot, lane_hot, total) = rest[:slabs], rest[slabs:]
    turn = pl.program_id(0)
    chunk = mass_ref.shape[1]
    me = lax.axis_index("slab")
    cell = cell_ref[...]
    relative = slab_ref[...] - me
    relative = jnp.where(relative < 0, relative + slabs, relative)
    z, y = cell >> 11, (cell >> 8) & 7
    code = ((relative * 2 + (y >> 2)) << 4) + (z << 2) + (y & 3)

    def tile(row):
        return jnp.broadcast_to(row.astype(F32), (16, chunk)).astype(BF16)

    sixteen = row_iota((16, chunk), 0)
    zero = jnp.zeros((16, chunk), BF16)
    one = jnp.ones((16, chunk), BF16)
    lane = tile(cell & (XL - 1))
    for group in range(XL // 16):
        same = lane == (sixteen + 16 * group).astype(F32).astype(BF16)
        lane_hot[16 * group : 16 * group + 16, :] = jnp.where(same, one, zero)
    values = [tile(mass_ref[...])]
    for component in range(3):
        pushed = (step_ref[0] * cot_ref[component : component + 1, :]).astype(BF16)
        values.append(tile(pushed))
    for base in range(0, 2 * slabs, 16):
        local_code = jnp.clip(code - 16 * base, -1, 256)
        code_tile = tile(local_code)
        for group in range(base, min(base + 16, 2 * slabs)):
            same = code_tile == (sixteen + 16 * (group - base)).astype(F32).astype(BF16)
            for field in range(FIELDS):
                first = group * 64 + field * 16
                hot[first : first + 16, :] = jnp.where(same, values[field], zero)
    part = dot_nt(hot[...], lane_hot[...])

    @pl.when(turn == 0)
    def first_turn():
        total[...] = part

    @pl.when(turn > 0)
    def later_turn():
        total[...] += part

    @pl.when(turn == pl.num_programs(0) - 1)
    def last_turn():
        for k in range(slabs):
            outs[k][...] = total[k * BLOCK : (k + 1) * BLOCK, :].astype(outs[k].dtype)


def paint(step_size, masses, target, cells, cotangent, slabs):
    count = masses.shape[1]
    chunk = math.gcd(count, 2048)
    row = pl.BlockSpec((1, chunk), lambda i: (0, i))
    whole = pl.BlockSpec((BLOCK, XL), lambda i: (0, 0))
    return pl.pallas_call(
        functools.partial(paint_kernel, slabs),
        grid=(count // chunk,),
        in_specs=[
            pl.BlockSpec(memory_space=pltpu.SMEM),
            row,
            row,
            row,
            pl.BlockSpec((3, chunk), lambda i: (0, i)),
        ],
        out_specs=[whole] * slabs,
        out_shape=[
            jax.ShapeDtypeStruct((BLOCK, XL), F32 if k == 0 else BF16) for k in range(slabs)
        ],
        scratch_shapes=[
            pltpu.VMEM((slabs * BLOCK, chunk), BF16),
            pltpu.VMEM((XL, chunk), BF16),
            pltpu.VMEM((slabs * BLOCK, XL), F32),
        ],
        compiler_params=pltpu.CompilerParams(vmem_limit_bytes=VMEM_LIMIT),
    )(step_size, masses, target, cells, cotangent)


def tap_columns(channels):
    width = 9 * channels * POS
    col = np.arange(width)
    pair, channel = col // (channels * POS), (col // POS) % channels
    rows = [((pair // 3 * 3 + b) * 3 + pair % 3) * channels + channel for b in range(3)]
    return np.stack(rows + [np.full(width, -1)] * 5).astype(np.int32)


def tap_hot(taps, b, count):
    width = taps.shape[1]
    same = row_iota((count, width), 0) == taps[b : b + 1, :]
    return jnp.where(same, 1.0, 0.0).astype(F32)


def y_distance(rows, width):
    return (row_iota((rows, width), 1) - row_iota((rows, width), 0)) & (POS - 1)


Y_SHIFTS = (POS - 1, 0, 1)


def band(weight, taps):
    outs, count = weight.shape
    rows, width = outs * POS, taps.shape[1]
    pick = jnp.where(row_iota((rows, outs), 0) >> 4 == row_iota((rows, outs), 1), 1.0, 0.0)
    spread = dot(pick.astype(BF16), weight).astype(BF16)
    distance = y_distance(rows, width)
    result = jnp.zeros((rows, width), F32)
    for b in range(3):
        picked = dot(spread, tap_hot(taps, b, count).astype(BF16))
        result = jnp.where(distance == Y_SHIFTS[b], picked, result)
    return result


def band_kernel(
    first_ref, middle_ref, last_ref, one_ref, many_ref, b1_ref, b2_ref, b3_ref, t1_ref, t2_ref, t3_ref
):
    many = many_ref[...]
    for weight_ref, taps, b_ref, t_ref in (
        (first_ref, one_ref[...], b1_ref, t1_ref),
        (middle_ref, many, b2_ref, t2_ref),
        (last_ref, many, b3_ref, t3_ref),
    ):
        full = band(weight_ref[...], taps)
        b_ref[...] = full.astype(BF16)
        outs, ins = full.shape[0], full.shape[1] // 9
        for pair in range(9):
            block = full[:, pair * ins : (pair + 1) * ins].T.astype(BF16)
            t_ref[:, (8 - pair) * outs : (9 - pair) * outs] = block


def bands(w_first, w_middle, w_last):
    sizes = [(w.shape[0] * POS, w.shape[1] // 27 * POS) for w in (w_first, w_middle, w_last)]
    shapes = [(o, 9 * c) for o, c in sizes] + [(c, 9 * o) for o, c in sizes]
    one = tap_columns(1)
    many = tap_columns(w_middle.shape[1] // 27)
    return pl.pallas_call(
        band_kernel,
        out_shape=[jax.ShapeDtypeStruct(s, BF16) for s in shapes],
        compiler_params=pltpu.CompilerParams(vmem_limit_bytes=VMEM_LIMIT),
        cost_estimate=pl.CostEstimate(
            flops=800_000_000, bytes_accessed=4_000_000, transcendentals=0
        ),
    )(w_first, w_middle, w_last, jnp.asarray(one), jnp.asarray(many))


def lay_out(store, plane, value):
    rows = value.shape[0]
    for e, shift in enumerate((1, 0, XL - 1)):
        moved = value if shift == 0 else pltpu.roll(value, shift, 1)
        store[plane, e * rows : (e + 1) * rows, :] = moved.astype(BF16)


def window(store, plane):
    rows = store.shape[1]
    return store[plane - 1 : plane + 2].reshape(3 * rows, XL)


def centre(store, plane):
    rows = store.shape[1] // 3
    return store[plane, rows : 2 * rows, :]


def slope(pre, sigma):
    return sigma * (1.0 + pre * (1.0 - sigma))


def split_three(value):
    high = value.astype(BF16).astype(F32)
    rest = value - high
    mid = rest.astype(BF16).astype(F32)
    return jnp.concatenate([high, mid, rest - mid], axis=0).astype(BF16)


def weight_sum(full, taps, count):
    outs, width = full.shape[0] // POS, full.shape[1]
    distance = y_distance(YL, width)
    result = None
    for b in range(3):
        rows = [
            jnp.sum(
                jnp.where(distance == Y_SHIFTS[b], full[o * POS : o * POS + YL, :], 0.0),
                axis=0,
                keepdims=True,
            )
            for o in range(outs)
        ]
        rows += [jnp.zeros_like(rows[0])] * (8 - outs)
        parts = dot_nt(split_three(jnp.concatenate(rows, axis=0)), tap_hot(taps, b, count).astype(BF16))
        term = parts[0:8] + parts[8:16] + parts[16:24]
        result = term if result is None else result + term
    return result


def net_kernel(
    below_ref, own_ref, above_ref, before_ref, after_ref,
    b1_ref, b2_ref, b3_ref, t1_ref, t2_ref, t3_ref, one_ref, many_ref, order_ref,
    mesh_ref, grads_ref,
    s0, s1, s2, sg, d2, d1, slope1, slope2, fields,
):
    order = order_ref[...]
    for b, block in enumerate((below_ref, own_ref, above_ref)):
        for c in range(FIELDS):
            pieces = [
                block[c * 16 : c * 16 + 16, :],
                block[64 + c * 16 : 80 + c * 16, :],
                after_ref[b * 64 + c * 16 : b * 64 + c * 16 + 16, :],
                before_ref[b * 64 + c * 16 : b * 64 + c * 16 + 16, :],
            ]
            rows = dot(order, jnp.concatenate(pieces, axis=0))
            for z in range(ZL):
                value = rows[z * POS : (z + 1) * POS, :]
                for e, shift in enumerate((1, 0, XL - 1)):
                    moved = value if shift == 0 else pltpu.roll(value, shift, 1)
                    if c == 0:
                        s0[b * ZL + z, e * 16 : e * 16 + 16, :] = moved.astype(BF16)
                    else:
                        first = e * 48 + (c - 1) * 16
                        sg[b * ZL + z, first : first + 16, :] = moved.astype(BF16)
    b1, b2, b3 = b1_ref[...], b2_ref[...], b3_ref[...]
    t1, t2, t3 = t1_ref[...], t2_ref[...], t3_ref[...]
    for plane in range(1, DEPTH - 1):
        pre = dot(b1, window(s0, plane))
        sigma = jax.nn.sigmoid(pre)
        lay_out(s1, plane, pre * sigma)
        if 3 <= plane < DEPTH - 3:
            slope1[plane] = slope(pre, sigma)
    for plane in range(2, DEPTH - 2):
        pre = dot(b2, window(s1, plane))
        sigma = jax.nn.sigmoid(pre)
        if 3 <= plane < DEPTH - 3:
            lay_out(s2, plane, pre * sigma)
        slope2[plane] = slope(pre, sigma)
    for z in range(ZL):
        force = dot(b3, window(s2, ZL + z))
        for c in range(3):
            first = c * ROWS + z * YL
            fields[first : first + YL, :] = force[c * POS : c * POS + YL, :]
    for plane in range(2, DEPTH - 2):
        lay_out(d2, plane, dot(t3, window(sg, plane)) * slope2[plane])
    for plane in range(3, DEPTH - 3):
        lay_out(d1, plane, dot(t2, window(d2, plane)) * slope1[plane])
    for z in range(ZL):
        pull = dot(t1, window(d1, ZL + z))
        first = 3 * ROWS + z * YL
        fields[first : first + YL, :] = pull[0:YL, :]
    mesh_ref[...] = fields[...].astype(BF16)
    one, many = one_ref[...], many_ref[...]
    grads_ref[...] = jnp.zeros_like(grads_ref)
    for first, (delta, source, taps) in zip(
        (0, 8, 16), ((d1, s0, one), (d2, s1, many), (sg, s2, many))
    ):
        full = None
        for z in range(ZL):
            term = dot_nt(centre(delta, ZL + z), window(source, ZL + z))
            full = term if full is None else full + term
        count = 3 * taps.shape[1] // POS
        grads_ref[first : first + 8, 0:count] = weight_sum(full, taps, count)


def network(blocks, halves, band_list, channels):
    rows = channels * POS
    order = np.zeros((64, 64), np.float32)
    for z in range(4):
        for h in range(4):
            for y in range(4):
                order[z * 16 + h * 4 + y, h * 16 + z * 4 + y] = 1.0
    one, many = tap_columns(1), tap_columns(channels)
    return pl.pallas_call(
        net_kernel,
        out_shape=[
            jax.ShapeDtypeStruct((BLOCK, XL), BF16),
            jax.ShapeDtypeStruct((24, 256), F32),
        ],
        scratch_shapes=[
            pltpu.VMEM((DEPTH, 3 * POS, XL), BF16),
            pltpu.VMEM((DEPTH, 3 * rows, XL), BF16),
            pltpu.VMEM((DEPTH, 3 * rows, XL), BF16),
            pltpu.VMEM((DEPTH, 9 * POS, XL), BF16),
            pltpu.VMEM((DEPTH, 3 * rows, XL), BF16),
            pltpu.VMEM((DEPTH, 3 * rows, XL), BF16),
            pltpu.VMEM((DEPTH, rows, XL), F32),
            pltpu.VMEM((DEPTH, rows, XL), F32),
            pltpu.VMEM((BLOCK, XL), F32),
        ],
        compiler_params=pltpu.CompilerParams(vmem_limit_bytes=VMEM_LIMIT),
    )(*blocks, *halves, *band_list, jnp.asarray(one), jnp.asarray(many), jnp.asarray(order, BF16))


def readout_kernel(slabs, step_ref, slab_ref, cell_ref, velocity_ref, *rest):
    meshes, (velocity_out, mass_out, lane_hot) = rest[:slabs], rest[slabs:]
    chunk = cell_ref.shape[1]
    me = lax.axis_index("slab")
    cell = cell_ref[...]
    relative = slab_ref[...] - me
    relative = jnp.where(relative < 0, relative + slabs, relative)
    code = relative * ROWS + (cell >> 8)
    sixteen = row_iota((16, chunk), 0)
    zero = jnp.zeros((16, chunk), BF16)
    one = jnp.ones((16, chunk), BF16)
    lane = jnp.broadcast_to((cell & (XL - 1)).astype(F32), (16, chunk)).astype(BF16)
    for group in range(XL // 16):
        same = lane == (sixteen + 16 * group).astype(F32).astype(BF16)
        lane_hot[16 * group : 16 * group + 16, :] = jnp.where(same, one, zero)
    code_tile = jnp.broadcast_to(code, (8, chunk))
    eight = row_iota((8, chunk), 0)
    sums = [jnp.zeros((8, chunk), F32) for _ in range(FIELDS)]
    for k in range(slabs):
        rows = dot(meshes[k][...], lane_hot[...])
        for group in range(ROWS // 8):
            same = code_tile == eight + (k * ROWS + group * 8)
            for c in range(FIELDS):
                first = c * ROWS + group * 8
                sums[c] = sums[c] + jnp.where(same, rows[first : first + 8, :], 0.0)
    for c in range(3):
        force = jnp.sum(sums[c], axis=0, keepdims=True)
        velocity_out[c : c + 1, :] = velocity_ref[c : c + 1, :] + step_ref[0] * force
    mass_out[...] = jnp.sum(sums[3], axis=0, keepdims=True).astype(mass_out.dtype)


def read_out(step_size, target, cells, velocity, meshes, slabs):
    count = cells.shape[1]
    chunk = math.gcd(count, 1024)
    row = pl.BlockSpec((1, chunk), lambda i: (0, i))
    three = pl.BlockSpec((3, chunk), lambda i: (0, i))
    whole = pl.BlockSpec((BLOCK, XL), lambda i: (0, 0))
    return pl.pallas_call(
        functools.partial(readout_kernel, slabs),
        grid=(count // chunk,),
        in_specs=[pl.BlockSpec(memory_space=pltpu.SMEM), row, row, three] + [whole] * slabs,
        out_specs=[three, row],
        out_shape=[
            jax.ShapeDtypeStruct((3, count), F32),
            jax.ShapeDtypeStruct((1, count), BF16),
        ],
        scratch_shapes=[pltpu.VMEM((XL, chunk), BF16)],
        compiler_params=pltpu.CompilerParams(vmem_limit_bytes=VMEM_LIMIT),
    )(step_size, target, cells, velocity, *meshes)


def shifted(value, axis, distance):
    count = lax.axis_size(axis)
    return lax.ppermute(value, axis, [(i, (i + distance) % count) for i in range(count)])


def sum_over(value, axis):
    count = lax.axis_size(axis)
    others = [shifted(value, axis, k) for k in range(1, count)]
    return functools.reduce(jnp.add, others, value)


def local(masses, velocity, dest_slab, dest_cell, w_first, w_middle, w_last, step_size, cotangent):
    slabs = lax.axis_size("slab")
    column = ("pencil", "sub")
    count = masses.shape[0]
    target = dest_slab.reshape(1, count)
    cells = dest_cell.reshape(1, count)
    band_list = bands(w_first, w_middle, w_last)
    parts = paint(step_size, masses.reshape(1, count), target, cells, cotangent, slabs)
    arrived = [shifted(parts[k], "slab", k) for k in range(1, slabs)]
    own = functools.reduce(jnp.add, [a.astype(F32) for a in arrived], parts[0]).astype(BF16)
    blocks = (shifted(own, "slab", 1), own, shifted(own, "slab", -1))
    half = BLOCK // 2
    before = shifted(jnp.concatenate([b[half:] for b in blocks], axis=0), column, 1)
    after = shifted(jnp.concatenate([b[:half] for b in blocks], axis=0), column, -1)
    mesh_own, grads = network(blocks, (before, after), band_list, w_middle.shape[0])
    meshes = [mesh_own] + [shifted(mesh_own, "slab", -k) for k in range(1, slabs)]
    grads = sum_over(sum_over(grads, column), "slab")
    velocity_new, grad_mass = read_out(step_size, target, cells, velocity, meshes, slabs)
    cell_total = ZL * YL * XL * slabs * lax.axis_size("pencil") * lax.axis_size("sub")
    grads = grads * (1.0 / math.sqrt(cell_total))
    return (
        velocity_new,
        grad_mass.reshape(count),
        grads[0 : w_first.shape[0], 0 : w_first.shape[1]],
        grads[8 : 8 + w_middle.shape[0], 0 : w_middle.shape[1]],
        grads[16 : 16 + w_last.shape[0], 0 : w_last.shape[1]],
    )


def solution(mesh):
    everywhere = ("runs", "slab", "pencil", "sub")
    placed = (
        P(everywhere),
        P(None, everywhere),
        P(everywhere, None),
        P(everywhere),
        P(),
        P(),
        P(),
        P(),
        P(None, everywhere),
    )
    return jax.shard_map(
        local,
        mesh=mesh,
        in_specs=placed,
        out_specs=(
            P(None, everywhere),
            P(everywhere),
            P("runs", None),
            P("runs", None),
            P("runs", None),
        ),
        check_vma=False,
    )
```

time: 672 us -> 69 us (0.10); the launches traced: 662 us -> 68.1 us
  local copies, waits for them, and re-layouts: 441 us -> 5.45 us
  blocking collectives: 58.2 us -> 0 us
  starting transfers between devices: 57.6 us -> 22.1 us
  other arithmetic: 37.6 us -> 3.16 us
  matrix products: 31 us -> 0 us
  Pallas kernels: 0 us -> 22.6 us
  loops' own time: 22.5 us -> 0 us
    gather x6 -> x0, local copies, waits for them, and re-layouts: 269 us -> none  [the longest x4 162 us: readout(): picked = jnp.take(mesh_field, safe_cells, axis=1)]
    unnamed x130 -> x18, local copies, waits for them, and re-layouts: 104 us -> 2.3 us
    psum x1 -> x0, blocking collectives: 58.2 us -> none  [local(): lax.psum((grad_first, grad_middle, grad_last), ('slab', 'pencil', 'sub'))]
    dot_general x59 -> x0, matrix products: 31 us -> none  [the longest x32 18 us: add_block(): jnp.einsum('kst,sl->ktl', weighted, lane_hot, preferred_element_type=jnp....]
    scatter x1 -> x0, local copies, waits for them, and re-layouts: 23.8 us -> none  [local(): jnp.zeros((3, buffer_len), jnp.bfloat16).at[:, placed].set(pushed)]
    all_to_all x5 -> x0, starting transfers between devices: 23.3 us -> none  [the longest x1 6.32 us: local(): lax.all_to_all(mass_rows, 'slab', split_axis=1, concat_axis=1, tiled=True)]
    pallas_call x0 -> x4, Pallas kernels: none -> 22.6 us  [the longest x1 8.33 us: network(): pl.pallas_call(net_kernel, out_shape=[jax.ShapeDtypeStruct((BLOCK, XL), B...]
    another operation x2 -> x0, loops' own time: 22.5 us -> none  [paint_slots(): lax.scan(add_block, initial, jnp.arange(slot_total // block_rows, dtype=j...]
  transfers between devices with their start and end apart: 29 -> 16, of which waited for: 8 -> 9; matrix products, arithmetic and copies ran while one was open for 44% -> 3% of each run, Pallas kernels for 0% -> 5%
where the time goes in v1:
time: 69 us; the launch traced here: 68.1 us
  Pallas kernels  22.6 us (33%)
  starting transfers between devices  22.1 us (32%)
  waiting for transfers between devices  13.3 us (19%)
  local copies, waits for them, and re-layouts  5.45 us (8%)
  other arithmetic  3.16 us (5%)
  between operations  1.38 us (2%)
    ppermute x16, starting transfers between devices, shifted(): lax.ppermute(value, axis, [(i, (i + distance) % count) for i in range(cou...  22.1 us
    ppermute x16, waiting for transfers between devices, shifted(): lax.ppermute(value, axis, [(i, (i + distance) % count) for i in range(cou...  13.3 us
    pallas_call x1, Pallas kernels, network(): pl.pallas_call(net_kernel, out_shape=[jax.ShapeDtypeStruct((BLOCK, XL), B...  8.33 us
    pallas_call x1, Pallas kernels, read_out(): pl.pallas_call(functools.partial(readout_kernel, slabs), grid=(count // c...  6.4 us
    pallas_call x1, Pallas kernels, paint(): pl.pallas_call(functools.partial(paint_kernel, slabs), grid=(count // chu...  4.81 us
    pallas_call x1, Pallas kernels, bands(): pl.pallas_call(band_kernel, out_shape=[jax.ShapeDtypeStruct(s, BF16) for...  3.08 us
    unnamed x18, local copies, waits for them, and re-layouts  2.3 us
    pallas_call x1, other arithmetic, read_out(): pl.pallas_call(functools.partial(readout_kernel, slabs), grid=(count // c...  1.45 us
  transfers between devices with their start and end apart: 16, of which 9 were waited for; matrix products, arithmetic and copies ran while one was open for 3% of the time, Pallas kernels for 5%

profile of v1, /device:TPU:0, one launch (start us, length us, event | category | flops | bytes accessed | tf_op | source)
XLA Modules:
  0.0 68.1 jit_solution(1261057448193380339)
XLA Ops:
  1.3 1.3 %reshape.24.mass_ref = bf16[1,8192]{1,0:T(2,128)(2,1)} reshape(bf16[8192]{0:T(1024)(128)(2,1)} %param.14) | data formatting | bytes 32768 | tf_op jit(solution)/shard_map/reshape | solution.py:393
  2.6 4.8 %shard_map.173 = (f32[128,256]{1,0:T(8,128)}, bf16[128,256]{1,0:T(8,128)(2,1)}, bf16[128,256]{1,0:T(8,128)(2,1)}, bf16[128,256]{1,0:T(8,128)(2,1)}) custom-call(f32[1]{0:T(128)S(6)} %copy.19.step_ref, bf16[1,8192]{1,0:T(2,128)(2,1)} %reshape.24.mass_ref, s32[1,8192]{1,0:T(1,128)} %bitcast.2, s32[1,8192]{1,0:T(1,128)} %bitcast.4, f32[3,8192]{1,0:T(4,128)} %cot_ref.1), custom_call_target="tpu_custom_call" | custom-call | tf_op jit(solution)/shard_map/pallas_call | solution.py:92
  7.4 3.0 %collective-permute-start = (bf16[128,256]{1,0:T(8,128)(2,1)}, bf16[128,256]{1,0:T(8,128)(2,1)S(1)}, u32[]{:S(2)}, u32[]{:S(2)}) collective-permute-start(bf16[128,256]{1,0:T(8,128)(2,1)} %get-tuple-element.20), channel_id=1, source_target_pairs={{0,4},{4,8},{8,12},{12,0},{1,5},{5,9},{9,13},{13,1},{2,6},{6,10},{... | collective-permute-start | bytes 196616 | tf_op jit(solution)/shard_map/ppermute | solution.py:377
  10.4 2.6 %collective-permute-start.1 = (bf16[128,256]{1,0:T(8,128)(2,1)}, bf16[128,256]{1,0:T(8,128)(2,1)S(1)}, u32[]{:S(2)}, u32[]{:S(2)}) collective-permute-start(bf16[128,256]{1,0:T(8,128)(2,1)} %get-tuple-element.21), channel_id=1, source_target_pairs={{0,8},{4,12},{8,0},{12,4},{1,9},{5,13},{9,1},{13,5},{2,10},{6,14},... | collective-permute-start | bytes 196616 | tf_op jit(solution)/shard_map/ppermute | solution.py:377
  13.0 1.3 %collective-permute-start.2 = (bf16[128,256]{1,0:T(8,128)(2,1)}, bf16[128,256]{1,0:T(8,128)(2,1)S(1)}, u32[]{:S(2)}, u32[]{:S(2)}) collective-permute-start(bf16[128,256]{1,0:T(8,128)(2,1)} %get-tuple-element.22), channel_id=1, source_target_pairs={{0,12},{4,0},{8,4},{12,8},{1,13},{5,1},{9,5},{13,9},{2,14},{6,2},{... | collective-permute-start | bytes 196616 | tf_op jit(solution)/shard_map/ppermute | solution.py:377
  14.4 0.8 %collective-permute-done = bf16[128,256]{1,0:T(8,128)(2,1)S(1)} collective-permute-done((bf16[128,256]{1,0:T(8,128)(2,1)}, bf16[128,256]{1,0:T(8,128)(2,1)S(1)}, u32[]{:S(2)}, u32[]{:S(2)}) %collective-permute-start) | collective-permute-done | bytes 65568 | tf_op jit(solution)/shard_map/ppermute | solution.py:377
  15.2 2.5 %collective-permute-done.1 = bf16[128,256]{1,0:T(8,128)(2,1)S(1)} collective-permute-done((bf16[128,256]{1,0:T(8,128)(2,1)}, bf16[128,256]{1,0:T(8,128)(2,1)S(1)}, u32[]{:S(2)}, u32[]{:S(2)}) %collective-permute-start.1) | collective-permute-done | bytes 65568 | tf_op jit(solution)/shard_map/ppermute | solution.py:377
  18.0 0.9 %add_convert_fusion.own_ref = bf16[128,256]{1,0:T(8,128)(2,1)S(1)} fusion(bf16[128,256]{1,0:T(8,128)(2,1)S(1)} %collective-permute-done.2, bf16[128,256]{1,0:T(8,128)(2,1)S(1)} %collective-permute-done.1, f32[128,256]{1,0:T(8,128)} %get-tuple-element.19, bf16[128,256]{1,0:T(8,128)(2,1)S(1)} %collective-permute-done), kind=kLoop, calls=%fused_computation | loop fusion | flops 229376 | bytes 393216 | tf_op jit(solution)/shard_map/convert_element_type | solution.py:395
  18.9 3.1 %collective-permute-start.4 = (bf16[128,256]{1,0:T(8,128)(2,1)S(1)}, bf16[128,256]{1,0:T(8,128)(2,1)S(1)}, u32[]{:S(2)}, u32[]{:S(2)}) collective-permute-start(bf16[128,256]{1,0:T(8,128)(2,1)S(1)} %add_convert_fusion.own_ref), channel_id=1, source_target_pairs={{0,12},{4,0},{8,4},{12,8},{1,13},{5,1},{9,5},{13,9},{2,14},{6,2},{... | collective-permute-start | bytes 196616 | tf_op jit(solution)/shard_map/ppermute | solution.py:377
  22.0 1.9 %collective-permute-done.4.above_ref = bf16[128,256]{1,0:T(8,128)(2,1)S(1)} collective-permute-done((bf16[128,256]{1,0:T(8,128)(2,1)S(1)}, bf16[128,256]{1,0:T(8,128)(2,1)S(1)}, u32[]{:S(2)}, u32[]{:S(2)}) %collective-permute-start.4) | collective-permute-done | bytes 65568 | tf_op jit(solution)/shard_map/ppermute | solution.py:377
  23.9 4.2 %collective-permute-done.3.below_ref = bf16[128,256]{1,0:T(8,128)(2,1)S(1)} collective-permute-done((bf16[128,256]{1,0:T(8,128)(2,1)S(1)}, bf16[128,256]{1,0:T(8,128)(2,1)S(1)}, u32[]{:S(2)}, u32[]{:S(2)}) %collective-permute-start.3) | collective-permute-done | bytes 65568 | tf_op jit(solution)/shard_map/ppermute | solution.py:377
  28.8 1.8 %collective-permute-start.6 = (bf16[192,256]{1,0:T(8,128)(2,1)S(1)}, bf16[192,256]{1,0:T(8,128)(2,1)S(1)}, u32[]{:S(2)}, u32[]{:S(2)}) collective-permute-start(bf16[192,256]{1,0:T(8,128)(2,1)S(1)} %pad_maximum_fusion.1), channel_id=1, source_target_pairs={{0,3},{1,0},{2,1},{3,2},{4,7},{5,4},{6,5},{7,6},{8,11},{9,8},{10,9... | collective-permute-start | bytes 294920 | tf_op jit(solution)/shard_map/ppermute | solution.py:377
  30.6 3.1 %shard_map.174 = (bf16[128,144]{1,0:T(8,128)(2,1)}, bf16[128,1152]{1,0:T(8,128)(2,1)}, bf16[48,1152]{1,0:T(8,128)(2,1)}, bf16[16,1152]{1,0:T(8,128)(2,1)}, bf16[...) custom-call(bf16[8,27]{1,0:T(8,128)(2,1)} %first_ref.1, bf16[8,216]{1,0:T(8,128)(2,1)} %middle_ref.1, ...), custom_call_target="tpu_custom_call" | custom-call | flops 800000000 | bytes 4000000 | tf_op jit(solution)/shard_map/pallas_call | solution.py:171
  34.3 8.3 %shard_map.175 = (bf16[128,256]{1,0:T(8,128)(2,1)}, f32[24,256]{1,0:T(8,128)}) custom-call(bf16[128,256]{1,0:T(8,128)(2,1)} %copy-done.2, bf16[128,256]{1,0:T(8,128)(2,1)} %copy-done, bf16[128,256]{1,0:T(8,128)(2,1)} %copy-done.1, bf16[192,256]{1,0:T(8,128)(2,1)} %copy-done.3, bf16[192,256]{1,0:T(8,128)(2,1)} %copy-done.4, ...), custom_call_target="tpu_custom_call" | custom-call | tf_op jit(solution)/shard_map/pallas_call | solution.py:303
  42.7 1.1 %collective-permute-start.12 = (f32[24,256]{1,0:T(8,128)}, f32[24,256]{1,0:T(8,128)S(1)}, u32[]{:S(2)}, u32[]{:S(2)}) collective-permute-start(f32[24,256]{1,0:T(8,128)} %get-tuple-element.32), channel_id=1, source_target_pairs={{0,3},{1,0},{2,1},{3,2},{4,7},{5,4},{6,5},{7,6},{8,11},{9,8},{10,9... | collective-permute-start | bytes 73736 | tf_op jit(solution)/shard_map/ppermute | solution.py:377
  43.7 1.3 %collective-permute-start.11 = (f32[24,256]{1,0:T(8,128)}, f32[24,256]{1,0:T(8,128)S(1)}, u32[]{:S(2)}, u32[]{:S(2)}) collective-permute-start(f32[24,256]{1,0:T(8,128)} %get-tuple-element.32), channel_id=1, source_target_pairs={{0,2},{1,3},{2,0},{3,1},{4,6},{5,7},{6,4},{7,5},{8,10},{9,11},{10,... | collective-permute-start | bytes 73736 | tf_op jit(solution)/shard_map/ppermute | solution.py:377
  45.5 2.3 %collective-permute-done.11 = f32[24,256]{1,0:T(8,128)S(1)} collective-permute-done((f32[24,256]{1,0:T(8,128)}, f32[24,256]{1,0:T(8,128)S(1)}, u32[]{:S(2)}, u32[]{:S(2)}) %collective-permute-start.11) | collective-permute-done | bytes 24608 | tf_op jit(solution)/shard_map/ppermute | solution.py:377
  48.5 0.7 %add_add_fusion = f32[24,256]{1,0:T(8,128)S(1)} fusion(f32[24,256]{1,0:T(8,128)S(1)} %collective-permute-done.12, f32[24,256]{1,0:T(8,128)S(1)} %collective-permute-done.11, f32[24,256]{1,0:T(8,128)} %get-tuple-element.32, f32[24,256]{1,0:T(8,128)S(1)} %collective-permute-done.10), kind=kLoop, calls=%fused_computation.4 | loop fusion | flops 18432 | bytes 122880 | tf_op jit(solution)/shard_map/add | solution.py:383
  49.6 1.7 %collective-permute-start.13 = (f32[24,256]{1,0:T(8,128)S(1)}, f32[24,256]{1,0:T(8,128)S(1)}, u32[]{:S(2)}, u32[]{:S(2)}) collective-permute-start(f32[24,256]{1,0:T(8,128)S(1)} %add_add_fusion), channel_id=1, source_target_pairs={{0,4},{4,8},{8,12},{12,0},{1,5},{5,9},{9,13},{13,1},{2,6},{6,10},{... | collective-permute-start | bytes 73736 | tf_op jit(solution)/shard_map/ppermute | solution.py:377
  51.3 1.5 %collective-permute-start.9 = (bf16[128,256]{1,0:T(8,128)(2,1)S(1)}, bf16[128,256]{1,0:T(8,128)(2,1)S(1)}, u32[]{:S(2)}, u32[]{:S(2)}) collective-permute-start(bf16[128,256]{1,0:T(8,128)(2,1)S(1)} %copy-done.5), channel_id=1, source_target_pairs={{0,4},{4,8},{8,12},{12,0},{1,5},{5,9},{9,13},{13,1},{2,6},{6,10},{... | collective-permute-start | bytes 196616 | tf_op jit(solution)/shard_map/ppermute | solution.py:377
  52.8 1.4 %collective-permute-start.8 = (bf16[128,256]{1,0:T(8,128)(2,1)S(1)}, bf16[128,256]{1,0:T(8,128)(2,1)S(1)}, u32[]{:S(2)}, u32[]{:S(2)}) collective-permute-start(bf16[128,256]{1,0:T(8,128)(2,1)S(1)} %copy-done.5), channel_id=1, source_target_pairs={{0,8},{4,12},{8,0},{12,4},{1,9},{5,13},{9,1},{13,5},{2,10},{6,14},... | collective-permute-start | bytes 196616 | tf_op jit(solution)/shard_map/ppermute | solution.py:377
  54.2 2.9 %collective-permute-start.7 = (bf16[128,256]{1,0:T(8,128)(2,1)S(1)}, bf16[128,256]{1,0:T(8,128)(2,1)S(1)}, u32[]{:S(2)}, u32[]{:S(2)}) collective-permute-start(bf16[128,256]{1,0:T(8,128)(2,1)S(1)} %copy-done.5), channel_id=1, source_target_pairs={{0,12},{4,0},{8,4},{12,8},{1,13},{5,1},{9,5},{13,9},{2,14},{6,2},{... | collective-permute-start | bytes 196616 | tf_op jit(solution)/shard_map/ppermute | solution.py:377
  60.2 6.4 %shard_map.176 = (f32[3,8192]{1,0:T(4,128)}, bf16[1,8192]{1,0:T(2,128)(2,1)}) custom-call(f32[1]{0:T(128)S(6)} %copy.19.step_ref, s32[1,8192]{1,0:T(1,128)} %bitcast.3, s32[1,8192]{1,0:T(1,128)} %bitcast.5, f32[3,8192]{1,0:T(4,128)} %velocity_ref.1, bf16[128,256]{1,0:T(8,128)(2,1)} %get-tuple-element.29.rest_0_, bf16[128,256]{1,0:T(8,128)(2,1)} %copy-done.8, ...), custom_call_target="tpu_custom_call" | custom-call | tf_op jit(solution)/shard_map/pallas_call | solution.py:361
  66.6 1.5 %reduce = bf16[8192]{0:T(1024)(128)(2,1)} reduce(bf16[1,8192]{1,0:T(2,128)(2,1)} %get-tuple-element.31, bf16[]{:T(256)} %constant.11), dimensions={0}, to_apply=%get-tuple-element.31.reduce_sub_computation | reduce | bytes 32770 | tf_op jit(solution)/shard_map/pallas_call | solution.py:361
  (43 shorter events, 6.2 us)
Async XLA Ops:
  7.4 7.8 %collective-permute-start = (bf16[128,256]{1,0:T(8,128)(2,1)}, bf16[128,256]{1,0:T(8,128)(2,1)S(1)}, u32[]{:S(2)}, u32[]{:S(2)}) collective-permute-start(bf16[128,256]{1,0:T(8,128)(2,1)} %get-tuple-element.20), channel_id=1, source_target_pairs={{0,4},{4,8},{8,12},{12,0},{1,5},{5,9},{9,13},{13,1},{2,6},{6,10},{... | collective-permute-start | bytes 196616 | tf_op jit(solution)/shard_map/ppermute | solution.py:377
  10.4 7.3 %collective-permute-start.1 = (bf16[128,256]{1,0:T(8,128)(2,1)}, bf16[128,256]{1,0:T(8,128)(2,1)S(1)}, u32[]{:S(2)}, u32[]{:S(2)}) collective-permute-start(bf16[128,256]{1,0:T(8,128)(2,1)} %get-tuple-element.21), channel_id=1, source_target_pairs={{0,8},{4,12},{8,0},{12,4},{1,9},{5,13},{9,1},{13,5},{2,10},{6,14},... | collective-permute-start | bytes 196616 | tf_op jit(solution)/shard_map/ppermute | solution.py:377
  13.0 4.9 %collective-permute-start.2 = (bf16[128,256]{1,0:T(8,128)(2,1)}, bf16[128,256]{1,0:T(8,128)(2,1)S(1)}, u32[]{:S(2)}, u32[]{:S(2)}) collective-permute-start(bf16[128,256]{1,0:T(8,128)(2,1)} %get-tuple-element.22), channel_id=1, source_target_pairs={{0,12},{4,0},{8,4},{12,8},{1,13},{5,1},{9,5},{13,9},{2,14},{6,2},{... | collective-permute-start | bytes 196616 | tf_op jit(solution)/shard_map/ppermute | solution.py:377
  18.9 5.0 %copy-start = (bf16[128,256]{1,0:T(8,128)(2,1)}, bf16[128,256]{1,0:T(8,128)(2,1)S(1)}, u32[]{:S(2)}) copy-start(bf16[128,256]{1,0:T(8,128)(2,1)S(1)} %add_convert_fusion.own_ref) | copy-start | bytes 196612
  18.9 5.0 %collective-permute-start.4 = (bf16[128,256]{1,0:T(8,128)(2,1)S(1)}, bf16[128,256]{1,0:T(8,128)(2,1)S(1)}, u32[]{:S(2)}, u32[]{:S(2)}) collective-permute-start(bf16[128,256]{1,0:T(8,128)(2,1)S(1)} %add_convert_fusion.own_ref), channel_id=1, source_target_pairs={{0,12},{4,0},{8,4},{12,8},{1,13},{5,1},{9,5},{13,9},{2,14},{6,2},{... | collective-permute-start | bytes 196616 | tf_op jit(solution)/shard_map/ppermute | solution.py:377
  22.0 6.1 %collective-permute-start.3 = (bf16[128,256]{1,0:T(8,128)(2,1)S(1)}, bf16[128,256]{1,0:T(8,128)(2,1)S(1)}, u32[]{:S(2)}, u32[]{:S(2)}) collective-permute-start(bf16[128,256]{1,0:T(8,128)(2,1)S(1)} %add_convert_fusion.own_ref), channel_id=1, source_target_pairs={{0,4},{4,8},{8,12},{12,0},{1,5},{5,9},{9,13},{13,1},{2,6},{6,10},{... | collective-permute-start | bytes 196616 | tf_op jit(solution)/shard_map/ppermute | solution.py:377
  23.9 4.2 %copy-start.1 = (bf16[128,256]{1,0:T(8,128)(2,1)}, bf16[128,256]{1,0:T(8,128)(2,1)S(1)}, u32[]{:S(2)}) copy-start(bf16[128,256]{1,0:T(8,128)(2,1)S(1)} %collective-permute-done.4.above_ref) | copy-start | bytes 196612
  28.1 0.6 copy-start.2
  28.7 4.9 %collective-permute-start.5 = (bf16[192,256]{1,0:T(8,128)(2,1)S(1)}, bf16[192,256]{1,0:T(8,128)(2,1)S(1)}, u32[]{:S(2)}, u32[]{:S(2)}) collective-permute-start(bf16[192,256]{1,0:T(8,128)(2,1)S(1)} %pad_maximum_fusion), channel_id=1, source_target_pairs={{0,1},{1,2},{2,3},{3,0},{4,5},{5,6},{6,7},{7,4},{8,9},{9,10},{10,1... | collective-permute-start | bytes 294920 | tf_op jit(solution)/shard_map/ppermute | solution.py:377
  28.8 4.9 %collective-permute-start.6 = (bf16[192,256]{1,0:T(8,128)(2,1)S(1)}, bf16[192,256]{1,0:T(8,128)(2,1)S(1)}, u32[]{:S(2)}, u32[]{:S(2)}) collective-permute-start(bf16[192,256]{1,0:T(8,128)(2,1)S(1)} %pad_maximum_fusion.1), channel_id=1, source_target_pairs={{0,3},{1,0},{2,1},{3,2},{4,7},{5,4},{6,5},{7,6},{8,11},{9,8},{10,9... | collective-permute-start | bytes 294920 | tf_op jit(solution)/shard_map/ppermute | solution.py:377
  33.6 0.6 copy-start.3
  33.7 0.7 copy-start.4
  42.6 8.6 %copy-start.5 = (bf16[128,256]{1,0:T(8,128)(2,1)S(1)}, bf16[128,256]{1,0:T(8,128)(2,1)}, u32[]{:S(2)}) copy-start(bf16[128,256]{1,0:T(8,128)(2,1)} %get-tuple-element.29.rest_0_) | copy-start | bytes 196612
  42.7 2.8 %collective-permute-start.12 = (f32[24,256]{1,0:T(8,128)}, f32[24,256]{1,0:T(8,128)S(1)}, u32[]{:S(2)}, u32[]{:S(2)}) collective-permute-start(f32[24,256]{1,0:T(8,128)} %get-tuple-element.32), channel_id=1, source_target_pairs={{0,3},{1,0},{2,1},{3,2},{4,7},{5,4},{6,5},{7,6},{8,11},{9,8},{10,9... | collective-permute-start | bytes 73736 | tf_op jit(solution)/shard_map/ppermute | solution.py:377
  43.7 4.0 %collective-permute-start.11 = (f32[24,256]{1,0:T(8,128)}, f32[24,256]{1,0:T(8,128)S(1)}, u32[]{:S(2)}, u32[]{:S(2)}) collective-permute-start(f32[24,256]{1,0:T(8,128)} %get-tuple-element.32), channel_id=1, source_target_pairs={{0,2},{1,3},{2,0},{3,1},{4,6},{5,7},{6,4},{7,5},{8,10},{9,11},{10,... | collective-permute-start | bytes 73736 | tf_op jit(solution)/shard_map/ppermute | solution.py:377
  45.0 3.5 %collective-permute-start.10 = (f32[24,256]{1,0:T(8,128)}, f32[24,256]{1,0:T(8,128)S(1)}, u32[]{:S(2)}, u32[]{:S(2)}) collective-permute-start(f32[24,256]{1,0:T(8,128)} %get-tuple-element.32), channel_id=1, source_target_pairs={{0,1},{1,2},{2,3},{3,0},{4,5},{5,6},{6,7},{7,4},{8,9},{9,10},{10,1... | collective-permute-start | bytes 73736 | tf_op jit(solution)/shard_map/ppermute | solution.py:377
  49.2 5.0 %collective-permute-start.15 = (f32[24,256]{1,0:T(8,128)S(1)}, f32[24,256]{1,0:T(8,128)S(1)}, u32[]{:S(2)}, u32[]{:S(2)}) collective-permute-start(f32[24,256]{1,0:T(8,128)S(1)} %add_add_fusion), channel_id=1, source_target_pairs={{0,12},{4,0},{8,4},{12,8},{1,13},{5,1},{9,5},{13,9},{2,14},{6,2},{... | collective-permute-start | bytes 73736 | tf_op jit(solution)/shard_map/ppermute | solution.py:377
  49.3 7.8 %collective-permute-start.14 = (f32[24,256]{1,0:T(8,128)S(1)}, f32[24,256]{1,0:T(8,128)S(1)}, u32[]{:S(2)}, u32[]{:S(2)}) collective-permute-start(f32[24,256]{1,0:T(8,128)S(1)} %add_add_fusion), channel_id=1, source_target_pairs={{0,8},{4,12},{8,0},{12,4},{1,9},{5,13},{9,1},{13,5},{2,10},{6,14},... | collective-permute-start | bytes 73736 | tf_op jit(solution)/shard_map/ppermute | solution.py:377
  49.6 7.5 %collective-permute-start.13 = (f32[24,256]{1,0:T(8,128)S(1)}, f32[24,256]{1,0:T(8,128)S(1)}, u32[]{:S(2)}, u32[]{:S(2)}) collective-permute-start(f32[24,256]{1,0:T(8,128)S(1)} %add_add_fusion), channel_id=1, source_target_pairs={{0,4},{4,8},{8,12},{12,0},{1,5},{5,9},{9,13},{13,1},{2,6},{6,10},{... | collective-permute-start | bytes 73736 | tf_op jit(solution)/shard_map/ppermute | solution.py:377
  51.3 7.7 %collective-permute-start.9 = (bf16[128,256]{1,0:T(8,128)(2,1)S(1)}, bf16[128,256]{1,0:T(8,128)(2,1)S(1)}, u32[]{:S(2)}, u32[]{:S(2)}) collective-permute-start(bf16[128,256]{1,0:T(8,128)(2,1)S(1)} %copy-done.5), channel_id=1, source_target_pairs={{0,4},{4,8},{8,12},{12,0},{1,5},{5,9},{9,13},{13,1},{2,6},{6,10},{... | collective-permute-start | bytes 196616 | tf_op jit(solution)/shard_map/ppermute | solution.py:377
  52.8 6.1 %collective-permute-start.8 = (bf16[128,256]{1,0:T(8,128)(2,1)S(1)}, bf16[128,256]{1,0:T(8,128)(2,1)S(1)}, u32[]{:S(2)}, u32[]{:S(2)}) collective-permute-start(bf16[128,256]{1,0:T(8,128)(2,1)S(1)} %copy-done.5), channel_id=1, source_target_pairs={{0,8},{4,12},{8,0},{12,4},{1,9},{5,13},{9,1},{13,5},{2,10},{6,14},... | collective-permute-start | bytes 196616 | tf_op jit(solution)/shard_map/ppermute | solution.py:377
  54.2 4.9 %collective-permute-start.7 = (bf16[128,256]{1,0:T(8,128)(2,1)S(1)}, bf16[128,256]{1,0:T(8,128)(2,1)S(1)}, u32[]{:S(2)}, u32[]{:S(2)}) collective-permute-start(bf16[128,256]{1,0:T(8,128)(2,1)S(1)} %copy-done.5), channel_id=1, source_target_pairs={{0,12},{4,0},{8,4},{12,8},{1,13},{5,1},{9,5},{13,9},{2,14},{6,2},{... | collective-permute-start | bytes 196616 | tf_op jit(solution)/shard_map/ppermute | solution.py:377
  58.9 0.6 copy-start.6
  58.9 0.6 copy-start.7
  (1 other events, 0.6 us)

commit v2 on v1

v2 whole, which is shorter than its diff:
```python
import functools
import math

import jax
import jax.numpy as jnp
import numpy as np
from jax import lax
from jax.experimental import pallas as pl
from jax.experimental.pallas import tpu as pltpu
from jax.sharding import PartitionSpec as P

ZL = 4
YL = 8
XL = 256
ROWS = ZL * YL
FIELDS = 4
BLOCK = FIELDS * ROWS
POS = 16
DEPTH = 3 * ZL
BF16 = jnp.bfloat16
F32 = jnp.float32
NT = (((1,), (1,)), ((), ()))
MIB = 1024 * 1024


def dot(a, b):
    return jnp.dot(a, b, preferred_element_type=F32)


def dot_nt(a, b):
    return lax.dot_general(a, b, NT, preferred_element_type=F32)


def row_iota(shape, dim):
    return lax.broadcasted_iota(jnp.int32, shape, dim)


def spread_rows(dense, height, first, count):
    tiles = [
        jnp.broadcast_to(dense[t : t + 1, :], (height, 128)) for t in range(first, first + count)
    ]
    return jnp.concatenate(tiles, axis=1)


def fill_lane_hot(store, lane, chunk):
    sixteen = row_iota((16, chunk), 0)
    zero, one = jnp.zeros((16, chunk), BF16), jnp.ones((16, chunk), BF16)
    for group in range(XL // 16):
        same = lane == (sixteen + 16 * group).astype(F32).astype(BF16)
        store[16 * group : 16 * group + 16, :] = jnp.where(same, one, zero)


def from_here(target, slabs):
    relative = target - lax.axis_index("slab")
    return jnp.where(relative < 0, relative + slabs, relative)


def paint_kernel(slabs, chunk, step_ref, mass_ref, slab_ref, cell_ref, cot_ref, *rest):
    outs, (hot, lane_hot, total) = rest[:slabs], rest[slabs:]
    cell = cell_ref[...]
    z, y = cell >> 11, (cell >> 8) & 7
    code = ((from_here(slab_ref[...], slabs) * 2 + (y >> 2)) << 4) + (z << 2) + (y & 3)
    lanes = (cell & (XL - 1)).astype(F32)
    mass = mass_ref[...].astype(F32)
    tiles = chunk // 128
    sixteen = row_iota((16, chunk), 0)
    zero = jnp.zeros((16, chunk), BF16)
    bases = range(0, 2 * slabs, 16)
    codes = [jnp.clip(code - 16 * base, -1, 256).astype(F32) for base in bases]
    for turn in range(mass.shape[0] // tiles):
        first_tile = turn * tiles
        here, here_lane = hot.at[turn % 2], lane_hot.at[turn % 2]
        fill_lane_hot(here_lane, spread_rows(lanes, 16, first_tile, tiles).astype(BF16), chunk)
        values = [spread_rows(mass, 16, first_tile, tiles).astype(BF16)]
        for component in range(3):
            pushed = step_ref[0] * cot_ref[component : component + 1, turn * chunk : (turn + 1) * chunk]
            values.append(jnp.broadcast_to(pushed, (16, chunk)).astype(BF16))
        for base, code_part in zip(bases, codes):
            code_tile = spread_rows(code_part, 16, first_tile, tiles).astype(BF16)
            for group in range(base, min(base + 16, 2 * slabs)):
                same = code_tile == (sixteen + 16 * (group - base)).astype(F32).astype(BF16)
                for field in range(FIELDS):
                    first = group * 64 + field * 16
                    here[first : first + 16, :] = jnp.where(same, values[field], zero)
        part = dot_nt(here[...], here_lane[...])
        if turn == 0:
            total[...] = part
        else:
            total[...] += part
    for k in range(slabs):
        outs[k][...] = total[k * BLOCK : (k + 1) * BLOCK, :].astype(outs[k].dtype)


def paint(step_size, masses, target, cells, cotangent, slabs):
    count = cotangent.shape[1]
    chunk = math.gcd(count, 2048)
    scratch = 2 * chunk * (slabs * BLOCK + XL) * 2 + slabs * BLOCK * XL * 4
    vmem = pl.BlockSpec(memory_space=pltpu.VMEM)
    return pl.pallas_call(
        functools.partial(paint_kernel, slabs, chunk),
        in_specs=[pl.BlockSpec(memory_space=pltpu.SMEM)] + [vmem] * 4,
        out_specs=[vmem] * slabs,
        out_shape=[
            jax.ShapeDtypeStruct((BLOCK, XL), F32 if k == 0 else BF16) for k in range(slabs)
        ],
        scratch_shapes=[
            pltpu.VMEM((2, slabs * BLOCK, chunk), BF16),
            pltpu.VMEM((2, XL, chunk), BF16),
            pltpu.VMEM((slabs * BLOCK, XL), F32),
        ],
        compiler_params=pltpu.CompilerParams(vmem_limit_bytes=scratch + 12 * MIB),
    )(step_size, masses, target, cells, cotangent)


def tap_columns(channels):
    width = 9 * channels * POS
    col = np.arange(width)
    pair, channel = col // (channels * POS), (col // POS) % channels
    rows = [((pair // 3 * 3 + b) * 3 + pair % 3) * channels + channel for b in range(3)]
    return np.stack(rows + [np.full(width, -1)] * 5).astype(np.int32)


def tap_hot(taps, b, count):
    width = taps.shape[1]
    same = row_iota((count, width), 0) == taps[b : b + 1, :]
    return jnp.where(same, 1.0, 0.0).astype(F32)


def y_distance(rows, width):
    return (row_iota((rows, width), 1) - row_iota((rows, width), 0)) & (POS - 1)


Y_SHIFTS = (POS - 1, 0, 1)


def band(weight, taps):
    outs, count = weight.shape
    rows, width = outs * POS, taps.shape[1]
    pick = jnp.where(row_iota((rows, outs), 0) >> 4 == row_iota((rows, outs), 1), 1.0, 0.0)
    spread = dot(pick.astype(BF16), weight).astype(BF16)
    distance = y_distance(rows, width)
    result = jnp.zeros((rows, width), F32)
    for b in range(3):
        picked = dot(spread, tap_hot(taps, b, count).astype(BF16))
        result = jnp.where(distance == Y_SHIFTS[b], picked, result)
    return result


def band_kernel(
    first_ref, middle_ref, last_ref, one_ref, many_ref, b1_ref, b2_ref, b3_ref, t1_ref, t2_ref, t3_ref
):
    many = many_ref[...]
    for weight_ref, taps, b_ref, t_ref in (
        (first_ref, one_ref[...], b1_ref, t1_ref),
        (middle_ref, many, b2_ref, t2_ref),
        (last_ref, many, b3_ref, t3_ref),
    ):
        full = band(weight_ref[...], taps)
        b_ref[...] = full.astype(BF16)
        outs, ins = full.shape[0], full.shape[1] // 9
        for pair in range(9):
            block = full[:, pair * ins : (pair + 1) * ins].T.astype(BF16)
            t_ref[:, (8 - pair) * outs : (9 - pair) * outs] = block


def bands(w_first, w_middle, w_last):
    sizes = [(w.shape[0] * POS, w.shape[1] // 27 * POS) for w in (w_first, w_middle, w_last)]
    shapes = [(o, 9 * c) for o, c in sizes] + [(c, 9 * o) for o, c in sizes]
    one = tap_columns(1)
    many = tap_columns(w_middle.shape[1] // 27)
    return pl.pallas_call(
        band_kernel,
        out_shape=[jax.ShapeDtypeStruct(s, BF16) for s in shapes],
        compiler_params=pltpu.CompilerParams(vmem_limit_bytes=20 * MIB),
        cost_estimate=pl.CostEstimate(
            flops=800_000_000, bytes_accessed=4_000_000, transcendentals=0
        ),
    )(w_first, w_middle, w_last, jnp.asarray(one), jnp.asarray(many))


def lay_out(store, plane, value):
    rows = value.shape[0]
    for e, shift in enumerate((1, 0, XL - 1)):
        moved = value if shift == 0 else pltpu.roll(value, shift, 1)
        store[plane, e * rows : (e + 1) * rows, :] = moved.astype(BF16)


def window(store, plane):
    rows = store.shape[1]
    return store[plane - 1 : plane + 2].reshape(3 * rows, XL)


def centre(store, plane):
    rows = store.shape[1] // 3
    return store[plane, rows : 2 * rows, :]


def slope(pre, sigma):
    return sigma * (1.0 + pre * (1.0 - sigma))


def split_three(value):
    high = value.astype(BF16).astype(F32)
    rest = value - high
    mid = rest.astype(BF16).astype(F32)
    return jnp.concatenate([high, mid, rest - mid], axis=0).astype(BF16)


def weight_sum(full, outs, channels):
    width = full.shape[1]
    distance = y_distance(YL, width)
    group = row_iota((width // POS, width), 1) >> 4 == row_iota((width // POS, width), 0)
    group = jnp.where(group, 1.0, 0.0).astype(BF16)
    sums = []
    for b in range(3):
        mask = distance == Y_SHIFTS[b]
        rows = [
            jnp.sum(
                jnp.where(mask, full[o * POS : o * POS + YL, :], 0.0), axis=0, keepdims=True
            )
            for o in range(outs)
        ]
        rows += [jnp.zeros_like(rows[0])] * (8 - outs)
        parts = dot_nt(split_three(jnp.concatenate(rows, axis=0)), group)
        sums.append(parts[0:8] + parts[8:16] + parts[16:24])
    span = 3 * channels
    pieces = [sums[b][:, a * span : (a + 1) * span] for a in range(3) for b in range(3)]
    return jnp.concatenate(pieces, axis=1)


def net_kernel(
    below_ref, own_ref, above_ref, before_ref, after_ref,
    b1_ref, b2_ref, b3_ref, t1_ref, t2_ref, t3_ref, order_ref,
    mesh_ref, grads_ref,
    s0, s1, s2, sg, d2, d1, slope1, slope2, fields,
):
    order = order_ref[...]
    for b, block in enumerate((below_ref, own_ref, above_ref)):
        for c in range(FIELDS):
            pieces = [
                block[c * 16 : c * 16 + 16, :],
                block[64 + c * 16 : 80 + c * 16, :],
                after_ref[b * 64 + c * 16 : b * 64 + c * 16 + 16, :],
                before_ref[b * 64 + c * 16 : b * 64 + c * 16 + 16, :],
            ]
            rows = dot(order, jnp.concatenate(pieces, axis=0))
            for z in range(ZL):
                value = rows[z * POS : (z + 1) * POS, :]
                for e, shift in enumerate((1, 0, XL - 1)):
                    moved = value if shift == 0 else pltpu.roll(value, shift, 1)
                    if c == 0:
                        s0[b * ZL + z, e * 16 : e * 16 + 16, :] = moved.astype(BF16)
                    else:
                        first = e * 48 + (c - 1) * 16
                        sg[b * ZL + z, first : first + 16, :] = moved.astype(BF16)
    b1, b2, b3 = b1_ref[...], b2_ref[...], b3_ref[...]
    t1, t2, t3 = t1_ref[...], t2_ref[...], t3_ref[...]
    for plane in range(1, DEPTH - 1):
        pre = dot(b1, window(s0, plane))
        sigma = jax.nn.sigmoid(pre)
        lay_out(s1, plane, pre * sigma)
        if 3 <= plane < DEPTH - 3:
            slope1[plane] = slope(pre, sigma)
    for plane in range(2, DEPTH - 2):
        pre = dot(b2, window(s1, plane))
        sigma = jax.nn.sigmoid(pre)
        if 3 <= plane < DEPTH - 3:
            lay_out(s2, plane, pre * sigma)
        slope2[plane] = slope(pre, sigma)
    for z in range(ZL):
        force = dot(b3, window(s2, ZL + z))
        for c in range(3):
            first = c * ROWS + z * YL
            fields[first : first + YL, :] = force[c * POS : c * POS + YL, :]
    for plane in range(2, DEPTH - 2):
        lay_out(d2, plane, dot(t3, window(sg, plane)) * slope2[plane])
    for plane in range(3, DEPTH - 3):
        lay_out(d1, plane, dot(t2, window(d2, plane)) * slope1[plane])
    for z in range(ZL):
        pull = dot(t1, window(d1, ZL + z))
        first = 3 * ROWS + z * YL
        fields[first : first + YL, :] = pull[0:YL, :]
    mesh_ref[...] = fields[...].astype(BF16)
    grads_ref[...] = jnp.zeros_like(grads_ref)
    channels = s1.shape[1] // (3 * POS)
    for first, (delta, source, outs, ins) in zip(
        (0, 8, 16), ((d1, s0, channels, 1), (d2, s1, channels, channels), (sg, s2, 3, channels))
    ):
        full = None
        for z in range(ZL):
            term = dot_nt(centre(delta, ZL + z), window(source, ZL + z))
            full = term if full is None else full + term
        grads_ref[first : first + 8, 0 : 27 * ins] = weight_sum(full, outs, ins)


def network(blocks, halves, band_list, channels):
    rows = channels * POS
    order = np.zeros((64, 64), np.float32)
    for z in range(4):
        for h in range(4):
            for y in range(4):
                order[z * 16 + h * 4 + y, h * 16 + z * 4 + y] = 1.0
    return pl.pallas_call(
        net_kernel,
        out_shape=[
            jax.ShapeDtypeStruct((BLOCK, XL), BF16),
            jax.ShapeDtypeStruct((24, 256), F32),
        ],
        scratch_shapes=[
            pltpu.VMEM((DEPTH, 3 * POS, XL), BF16),
            pltpu.VMEM((DEPTH, 3 * rows, XL), BF16),
            pltpu.VMEM((DEPTH, 3 * rows, XL), BF16),
            pltpu.VMEM((DEPTH, 9 * POS, XL), BF16),
            pltpu.VMEM((DEPTH, 3 * rows, XL), BF16),
            pltpu.VMEM((DEPTH, 3 * rows, XL), BF16),
            pltpu.VMEM((DEPTH, rows, XL), F32),
            pltpu.VMEM((DEPTH, rows, XL), F32),
            pltpu.VMEM((BLOCK, XL), F32),
        ],
        compiler_params=pltpu.CompilerParams(vmem_limit_bytes=28 * MIB),
    )(*blocks, *halves, *band_list, jnp.asarray(order, BF16))


def readout_kernel(slabs, chunk, stages, scale, step_ref, slab_ref, cell_ref, velocity_ref, *rest):
    meshes, rest = rest[:slabs], rest[slabs:]
    grads, rest = rest[:stages], rest[stages:]
    velocity_out, mass_out, first_out, middle_out, last_out, lane_hot, mass_rows = rest
    total = grads[0][...]
    for other in grads[1:]:
        total = total + other[...]
    total = total * scale
    first_out[...] = total[0 : first_out.shape[0], 0 : first_out.shape[1]]
    middle_out[...] = total[8 : 8 + middle_out.shape[0], 0 : middle_out.shape[1]]
    last_out[...] = total[16 : 16 + last_out.shape[0], 0 : last_out.shape[1]]
    cell = cell_ref[...]
    code = from_here(slab_ref[...], slabs) * ROWS + (cell >> 8)
    lanes = (cell & (XL - 1)).astype(F32)
    eight = row_iota((8, chunk), 0)
    tiles = chunk // 128
    for turn in range(cell.shape[0] // tiles):
        here = lane_hot.at[turn % 2]
        fill_lane_hot(here, spread_rows(lanes, 16, turn * tiles, tiles).astype(BF16), chunk)
        code_tile = spread_rows(code, 8, turn * tiles, tiles)
        sums = [jnp.zeros((8, chunk), F32) for _ in range(FIELDS)]
        for k in range(slabs):
            rows = dot(meshes[k][...], here[...])
            for group in range(ROWS // 8):
                same = code_tile == eight + (k * ROWS + group * 8)
                for c in range(FIELDS):
                    first = c * ROWS + group * 8
                    sums[c] = sums[c] + jnp.where(same, rows[first : first + 8, :], 0.0)
        span = slice(turn * chunk, (turn + 1) * chunk)
        for c in range(3):
            force = jnp.sum(sums[c], axis=0, keepdims=True)
            velocity_out[c : c + 1, span] = velocity_ref[c : c + 1, span] + step_ref[0] * force
        pull = jnp.sum(sums[3], axis=0, keepdims=True)
        for t in range(tiles):
            mass_rows[turn * tiles + t : turn * tiles + t + 1, :] = pull[:, t * 128 : (t + 1) * 128]
    mass_out[...] = mass_rows[...].astype(BF16)


def read_out(step_size, target, cells, velocity, meshes, grads, weights, scale, slabs):
    count = velocity.shape[1]
    chunk = math.gcd(count, 1024)
    vmem = pl.BlockSpec(memory_space=pltpu.VMEM)
    return pl.pallas_call(
        functools.partial(readout_kernel, slabs, chunk, len(grads), scale),
        in_specs=[pl.BlockSpec(memory_space=pltpu.SMEM)]
        + [vmem] * (3 + len(meshes) + len(grads)),
        out_specs=[vmem] * 5,
        out_shape=[
            jax.ShapeDtypeStruct((3, count), F32),
            jax.ShapeDtypeStruct((count // 128, 128), BF16),
        ]
        + [jax.ShapeDtypeStruct(w.shape, F32) for w in weights],
        scratch_shapes=[
            pltpu.VMEM((2, XL, chunk), BF16),
            pltpu.VMEM((count // 128, 128), F32),
        ],
        compiler_params=pltpu.CompilerParams(vmem_limit_bytes=24 * MIB),
        cost_estimate=pl.CostEstimate(
            flops=slabs * 2 * BLOCK * XL * count, bytes_accessed=1_000_000, transcendentals=0
        ),
    )(step_size, target, cells, velocity, *meshes, *grads)


def shifted(value, axis, distance):
    count = lax.axis_size(axis)
    return lax.ppermute(value, axis, [(i, (i + distance) % count) for i in range(count)])


def from_all(value, axis):
    return [value] + [shifted(value, axis, -k) for k in range(1, lax.axis_size(axis))]


def local(masses, velocity, dest_slab, dest_cell, w_first, w_middle, w_last, step_size, cotangent):
    slabs = lax.axis_size("slab")
    column = ("pencil", "sub")
    count = masses.shape[0]
    dense = (count // 128, 128)
    target, cells = dest_slab.reshape(dense), dest_cell.reshape(dense)
    band_list = bands(w_first, w_middle, w_last)
    parts = paint(step_size, masses.reshape(dense), target, cells, cotangent, slabs)
    arrived = [shifted(parts[k], "slab", k) for k in range(1, slabs)]
    own = functools.reduce(jnp.add, [a.astype(F32) for a in arrived], parts[0]).astype(BF16)
    own, band_list = lax.optimization_barrier((own, band_list))
    blocks = (shifted(own, "slab", 1), own, shifted(own, "slab", -1))
    half = BLOCK // 2
    before = shifted(jnp.concatenate([b[half:] for b in blocks], axis=0), column, 1)
    after = shifted(jnp.concatenate([b[:half] for b in blocks], axis=0), column, -1)
    mesh_own, grads = network(blocks, (before, after), band_list, w_middle.shape[0])
    meshes = from_all(mesh_own, "slab")
    grads = functools.reduce(jnp.add, from_all(grads, column))
    cell_total = ZL * YL * XL * slabs * lax.axis_size("pencil") * lax.axis_size("sub")
    velocity_new, grad_mass, *weight_grads = read_out(
        step_size, target, cells, velocity, meshes, from_all(grads, "slab"),
        (w_first, w_middle, w_last), 1.0 / math.sqrt(cell_total), slabs,
    )
    return (velocity_new, grad_mass.reshape(count), *weight_grads)


def solution(mesh):
    everywhere = ("runs", "slab", "pencil", "sub")
    placed = (
        P(everywhere),
        P(None, everywhere),
        P(everywhere, None),
        P(everywhere),
        P(),
        P(),
        P(),
        P(),
        P(None, everywhere),
    )
    return jax.shard_map(
        local,
        mesh=mesh,
        in_specs=placed,
        out_specs=(
            P(None, everywhere),
            P(everywhere),
            P("runs", None),
            P("runs", None),
            P("runs", None),
        ),
        check_vma=False,
    )
```

time: 69 us -> 56.3 us (0.82)
  Pallas kernels: 22.6 us -> 12.7 us
  waiting for transfers between devices: 13.3 us -> 17.5 us
  other arithmetic: 3.16 us -> 0.06 us
  local copies, waits for them, and re-layouts: 5.45 us -> 3.19 us
  starting transfers between devices: 22.1 us -> 21.1 us
    pallas_call x2, Pallas kernels: 11.2 us -> 5.62 us  [the longest x1 3.26 us: read_out(): pl.pallas_call(functools.partial(readout_kernel, slabs, chunk, len(grads)...]
    ppermute x16, waiting for transfers between devices: 13.3 us -> 17.5 us  [shifted(): lax.ppermute(value, axis, [(i, (i + distance) % count) for i in range(cou...]
    pallas_call x1, Pallas kernels: 8.33 us -> 5.57 us  [network(): pl.pallas_call(net_kernel, out_shape=[jax.ShapeDtypeStruct((BLOCK, XL), B...]
    slice x3 -> x0, local copies, waits for them, and re-layouts: 1.79 us -> none  [the longest x1 0.6 us: local(): grads[8:8 + w_middle.shape[0], 0:w_middle.shape[1]]]
    pallas_call x1, Pallas kernels: 3.08 us -> 1.56 us  [bands(): pl.pallas_call(band_kernel, out_shape=[jax.ShapeDtypeStruct(s, BF16) for...]
    pallas_call x1 -> x0, other arithmetic: 1.45 us -> none  [read_out(): pl.pallas_call(functools.partial(readout_kernel, slabs), grid=(count // c...]
    reshape x1 -> x0, local copies, waits for them, and re-layouts: 1.34 us -> none  [local(): masses.reshape(1, count)]
    ppermute x16, starting transfers between devices: 22.1 us -> 21.1 us  [shifted(): lax.ppermute(value, axis, [(i, (i + distance) % count) for i in range(cou...]
  transfers between devices with their start and end apart: 16 -> 16, of which waited for: 9 -> 9; matrix products, arithmetic and copies ran while one was open for 3% -> 0% of each run, Pallas kernels for 5% -> 3%
where the time goes in v2:
time: 56.3 us; the launch traced here: 56 us
  starting transfers between devices  21.1 us (37%)
  waiting for transfers between devices  17.5 us (31%)
  Pallas kernels  12.7 us (23%)
  local copies, waits for them, and re-layouts  3.19 us (6%)
  between operations  1.43 us (3%)
    ppermute x16, starting transfers between devices, shifted(): lax.ppermute(value, axis, [(i, (i + distance) % count) for i in range(cou...  21.1 us
    ppermute x16, waiting for transfers between devices, shifted(): lax.ppermute(value, axis, [(i, (i + distance) % count) for i in range(cou...  17.5 us
    pallas_call x1, Pallas kernels, network(): pl.pallas_call(net_kernel, out_shape=[jax.ShapeDtypeStruct((BLOCK, XL), B...  5.57 us
    pallas_call x1, Pallas kernels, read_out(): pl.pallas_call(functools.partial(readout_kernel, slabs, chunk, len(grads)...  3.26 us
    unnamed x26, local copies, waits for them, and re-layouts  3.17 us
    pallas_call x1, Pallas kernels, paint(): pl.pallas_call(functools.partial(paint_kernel, slabs, chunk), in_specs=[p...  2.36 us
    pallas_call x1, Pallas kernels, bands(): pl.pallas_call(band_kernel, out_shape=[jax.ShapeDtypeStruct(s, BF16) for...  1.56 us
  transfers between devices with their start and end apart: 16, of which 9 were waited for; matrix products, arithmetic and copies ran while one was open for 0% of the time, Pallas kernels for 3%

profile of v2, /device:TPU:0, one launch (start us, length us, event | category | flops | bytes accessed | tf_op | source)
XLA Modules:
  0.0 56.0 jit_solution(6776632039737953158)
XLA Ops:
  1.3 0.9 %copy-done = f32[3,8192]{1,0:T(4,128)S(1)} copy-done((f32[3,8192]{1,0:T(4,128)S(1)}, f32[3,8192]{1,0:T(4,128)}, u32[]{:S(2)}) %copy-start) | copy-done | bytes 98328
  2.2 0.8 %copy-done.1 = s32[8192,1]{0,1:T(1,128)S(1)} copy-done((s32[8192,1]{0,1:T(1,128)S(1)}, s32[8192,1]{0,1:T(1,128)}, u32[]{:S(2)}) %copy-start.1) | copy-done | bytes 32792
  2.9 0.8 %copy-done.3 = s32[8192]{0:T(1024)S(1)} copy-done((s32[8192]{0:T(1024)S(1)}, s32[8192]{0:T(1024)}, u32[]{:S(2)}) %copy-start.3) | copy-done | bytes 32792
  3.7 0.7 %copy-done.6 = bf16[8192]{0:T(1024)(128)(2,1)S(1)} copy-done((bf16[8192]{0:T(1024)(128)(2,1)S(1)}, bf16[8192]{0:T(1024)(128)(2,1)}, u32[]{:S(2)}) %copy-start.6) | copy-done | bytes 16408
  4.4 2.4 %shard_map.155 = (f32[128,256]{1,0:T(8,128)S(1)}, bf16[128,256]{1,0:T(8,128)(2,1)S(1)}, bf16[128,256]{1,0:T(8,128)(2,1)S(1)}, bf16[128,256]{1,0:T(8,128)(2,1)S(1)}) custom-call(f32[1]{0:T(128)S(6)} %copy.17.step_ref, bf16[64,128]{1,0:T(8,128)(2,1)S(1)} %bitcast.8, s32[64,128]{1,0:T(8,128)S(1)} %bitcast.4, s32[64,128]{1,0:T(8,128)S(1)} %bitcast.6, ...), custom_call_target="tpu_custom_call" | custom-call | tf_op jit(solution)/shard_map/pallas_call | solution.py:99
  6.8 3.1 %collective-permute-start = (bf16[128,256]{1,0:T(8,128)(2,1)S(1)}, bf16[128,256]{1,0:T(8,128)(2,1)S(1)}, u32[]{:S(2)}, u32[]{:S(2)}) collective-permute-start(bf16[128,256]{1,0:T(8,128)(2,1)S(1)} %get-tuple-element.30), channel_id=1, source_target_pairs={{0,4},{4,8},{8,12},{12,0},{1,5},{5,9},{9,13},{13,1},{2,6},{6,10},{... | collective-permute-start | bytes 196616 | tf_op jit(solution)/shard_map/ppermute | solution.py:389
  9.9 2.6 %collective-permute-start.1 = (bf16[128,256]{1,0:T(8,128)(2,1)S(1)}, bf16[128,256]{1,0:T(8,128)(2,1)S(1)}, u32[]{:S(2)}, u32[]{:S(2)}) collective-permute-start(bf16[128,256]{1,0:T(8,128)(2,1)S(1)} %get-tuple-element.31), channel_id=1, source_target_pairs={{0,8},{4,12},{8,0},{12,4},{1,9},{5,13},{9,1},{13,5},{2,10},{6,14},... | collective-permute-start | bytes 196616 | tf_op jit(solution)/shard_map/ppermute | solution.py:389
  12.5 1.3 %collective-permute-start.2 = (bf16[128,256]{1,0:T(8,128)(2,1)S(1)}, bf16[128,256]{1,0:T(8,128)(2,1)S(1)}, u32[]{:S(2)}, u32[]{:S(2)}) collective-permute-start(bf16[128,256]{1,0:T(8,128)(2,1)S(1)} %get-tuple-element.32), channel_id=1, source_target_pairs={{0,12},{4,0},{8,4},{12,8},{1,13},{5,1},{9,5},{13,9},{2,14},{6,2},{... | collective-permute-start | bytes 196616 | tf_op jit(solution)/shard_map/ppermute | solution.py:389
  13.9 1.6 %shard_map.156 = (bf16[128,144]{1,0:T(8,128)(2,1)S(1)}, bf16[128,1152]{1,0:T(8,128)(2,1)S(1)}, bf16[48,1152]{1,0:T(8,128)(2,1)S(1)}, bf16[16,1152]{1,0:T(8,128)(...) custom-call(bf16[8,27]{1,0:T(8,128)(2,1)S(1)} %copy-done.9, bf16[8,216]{1,0:T(8,128)(2,1)S(1)} %copy-done.8, ...), custom_call_target="tpu_custom_call" | custom-call | flops 800000000 | bytes 4000000 | tf_op jit(solution)/shard_map/pallas_call | solution.py:171
  15.4 1.5 %collective-permute-done.1 = bf16[128,256]{1,0:T(8,128)(2,1)S(1)} collective-permute-done((bf16[128,256]{1,0:T(8,128)(2,1)S(1)}, bf16[128,256]{1,0:T(8,128)(2,1)S(1)}, u32[]{:S(2)}, u32[]{:S(2)}) %collective-permute-start.1) | collective-permute-done | bytes 65568 | tf_op jit(solution)/shard_map/ppermute | solution.py:389
  17.2 3.1 %collective-permute-start.4 = (bf16[128,256]{1,0:T(8,128)(2,1)S(1)}, bf16[128,256]{1,0:T(8,128)(2,1)S(1)}, u32[]{:S(2)}, u32[]{:S(2)}) collective-permute-start(bf16[128,256]{1,0:T(8,128)(2,1)S(1)} %add_convert_fusion.own_ref), channel_id=1, source_target_pairs={{0,12},{4,0},{8,4},{12,8},{1,13},{5,1},{9,5},{13,9},{2,14},{6,2},{... | collective-permute-start | bytes 196616 | tf_op jit(solution)/shard_map/ppermute | solution.py:389
  20.3 1.9 %collective-permute-done.4.above_ref = bf16[128,256]{1,0:T(8,128)(2,1)S(1)} collective-permute-done((bf16[128,256]{1,0:T(8,128)(2,1)S(1)}, bf16[128,256]{1,0:T(8,128)(2,1)S(1)}, u32[]{:S(2)}, u32[]{:S(2)}) %collective-permute-start.4) | collective-permute-done | bytes 65568 | tf_op jit(solution)/shard_map/ppermute | solution.py:389
  22.2 4.2 %collective-permute-done.3.below_ref = bf16[128,256]{1,0:T(8,128)(2,1)S(1)} collective-permute-done((bf16[128,256]{1,0:T(8,128)(2,1)S(1)}, bf16[128,256]{1,0:T(8,128)(2,1)S(1)}, u32[]{:S(2)}, u32[]{:S(2)}) %collective-permute-start.3) | collective-permute-done | bytes 65568 | tf_op jit(solution)/shard_map/ppermute | solution.py:389
  26.5 1.8 %collective-permute-start.6 = (bf16[192,256]{1,0:T(8,128)(2,1)S(1)}, bf16[192,256]{1,0:T(8,128)(2,1)S(1)}, u32[]{:S(2)}, u32[]{:S(2)}) collective-permute-start(bf16[192,256]{1,0:T(8,128)(2,1)S(1)} %pad_maximum_fusion.1), channel_id=1, source_target_pairs={{0,3},{1,0},{2,1},{3,2},{4,7},{5,4},{6,5},{7,6},{8,11},{9,8},{10,9... | collective-permute-start | bytes 294920 | tf_op jit(solution)/shard_map/ppermute | solution.py:389
  28.3 2.2 %collective-permute-done.5.before_ref = bf16[192,256]{1,0:T(8,128)(2,1)S(1)} collective-permute-done((bf16[192,256]{1,0:T(8,128)(2,1)S(1)}, bf16[192,256]{1,0:T(8,128)(2,1)S(1)}, u32[]{:S(2)}, u32[]{:S(2)}) %collective-permute-start.5) | collective-permute-done | bytes 98336 | tf_op jit(solution)/shard_map/ppermute | solution.py:389
  30.6 5.6 %shard_map.157 = (bf16[128,256]{1,0:T(8,128)(2,1)S(1)}, f32[24,256]{1,0:T(8,128)S(1)}) custom-call(bf16[128,256]{1,0:T(8,128)(2,1)S(1)} %collective-permute-done.3.below_ref, bf16[128,256]{1,0:T(8,128)(2,1)S(1)} %add_convert_fusion.own_ref, bf16[128,256]{1,0:T(8,128)(2,1)S(1)} %collective-permute-done.4.above_ref, ...), custom_call_target="tpu_custom_call" | custom-call | tf_op jit(solution)/shard_map/pallas_call | solution.py:303
  36.1 1.6 %collective-permute-start.12 = (f32[24,256]{1,0:T(8,128)S(1)}, f32[24,256]{1,0:T(8,128)S(1)}, u32[]{:S(2)}, u32[]{:S(2)}) collective-permute-start(f32[24,256]{1,0:T(8,128)S(1)} %get-tuple-element.47), channel_id=1, source_target_pairs={{0,1},{1,2},{2,3},{3,0},{4,5},{5,6},{6,7},{7,4},{8,9},{9,10},{10,1... | collective-permute-start | bytes 73736 | tf_op jit(solution)/shard_map/ppermute | solution.py:389
  37.8 0.7 %collective-permute-start.11 = (f32[24,256]{1,0:T(8,128)S(1)}, f32[24,256]{1,0:T(8,128)S(1)}, u32[]{:S(2)}, u32[]{:S(2)}) collective-permute-start(f32[24,256]{1,0:T(8,128)S(1)} %get-tuple-element.47), channel_id=1, source_target_pairs={{0,2},{1,3},{2,0},{3,1},{4,6},{5,7},{6,4},{7,5},{8,10},{9,11},{10,... | collective-permute-start | bytes 73736 | tf_op jit(solution)/shard_map/ppermute | solution.py:389
  38.5 0.8 %collective-permute-start.10 = (f32[24,256]{1,0:T(8,128)S(1)}, f32[24,256]{1,0:T(8,128)S(1)}, u32[]{:S(2)}, u32[]{:S(2)}) collective-permute-start(f32[24,256]{1,0:T(8,128)S(1)} %get-tuple-element.47), channel_id=1, source_target_pairs={{0,3},{1,0},{2,1},{3,2},{4,7},{5,4},{6,5},{7,6},{8,11},{9,8},{10,9... | collective-permute-start | bytes 73736 | tf_op jit(solution)/shard_map/ppermute | solution.py:389
  39.8 3.2 %collective-permute-start.7 = (bf16[128,256]{1,0:T(8,128)(2,1)S(1)}, bf16[128,256]{1,0:T(8,128)(2,1)S(1)}, u32[]{:S(2)}, u32[]{:S(2)}) collective-permute-start(bf16[128,256]{1,0:T(8,128)(2,1)S(1)} %get-tuple-element.46.rest_0_), channel_id=1, source_target_pairs={{0,12},{4,0},{8,4},{12,8},{1,13},{5,1},{9,5},{13,9},{2,14},{6,2},{... | collective-permute-start | bytes 196616 | tf_op jit(solution)/shard_map/ppermute | solution.py:389
  43.7 1.5 %collective-permute-start.14 = (f32[24,256]{1,0:T(8,128)S(1)}, f32[24,256]{1,0:T(8,128)S(1)}, u32[]{:S(2)}, u32[]{:S(2)}) collective-permute-start(f32[24,256]{1,0:T(8,128)S(1)} %add_add_fusion.rest_4_), channel_id=1, source_target_pairs={{0,8},{4,12},{8,0},{12,4},{1,9},{5,13},{9,1},{13,5},{2,10},{6,14},... | collective-permute-start | bytes 73736 | tf_op jit(solution)/shard_map/ppermute | solution.py:389
  45.2 3.6 %collective-permute-done.15.rest_7_ = f32[24,256]{1,0:T(8,128)S(1)} collective-permute-done((f32[24,256]{1,0:T(8,128)S(1)}, f32[24,256]{1,0:T(8,128)S(1)}, u32[]{:S(2)}, u32[]{:S(2)}) %collective-permute-start.15) | collective-permute-done | bytes 24608 | tf_op jit(solution)/shard_map/ppermute | solution.py:389
  49.6 3.1 %collective-permute-done.13.rest_5_ = f32[24,256]{1,0:T(8,128)S(1)} collective-permute-done((f32[24,256]{1,0:T(8,128)S(1)}, f32[24,256]{1,0:T(8,128)S(1)}, u32[]{:S(2)}, u32[]{:S(2)}) %collective-permute-start.13) | collective-permute-done | bytes 24608 | tf_op jit(solution)/shard_map/ppermute | solution.py:389
  52.7 3.3 %shard_map.158 = (f32[3,8192]{1,0:T(4,128)}, bf16[64,128]{1,0:T(8,128)(2,1)}, f32[8,27]{1,0:T(8,128)}, f32[8,216]{1,0:T(8,128)}, f32[3,216]{1,0:T(4,128)}) custom-call(f32[1]{0:T(128)S(6)} %copy.17.step_ref, s32[64,128]{1,0:T(8,128)S(1)} %bitcast.5, s32[64,128]{1,0:T(8,128)S(1)} %bitcast.7, f32[3,8192]{1,0:T(4,128)S(1)} %copy-done.7, ...), custom_call_target="tpu_custom_call" | custom-call | flops 2147483648 | bytes 1000000 | tf_op jit(solution)/shard_map/pallas_call | solution.py:366
  (45 shorter events, 2.5 us)
Async XLA Ops:
  4.4 9.4 %copy-start.9 = (bf16[8,27]{1,0:T(8,128)(2,1)S(1)}, bf16[8,27]{1,0:T(8,128)(2,1)}, u32[]{:S(2)}) copy-start(bf16[8,27]{1,0:T(8,128)(2,1)} %first_ref.1) | copy-start | bytes 1300
  4.4 9.4 %copy-start.10 = (bf16[3,216]{1,0:T(4,128)(2,1)S(1)}, bf16[3,216]{1,0:T(4,128)(2,1)}, u32[]{:S(2)}) copy-start(bf16[3,216]{1,0:T(4,128)(2,1)} %last_ref.1) | copy-start | bytes 3892
  4.4 9.4 %copy-start.11 = (s32[8,1152]{1,0:T(8,128)S(1)}, s32[8,1152]{1,0:T(8,128)}, u32[]{:S(2)}) copy-start(s32[8,1152]{1,0:T(8,128)} %constant.7.clone.many_ref) | copy-start | bytes 110596
  4.4 9.4 %copy-start.12 = (s32[8,144]{1,0:T(8,128)S(1)}, s32[8,144]{1,0:T(8,128)}, u32[]{:S(2)}) copy-start(s32[8,144]{1,0:T(8,128)} %constant.6.clone.one_ref) | copy-start | bytes 13828
  6.8 7.0 %copy-start.8 = (bf16[8,216]{1,0:T(8,128)(2,1)S(1)}, bf16[8,216]{1,0:T(8,128)(2,1)}, u32[]{:S(2)}) copy-start(bf16[8,216]{1,0:T(8,128)(2,1)} %middle_ref.1) | copy-start | bytes 10372
  6.8 8.6 %collective-permute-start = (bf16[128,256]{1,0:T(8,128)(2,1)S(1)}, bf16[128,256]{1,0:T(8,128)(2,1)S(1)}, u32[]{:S(2)}, u32[]{:S(2)}) collective-permute-start(bf16[128,256]{1,0:T(8,128)(2,1)S(1)} %get-tuple-element.30), channel_id=1, source_target_pairs={{0,4},{4,8},{8,12},{12,0},{1,5},{5,9},{9,13},{13,1},{2,6},{6,10},{... | collective-permute-start | bytes 196616 | tf_op jit(solution)/shard_map/ppermute | solution.py:389
  9.9 7.1 %collective-permute-start.1 = (bf16[128,256]{1,0:T(8,128)(2,1)S(1)}, bf16[128,256]{1,0:T(8,128)(2,1)S(1)}, u32[]{:S(2)}, u32[]{:S(2)}) collective-permute-start(bf16[128,256]{1,0:T(8,128)(2,1)S(1)} %get-tuple-element.31), channel_id=1, source_target_pairs={{0,8},{4,12},{8,0},{12,4},{1,9},{5,13},{9,1},{13,5},{2,10},{6,14},... | collective-permute-start | bytes 196616 | tf_op jit(solution)/shard_map/ppermute | solution.py:389
  12.5 4.7 %collective-permute-start.2 = (bf16[128,256]{1,0:T(8,128)(2,1)S(1)}, bf16[128,256]{1,0:T(8,128)(2,1)S(1)}, u32[]{:S(2)}, u32[]{:S(2)}) collective-permute-start(bf16[128,256]{1,0:T(8,128)(2,1)S(1)} %get-tuple-element.32), channel_id=1, source_target_pairs={{0,12},{4,0},{8,4},{12,8},{1,13},{5,1},{9,5},{13,9},{2,14},{6,2},{... | collective-permute-start | bytes 196616 | tf_op jit(solution)/shard_map/ppermute | solution.py:389
  17.2 5.0 %collective-permute-start.4 = (bf16[128,256]{1,0:T(8,128)(2,1)S(1)}, bf16[128,256]{1,0:T(8,128)(2,1)S(1)}, u32[]{:S(2)}, u32[]{:S(2)}) collective-permute-start(bf16[128,256]{1,0:T(8,128)(2,1)S(1)} %add_convert_fusion.own_ref), channel_id=1, source_target_pairs={{0,12},{4,0},{8,4},{12,8},{1,13},{5,1},{9,5},{13,9},{2,14},{6,2},{... | collective-permute-start | bytes 196616 | tf_op jit(solution)/shard_map/ppermute | solution.py:389
  20.3 6.1 %collective-permute-start.3 = (bf16[128,256]{1,0:T(8,128)(2,1)S(1)}, bf16[128,256]{1,0:T(8,128)(2,1)S(1)}, u32[]{:S(2)}, u32[]{:S(2)}) collective-permute-start(bf16[128,256]{1,0:T(8,128)(2,1)S(1)} %add_convert_fusion.own_ref), channel_id=1, source_target_pairs={{0,4},{4,8},{8,12},{12,0},{1,5},{5,9},{9,13},{13,1},{2,6},{6,10},{... | collective-permute-start | bytes 196616 | tf_op jit(solution)/shard_map/ppermute | solution.py:389
  26.4 4.1 %collective-permute-start.5 = (bf16[192,256]{1,0:T(8,128)(2,1)S(1)}, bf16[192,256]{1,0:T(8,128)(2,1)S(1)}, u32[]{:S(2)}, u32[]{:S(2)}) collective-permute-start(bf16[192,256]{1,0:T(8,128)(2,1)S(1)} %pad_maximum_fusion), channel_id=1, source_target_pairs={{0,1},{1,2},{2,3},{3,0},{4,5},{5,6},{6,7},{7,4},{8,9},{9,10},{10,1... | collective-permute-start | bytes 294920 | tf_op jit(solution)/shard_map/ppermute | solution.py:389
  26.5 26.2 %copy-start.7 = (f32[3,8192]{1,0:T(4,128)S(1)}, f32[3,8192]{1,0:T(4,128)}, u32[]{:S(2)}) copy-start(f32[3,8192]{1,0:T(4,128)} %velocity_ref.1) | copy-start | bytes 294916
  26.5 4.1 %collective-permute-start.6 = (bf16[192,256]{1,0:T(8,128)(2,1)S(1)}, bf16[192,256]{1,0:T(8,128)(2,1)S(1)}, u32[]{:S(2)}, u32[]{:S(2)}) collective-permute-start(bf16[192,256]{1,0:T(8,128)(2,1)S(1)} %pad_maximum_fusion.1), channel_id=1, source_target_pairs={{0,3},{1,0},{2,1},{3,2},{4,7},{5,4},{6,5},{7,6},{8,11},{9,8},{10,9... | collective-permute-start | bytes 294920 | tf_op jit(solution)/shard_map/ppermute | solution.py:389
  36.1 3.7 %collective-permute-start.12 = (f32[24,256]{1,0:T(8,128)S(1)}, f32[24,256]{1,0:T(8,128)S(1)}, u32[]{:S(2)}, u32[]{:S(2)}) collective-permute-start(f32[24,256]{1,0:T(8,128)S(1)} %get-tuple-element.47), channel_id=1, source_target_pairs={{0,1},{1,2},{2,3},{3,0},{4,5},{5,6},{6,7},{7,4},{8,9},{9,10},{10,1... | collective-permute-start | bytes 73736 | tf_op jit(solution)/shard_map/ppermute | solution.py:389
  37.8 5.3 %collective-permute-start.11 = (f32[24,256]{1,0:T(8,128)S(1)}, f32[24,256]{1,0:T(8,128)S(1)}, u32[]{:S(2)}, u32[]{:S(2)}) collective-permute-start(f32[24,256]{1,0:T(8,128)S(1)} %get-tuple-element.47), channel_id=1, source_target_pairs={{0,2},{1,3},{2,0},{3,1},{4,6},{5,7},{6,4},{7,5},{8,10},{9,11},{10,... | collective-permute-start | bytes 73736 | tf_op jit(solution)/shard_map/ppermute | solution.py:389
  38.5 4.6 %collective-permute-start.10 = (f32[24,256]{1,0:T(8,128)S(1)}, f32[24,256]{1,0:T(8,128)S(1)}, u32[]{:S(2)}, u32[]{:S(2)}) collective-permute-start(f32[24,256]{1,0:T(8,128)S(1)} %get-tuple-element.47), channel_id=1, source_target_pairs={{0,3},{1,0},{2,1},{3,2},{4,7},{5,4},{6,5},{7,6},{8,11},{9,8},{10,9... | collective-permute-start | bytes 73736 | tf_op jit(solution)/shard_map/ppermute | solution.py:389
  39.2 13.5 %copy-start.2 = (s32[8192,1]{0,1:T(1,128)S(1)}, s32[8192,1]{0,1:T(1,128)}, u32[]{:S(2)}) copy-start(s32[8192,1]{0,1:T(1,128)} %param.14) | copy-start | bytes 98308
  39.2 13.5 %copy-start.4 = (s32[8192]{0:T(1024)S(1)}, s32[8192]{0:T(1024)}, u32[]{:S(2)}) copy-start(s32[8192]{0:T(1024)} %param.15) | copy-start | bytes 98308
  39.2 13.5 %collective-permute-start.9 = (bf16[128,256]{1,0:T(8,128)(2,1)S(1)}, bf16[128,256]{1,0:T(8,128)(2,1)S(1)}, u32[]{:S(2)}, u32[]{:S(2)}) collective-permute-start(bf16[128,256]{1,0:T(8,128)(2,1)S(1)} %get-tuple-element.46.rest_0_), channel_id=1, source_target_pairs={{0,4},{4,8},{8,12},{12,0},{1,5},{5,9},{9,13},{13,1},{2,6},{6,10},{... | collective-permute-start | bytes 196616 | tf_op jit(solution)/shard_map/ppermute | solution.py:389
  39.2 13.5 %collective-permute-start.8 = (bf16[128,256]{1,0:T(8,128)(2,1)S(1)}, bf16[128,256]{1,0:T(8,128)(2,1)S(1)}, u32[]{:S(2)}, u32[]{:S(2)}) collective-permute-start(bf16[128,256]{1,0:T(8,128)(2,1)S(1)} %get-tuple-element.46.rest_0_), channel_id=1, source_target_pairs={{0,8},{4,12},{8,0},{12,4},{1,9},{5,13},{9,1},{13,5},{2,10},{6,14},... | collective-permute-start | bytes 196616 | tf_op jit(solution)/shard_map/ppermute | solution.py:389
  39.8 12.9 %collective-permute-start.7 = (bf16[128,256]{1,0:T(8,128)(2,1)S(1)}, bf16[128,256]{1,0:T(8,128)(2,1)S(1)}, u32[]{:S(2)}, u32[]{:S(2)}) collective-permute-start(bf16[128,256]{1,0:T(8,128)(2,1)S(1)} %get-tuple-element.46.rest_0_), channel_id=1, source_target_pairs={{0,12},{4,0},{8,4},{12,8},{1,13},{5,1},{9,5},{13,9},{2,14},{6,2},{... | collective-permute-start | bytes 196616 | tf_op jit(solution)/shard_map/ppermute | solution.py:389
  43.1 5.8 %collective-permute-start.15 = (f32[24,256]{1,0:T(8,128)S(1)}, f32[24,256]{1,0:T(8,128)S(1)}, u32[]{:S(2)}, u32[]{:S(2)}) collective-permute-start(f32[24,256]{1,0:T(8,128)S(1)} %add_add_fusion.rest_4_), channel_id=1, source_target_pairs={{0,4},{4,8},{8,12},{12,0},{1,5},{5,9},{9,13},{13,1},{2,6},{6,10},{... | collective-permute-start | bytes 73736 | tf_op jit(solution)/shard_map/ppermute | solution.py:389
  43.7 5.9 %collective-permute-start.14 = (f32[24,256]{1,0:T(8,128)S(1)}, f32[24,256]{1,0:T(8,128)S(1)}, u32[]{:S(2)}, u32[]{:S(2)}) collective-permute-start(f32[24,256]{1,0:T(8,128)S(1)} %add_add_fusion.rest_4_), channel_id=1, source_target_pairs={{0,8},{4,12},{8,0},{12,4},{1,9},{5,13},{9,1},{13,5},{2,10},{6,14},... | collective-permute-start | bytes 73736 | tf_op jit(solution)/shard_map/ppermute | solution.py:389
  48.9 3.8 %collective-permute-start.13 = (f32[24,256]{1,0:T(8,128)S(1)}, f32[24,256]{1,0:T(8,128)S(1)}, u32[]{:S(2)}, u32[]{:S(2)}) collective-permute-start(f32[24,256]{1,0:T(8,128)S(1)} %add_add_fusion.rest_4_), channel_id=1, source_target_pairs={{0,12},{4,0},{8,4},{12,8},{1,13},{5,1},{9,5},{13,9},{2,14},{6,2},{... | collective-permute-start | bytes 73736 | tf_op jit(solution)/shard_map/ppermute | solution.py:389
  (5 other events, 7.2 us)

commit v3 on v2

v3 whole, which is shorter than its diff:
```python
import functools
import math

import jax
import jax.numpy as jnp
import numpy as np
from jax import lax
from jax.experimental import pallas as pl
from jax.experimental.pallas import tpu as pltpu
from jax.sharding import PartitionSpec as P

ZL = 4
YL = 8
XL = 256
ROWS = ZL * YL
FIELDS = 4
POS = 16
HALF = POS // 4
BF16 = jnp.bfloat16
F32 = jnp.float32
NT = (((1,), (1,)), ((), ()))
MIB = 1024 * 1024
VMEM = pl.BlockSpec(memory_space=pltpu.VMEM)
SMEM = pl.BlockSpec(memory_space=pltpu.SMEM)


def dot(a, b):
    return jnp.dot(a, b, preferred_element_type=F32)


def dot_nt(a, b):
    return lax.dot_general(a, b, NT, preferred_element_type=F32)


def row_iota(shape, dim):
    return lax.broadcasted_iota(jnp.int32, shape, dim)


def limit(size):
    return pltpu.CompilerParams(vmem_limit_bytes=size)


def pack_kernel(step_ref, mass_ref, slab_ref, cell_ref, cot_ref, out_ref, rows):
    tiles = mass_ref.shape[0]
    cell, slab = cell_ref[...], slab_ref[...]
    z, y = cell >> 11, (cell >> 8) & 7
    code = ((slab & 7) << 5) + ((y >> 2) << 4) + (z << 2) + (y & 3)
    for component in range(3):
        for t in range(tiles):
            row = component * tiles + t
            rows[row : row + 1, :] = cot_ref[component : component + 1, t * 128 : (t + 1) * 128]
    out_ref[0:tiles, :] = mass_ref[...]
    out_ref[tiles : 4 * tiles, :] = (step_ref[0] * rows[...]).astype(BF16)
    out_ref[4 * tiles : 5 * tiles, :] = code.astype(F32).astype(BF16)
    out_ref[5 * tiles : 6 * tiles, :] = (cell & (XL - 1)).astype(F32).astype(BF16)
    if out_ref.shape[0] > 6 * tiles:
        out_ref[6 * tiles : 7 * tiles, :] = (slab >> 3).astype(F32).astype(BF16)


def pack(step_size, masses, target, cells, cotangent, slabs):
    tiles = masses.shape[0]
    return pl.pallas_call(
        pack_kernel,
        in_specs=[SMEM] + [VMEM] * 4,
        out_specs=VMEM,
        out_shape=jax.ShapeDtypeStruct(((6 if slabs <= 8 else 7) * tiles, 128), BF16),
        scratch_shapes=[pltpu.VMEM((3 * tiles, 128), F32)],
        compiler_params=limit(60 * MIB),
    )(step_size, masses, target, cells, cotangent)


def spread_rows(dense, height, first, count):
    tiles = [
        jnp.broadcast_to(dense[t : t + 1, :], (height, 128)) for t in range(first, first + count)
    ]
    return jnp.concatenate(tiles, axis=1)


def fill_lane_hot(store, lane, chunk):
    sixteen = row_iota((16, chunk), 0)
    zero, one = jnp.zeros((16, chunk), BF16), jnp.ones((16, chunk), BF16)
    for group in range(XL // 16):
        same = lane == (sixteen + 16 * group).astype(F32).astype(BF16)
        store[16 * group : 16 * group + 16, :] = jnp.where(same, one, zero)


def paint_kernel(slabs, chunk, tiles, started, final, *refs):
    before, refs = (refs[0], refs[1:]) if started else (None, refs)
    message, refs = refs[0], refs[1:]
    outs, (hot, lane_hot, total) = refs[:-3], refs[-3:]
    step = chunk // 128
    sixteen = row_iota((16, chunk), 0)
    zero = jnp.zeros((16, chunk), BF16)
    for turn in range(tiles // step):
        here, here_lane = hot.at[turn % 2], lane_hot.at[turn % 2]

        def spread(field):
            rows = message[field * tiles : (field + 1) * tiles, :].astype(F32)
            return spread_rows(rows, 16, turn * step, step)

        fill_lane_hot(here_lane, spread(5).astype(BF16), chunk)
        values = [spread(field).astype(BF16) for field in range(FIELDS)]
        code = spread(4)
        for eight in range(0, slabs, 8):
            code_tile = code if slabs <= 8 else jnp.where(spread(6) == eight // 8, code, -1.0)
            code_tile = code_tile.astype(BF16)
            for slab in range(eight, min(eight + 8, slabs)):
                for half in range(2):
                    place = ((slab - eight) * 2 + half) * 16
                    same = code_tile == (sixteen + place).astype(F32).astype(BF16)
                    for field in range(FIELDS):
                        first = ((half * FIELDS + field) * slabs + slab) * 16
                        here[first : first + 16, :] = jnp.where(same, values[field], zero)
        part = dot_nt(here[...], here_lane[...])
        if turn > 0:
            total[...] += part
        elif started:
            total[...] = before[...] + part
        else:
            total[...] = part
    if final:
        middle = total.shape[0] // 2
        outs[0][...] = total[:middle, :].astype(BF16)
        outs[1][...] = total[middle:, :].astype(BF16)
    else:
        outs[0][...] = total[...]


def paint(before, message, tiles, slabs, final):
    chunk = 128 * math.gcd(tiles, 16)
    height = 2 * FIELDS * slabs * 16
    scratch = 2 * chunk * (height + XL) * 2 + height * XL * 4
    shapes = [jax.ShapeDtypeStruct((height, XL), F32)]
    if final:
        shapes = [jax.ShapeDtypeStruct((height // 2, XL), BF16)] * 2
    given = [message] if before is None else [before, message]
    return pl.pallas_call(
        functools.partial(paint_kernel, slabs, chunk, tiles, before is not None, final),
        in_specs=[VMEM] * len(given),
        out_specs=[VMEM] * len(shapes),
        out_shape=shapes,
        scratch_shapes=[
            pltpu.VMEM((2, height, chunk), BF16),
            pltpu.VMEM((2, XL, chunk), BF16),
            pltpu.VMEM((height, XL), F32),
        ],
        compiler_params=limit(scratch + height * XL * 12 + 8 * MIB),
        cost_estimate=pl.CostEstimate(
            flops=2 * height * XL * tiles * 128, bytes_accessed=MIB, transcendentals=0
        ),
    )(*given)


def y_of(place):
    rest = place - 8
    if isinstance(place, np.ndarray):
        return np.where(place < 8, place + 4, np.where(rest % 2 == 0, 12 + rest // 2, 3 - rest // 2))
    halo = jnp.where((rest & 1) == 0, 12 + (rest >> 1), 3 - (rest >> 1))
    return jnp.where(place < 8, place + 4, halo)


def columns(rows, channels):
    col = np.arange(9 * rows * channels)
    pair, place, channel = col // (rows * channels), col // channels % rows, col % channels
    taps = [((pair // 3 * 3 + b) * 3 + pair % 3) * channels + channel for b in range(3)]
    return np.stack(taps + [y_of(place)] + [np.zeros_like(col)] * 4).astype(np.int32)


def window_columns(rows, channels):
    col = np.arange(3 * rows * channels)
    listed = [y_of(col // channels % rows), col // (rows * channels) * channels + col % channels]
    return np.stack(listed + [np.zeros_like(col)] * 6).astype(np.int32)


def band(weight, table, row_channel, row_place):
    outs, count = weight.shape
    width = table.shape[1]
    rows = row_channel.shape[0]
    pick = jnp.where(row_channel[:, 0:outs] == row_iota((rows, outs), 1), 1.0, 0.0)
    spread = dot(pick.astype(BF16), weight).astype(BF16)
    distance = table[3:4, :] - y_of(row_place)
    result = jnp.zeros((rows, width), F32)
    for b in range(3):
        same = row_iota((count, width), 0) == table[b : b + 1, :]
        picked = dot(spread, jnp.where(same, 1.0, 0.0).astype(BF16))
        result = jnp.where(distance == b - 1, picked, result)
    return result


def band_kernel(
    first_ref, middle_ref, last_ref, c1_ref, c2_ref, c3_ref,
    b1_ref, b2_ref, b3_ref, t1_ref, t2_ref, t3_ref,
):
    channels = first_ref.shape[0]
    bits = channels.bit_length() - 1

    def mixed(rows, width):
        row = row_iota((rows, width), 0)
        return row & (channels - 1), row >> bits

    def turned(full, pair, width, rows, out_ref):
        block = full[:, pair * width : (pair + 1) * width].T[0:rows].astype(BF16)
        out_ref[:, (8 - pair) * block.shape[1] : (9 - pair) * block.shape[1]] = block

    def stack(out_ref, pair, block):
        rows, width = block.shape
        first = pair % 3 * width
        out_ref[pair // 3 * rows : (pair // 3 + 1) * rows, first : first + width] = block

    rows = b1_ref.shape[0]
    table = c1_ref[...]
    full = band(first_ref[...], table, mixed(rows, 128)[0], mixed(rows, table.shape[1])[1])
    b1_ref[...] = full.astype(BF16)
    short = t1_ref.shape[1] // 3
    for pair in range(9):
        stack(t1_ref, 8 - pair, full[0:short, pair * POS : (pair + 1) * POS].T.astype(BF16))
    rows = b2_ref.shape[0]
    table = c2_ref[...]
    full = band(middle_ref[...], table, mixed(rows, 128)[0], mixed(rows, table.shape[1])[1])
    b2_ref[...] = full.astype(BF16)
    for pair in range(9):
        turned(full, pair, full.shape[1] // 9, t2_ref.shape[0], t2_ref)
    rows = 3 * POS
    table = c3_ref[...]
    channel = row_iota((rows, 128), 0) >> 4
    full = band(last_ref[...], table, channel, row_iota((rows, table.shape[1]), 0) & (POS - 1))
    width, short = full.shape[1] // 9, b3_ref.shape[1] // 3
    own = [full[o * POS : o * POS + YL] for o in range(3)] + [jnp.zeros((YL, full.shape[1]), F32)]
    own = jnp.concatenate(own, axis=0).astype(BF16)
    for pair in range(9):
        stack(b3_ref, pair, own[:, pair * width : pair * width + short])
        turned(full, pair, width, t3_ref.shape[0], t3_ref)


def bands(w_first, w_middle, w_last):
    c = w_middle.shape[0]
    tables = [jnp.asarray(t) for t in (columns(16, 1), columns(14, c), columns(12, c))]
    shapes = [
        (14 * c, 9 * 16), (12 * c, 9 * 14 * c), (3 * 4 * YL, 3 * 10 * c),
        (3 * POS, 3 * 10 * c), (10 * c, 9 * 12 * c), (12 * c, 9 * 3 * POS),
    ]
    return pl.pallas_call(
        band_kernel,
        in_specs=[VMEM] * 6,
        out_specs=[VMEM] * 6,
        out_shape=[jax.ShapeDtypeStruct(s, BF16) for s in shapes],
        compiler_params=limit(20 * MIB),
        cost_estimate=pl.CostEstimate(
            flops=800_000_000, bytes_accessed=4_000_000, transcendentals=0
        ),
    )(w_first, w_middle, w_last, *tables)


def slope(pre, sigma):
    return sigma * (1.0 + pre * (1.0 - sigma))


def split_three(value):
    high = value.astype(BF16).astype(F32)
    rest = value - high
    mid = rest.astype(BF16).astype(F32)
    return jnp.concatenate([high, mid, rest - mid], axis=0).astype(BF16)


def weight_sum(full, table, channels, mixed, outs):
    count, width = full.shape[0] // 3, full.shape[1]
    group = row_iota((3 * channels, width), 0) == table[1:2, :]
    group = jnp.where(group, 1.0, 0.0).astype(BF16)
    picked = []
    for b in range(3):
        for e in range(3):
            block = full[e * count : (e + 1) * count, :]
            if mixed:
                parts = [
                    jnp.where(table[0:1, :] == place + 3 + b, block[place * 8 : place * 8 + 8, :], 0.0)
                    for place in range(YL)
                ]
                picked.append(functools.reduce(jnp.add, parts))
                continue
            wanted = table[0:1, :] - row_iota((YL, width), 0) == 3 + b
            rows = [
                jnp.sum(
                    jnp.where(wanted, block[o * POS : o * POS + YL, :], 0.0), axis=0, keepdims=True
                )
                for o in range(outs)
            ]
            picked.append(jnp.concatenate(rows + [jnp.zeros_like(rows[0])] * (8 - outs), axis=0))
    parts = dot_nt(split_three(jnp.concatenate(picked, axis=0)), group)
    total = parts[0:72] + parts[72:144] + parts[144:216]
    pieces = [
        total[pair * 8 : pair * 8 + 8, a * channels : (a + 1) * channels]
        for a in range(3)
        for pair in range(9)
    ]
    return jnp.concatenate(pieces, axis=1)


class Store:
    def __init__(self, ref, depth, rows):
        self.ref, self.depth, self.rows = ref, depth, rows

    def put(self, plane, value, first=0):
        places = [plane + 1]
        if plane == 0:
            places.append(self.depth + 1)
        if plane == self.depth - 1:
            places.append(0)
        for e, shift in enumerate((1, 0, XL - 1)):
            moved = (value if shift == 0 else pltpu.roll(value, shift, 1)).astype(BF16)
            for place in places:
                row = (place * 3 + e) * self.rows + first
                self.ref[row : row + value.shape[0], :] = moved

    def window(self, plane):
        return self.ref[plane * 3 * self.rows : (plane + 3) * 3 * self.rows, :]

    def plane(self, plane):
        return self.ref[(plane + 1) * 3 * self.rows : (plane + 2) * 3 * self.rows, :]

    def shifted(self, plane, e, count):
        row = ((plane + 1) * 3 + e) * self.rows
        return self.ref[row : row + count, :]


def products(delta, count, source, depth):
    total = None
    for plane in range(0, depth, 4):
        left, right = [
            jnp.concatenate([rows(plane + k) for k in range(4)], axis=1)
            for rows in (
                lambda p: jnp.concatenate([delta.shifted(p, e, count) for e in (2, 1, 0)], axis=0),
                lambda p: jnp.concatenate(
                    [source.shifted(p + a, 1, source.rows) for a in (-1, 0, 1)], axis=0
                ),
            )
        ]
        if source.rows < count:
            term = dot_nt(left, right)
        else:
            term = dot_nt(right, left)
        total = term if total is None else total + term
    return total if source.rows < count else total.T


def stacked(weight, store, depth):
    rows = weight.shape[0] // 3
    parts = [dot(weight, store.plane(plane)) for plane in range(depth)]
    return [
        parts[(plane - 1) % depth][0:rows]
        + parts[plane][rows : 2 * rows]
        + parts[(plane + 1) % depth][2 * rows :]
        for plane in range(depth)
    ]


def net_kernel(
    slabs, channels, shared,
    low_ref, high_ref, after_ref, before_ref,
    b1_ref, b2_ref, b3_ref, t1_ref, t2_ref, t3_ref, order_ref, c1_ref, c2_ref, c3_ref,
    mesh_ref, grads_ref,
    s0_ref, sg_ref, a_ref, b_ref, slope1, slope2, fields, *more,
):
    depth = slabs * ZL
    s0, sg = Store(s0_ref, depth, POS), Store(sg_ref, depth, 3 * POS)
    s1, s2 = Store(a_ref, depth, 14 * channels), Store(b_ref, depth, 10 * channels)
    d2 = Store(b_ref if shared else more[0], depth, 12 * channels)
    d1 = Store(a_ref if shared else more[1], depth, 10 * channels)
    order = order_ref[...]
    for slab in range(slabs):
        for c in range(FIELDS):
            first = (c * slabs + slab) * 16
            pieces = [ref[first : first + 16, :] for ref in (low_ref, high_ref, after_ref, before_ref)]
            rows = dot(order, jnp.concatenate(pieces, axis=0))
            for z in range(ZL):
                value = rows[z * POS : (z + 1) * POS, :]
                if c == 0:
                    s0.put(slab * ZL + z, value)
                else:
                    sg.put(slab * ZL + z, value, (c - 1) * POS)
    grads_ref[...] = jnp.zeros_like(grads_ref)
    inner, outer = 10 * channels, 12 * channels
    b1 = b1_ref[...]
    for plane in range(depth):
        pre = dot(b1, s0.window(plane))
        sigma = jax.nn.sigmoid(pre)
        s1.put(plane, pre * sigma)
        slope1[plane] = slope(pre[0:inner], sigma[0:inner])
    b2 = b2_ref[...]
    for plane in range(depth):
        pre = dot(b2, s1.window(plane))
        sigma = jax.nn.sigmoid(pre)
        s2.put(plane, pre[0:inner] * sigma[0:inner])
        slope2[plane] = slope(pre, sigma)

    def place(plane, field):
        first = (plane // ZL * FIELDS + field) * ROWS + plane % ZL * YL
        return slice(first, first + YL)

    for plane, force in enumerate(stacked(b3_ref[...], s2, depth)):
        for c in range(3):
            fields[place(plane, c), :] = force[c * YL : (c + 1) * YL, :]
    full = products(sg, 3 * POS, s2, depth)
    grads_ref[16:24, 0 : 27 * channels] = weight_sum(full, c3_ref[...], channels, False, 3)
    t3 = t3_ref[...]
    for plane in range(depth):
        d2.put(plane, dot(t3, sg.window(plane)) * slope2[plane])
    full = products(d2, YL * channels, s1, depth)
    grads_ref[8:16, 0 : 27 * channels] = weight_sum(full, c2_ref[...], channels, True, channels)
    t2 = t2_ref[...]
    for plane in range(depth):
        d1.put(plane, dot(t2, d2.window(plane)) * slope1[plane])
    full = products(d1, YL * channels, s0, depth)
    grads_ref[0:8, 0:27] = weight_sum(full, c1_ref[...], 1, True, channels)
    for plane, pull in enumerate(stacked(t1_ref[...], d1, depth)):
        fields[place(plane, 3), :] = pull[0:YL, :]
    mesh_ref[...] = fields[...].astype(BF16)


def network(halves, band_list, channels, slabs):
    depth = slabs * ZL
    order = np.zeros((64, 64), np.float32)
    for z in range(4):
        for y in range(4):
            for h, place in enumerate((y, 4 + y, 8 + 2 * y, 15 - 2 * y)):
                order[z * 16 + place, h * 16 + z * 4 + y] = 1.0
    planes = 3 * (depth + 2)
    shared = slabs > 4
    sizes = [POS, 3 * POS, 14 * channels, (12 if shared else 10) * channels]
    stores = [pltpu.VMEM((planes * n, XL), BF16) for n in sizes]
    more = [] if shared else [12 * channels, 10 * channels]
    slopes = [pltpu.VMEM((depth, n * channels, XL), F32) for n in (10, 12)]
    size = sum(sizes + more) * planes * XL * 2 + (22 * channels + 32) * depth * XL * 4
    tables = [jnp.asarray(t) for t in (window_columns(16, 1), window_columns(14, channels), window_columns(10, channels))]
    given = (*halves, *band_list, jnp.asarray(order, BF16), *tables)
    return pl.pallas_call(
        functools.partial(net_kernel, slabs, channels, shared),
        in_specs=[VMEM] * len(given),
        out_specs=[VMEM] * 2,
        out_shape=[
            jax.ShapeDtypeStruct((slabs * FIELDS * ROWS, XL), BF16),
            jax.ShapeDtypeStruct((24, 256), F32),
        ],
        scratch_shapes=stores
        + slopes
        + [pltpu.VMEM((slabs * FIELDS * ROWS, XL), F32)]
        + [pltpu.VMEM((planes * n, XL), BF16) for n in more],
        compiler_params=limit(size + 12 * MIB),
    )(*given)


def readout_kernel(slabs, chunk, step_ref, slab_ref, cell_ref, velocity_ref, mesh_ref, *rest):
    velocity_out, mass_out, lane_hot, mass_rows = rest
    cell = cell_ref[...]
    code = slab_ref[...] * ROWS + (cell >> 8)
    lanes = (cell & (XL - 1)).astype(F32)
    eight = row_iota((8, chunk), 0)
    tiles = chunk // 128
    height = FIELDS * ROWS
    for turn in range(cell.shape[0] // tiles):
        here = lane_hot.at[turn % 2]
        fill_lane_hot(here, spread_rows(lanes, 16, turn * tiles, tiles).astype(BF16), chunk)
        code_tile = spread_rows(code, 8, turn * tiles, tiles)
        sums = [jnp.zeros((8, chunk), F32) for _ in range(FIELDS)]
        for k in range(slabs):
            rows = dot(mesh_ref[k * height : (k + 1) * height, :], here[...])
            for group in range(ROWS // 8):
                same = code_tile == eight + (k * ROWS + group * 8)
                for c in range(FIELDS):
                    first = c * ROWS + group * 8
                    sums[c] = sums[c] + jnp.where(same, rows[first : first + 8, :], 0.0)
        span = slice(turn * chunk, (turn + 1) * chunk)
        for c in range(3):
            force = jnp.sum(sums[c], axis=0, keepdims=True)
            velocity_out[c : c + 1, span] = velocity_ref[c : c + 1, span] + step_ref[0] * force
        pull = jnp.sum(sums[3], axis=0, keepdims=True)
        for t in range(tiles):
            mass_rows[turn * tiles + t : turn * tiles + t + 1, :] = pull[:, t * 128 : (t + 1) * 128]
    mass_out[...] = mass_rows[...].astype(BF16)


def read_out(step_size, target, cells, velocity, mesh, slabs):
    count = velocity.shape[1]
    chunk = math.gcd(count, 1024)
    return pl.pallas_call(
        functools.partial(readout_kernel, slabs, chunk),
        in_specs=[SMEM] + [VMEM] * 4,
        out_specs=[VMEM] * 2,
        out_shape=[
            jax.ShapeDtypeStruct((3, count), F32),
            jax.ShapeDtypeStruct((count // 128, 128), BF16),
        ],
        scratch_shapes=[
            pltpu.VMEM((2, XL, chunk), BF16),
            pltpu.VMEM((count // 128, 128), F32),
        ],
        compiler_params=limit(24 * MIB),
        cost_estimate=pl.CostEstimate(
            flops=slabs * 2 * FIELDS * ROWS * XL * count, bytes_accessed=1_000_000, transcendentals=0
        ),
    )(step_size, target, cells, velocity, mesh)


def total_kernel(scale, *refs):
    grads, outs = refs[:-3], refs[-3:]
    total = grads[0][...]
    for other in grads[1:]:
        total = total + other[...]
    total = total * scale
    for first, out in zip((0, 8, 16), outs):
        out[...] = total[first : first + out.shape[0], 0 : out.shape[1]]


def add_up(grads, weights, scale):
    return pl.pallas_call(
        functools.partial(total_kernel, scale),
        in_specs=[VMEM] * len(grads),
        out_specs=[VMEM] * 3,
        out_shape=[jax.ShapeDtypeStruct(w.shape, F32) for w in weights],
        compiler_params=limit(4 * MIB),
    )(*grads)


def shifted(value, axis, distance):
    count = lax.axis_size(axis)
    return lax.ppermute(value, axis, [(i, (i + distance) % count) for i in range(count)])


def from_all(value, axis):
    count = lax.axis_size(axis)
    others = []
    for k in range(1, count):
        if count & (count - 1):
            others.append(shifted(value, axis, -k))
        else:
            others.append(lax.ppermute(value, axis, [(i, i ^ k) for i in range(count)]))
    return [value] + others


def local(masses, velocity, dest_slab, dest_cell, w_first, w_middle, w_last, step_size, cotangent):
    slabs = lax.axis_size("slab")
    column = ("pencil", "sub")
    count = masses.shape[0]
    dense = (count // 128, 128)
    target, cells = dest_slab.reshape(dense), dest_cell.reshape(dense)
    message = pack(step_size, masses.reshape(dense), target, cells, cotangent, slabs)
    messages = from_all(message, "slab")
    painted = None
    for number, message in enumerate(messages):
        painted = paint(painted, message, dense[0], slabs, number == slabs - 1)
        painted = painted[0] if number < slabs - 1 else painted
    low, high = painted
    low, w_first, w_middle, w_last = lax.optimization_barrier((low, w_first, w_middle, w_last))
    before, after = shifted(high, column, 1), shifted(low, column, -1)
    band_list = bands(w_first, w_middle, w_last)
    mesh, grads = network((low, high, after, before), band_list, w_middle.shape[0], slabs)
    all_grads = from_all(grads, column)
    velocity_new, grad_mass = read_out(step_size, target, cells, velocity, mesh, slabs)
    cell_total = ZL * YL * XL * slabs * lax.axis_size("pencil") * lax.axis_size("sub")
    weight_grads = add_up(all_grads, (w_first, w_middle, w_last), 1.0 / math.sqrt(cell_total))
    return (velocity_new, grad_mass.reshape(count), *weight_grads)


def solution(mesh):
    everywhere = ("runs", "slab", "pencil", "sub")
    placed = (
        P(everywhere),
        P(None, everywhere),
        P(everywhere, None),
        P(everywhere),
        P(),
        P(),
        P(),
        P(),
        P(None, everywhere),
    )
    return jax.shard_map(
        local,
        mesh=mesh,
        in_specs=placed,
        out_specs=(
            P(None, everywhere),
            P(everywhere),
            P("runs", None),
            P("runs", None),
            P("runs", None),
        ),
        check_vma=False,
    )
```

time: 56.3 us -> 42.6 us (0.76)
  starting transfers between devices: 21.1 us -> 8.1 us
  Pallas kernels: 12.7 us -> 25.6 us
  waiting for transfers between devices: 17.5 us -> 6.21 us
  local copies, waits for them, and re-layouts: 3.19 us -> 1.09 us
    ppermute x16 -> x2, starting transfers between devices: 21.1 us -> 0.56 us  [shifted(): lax.ppermute(value, axis, [(i, (i + distance) % count) for i in range(cou...]
    ppermute x16 -> x2, waiting for transfers between devices: 17.5 us -> 3.44 us  [shifted(): lax.ppermute(value, axis, [(i, (i + distance) % count) for i in range(cou...]
    pallas_call x4 -> x9, Pallas kernels: 12.7 us -> 25.6 us  [the longest x4 9.46 us: paint(): pl.pallas_call(functools.partial(paint_kernel, slabs, chunk, tiles, befor...]
    ppermute x0 -> x6, starting transfers between devices: none -> 7.54 us  [from_all(): others.append(lax.ppermute(value, axis, [(i, i ^ k) for i in range(count)]))]
    ppermute x0 -> x6, waiting for transfers between devices: none -> 2.77 us  [from_all(): others.append(lax.ppermute(value, axis, [(i, i ^ k) for i in range(count)]))]
    unnamed x26 -> x28, local copies, waits for them, and re-layouts: 3.17 us -> 1.09 us
  transfers between devices with their start and end apart: 16 -> 8, of which waited for: 9 -> 3; matrix products, arithmetic and copies ran while one was open for 0% -> 0% of each run, Pallas kernels for 3% -> 29%
where the time goes in v3:
time: 42.6 us; the launch traced here: 42.4 us
  Pallas kernels  25.6 us (60%)
  starting transfers between devices  8.1 us (19%)
  waiting for transfers between devices  6.21 us (15%)
  between operations  1.46 us (3%)
  local copies, waits for them, and re-layouts  1.09 us (3%)
    pallas_call x4, Pallas kernels, paint(): pl.pallas_call(functools.partial(paint_kernel, slabs, chunk, tiles, befor...  9.46 us
    pallas_call x1, Pallas kernels, network(): pl.pallas_call(functools.partial(net_kernel, slabs, channels, shared), in...  8.78 us
    ppermute x6, starting transfers between devices, from_all(): others.append(lax.ppermute(value, axis, [(i, i ^ k) for i in range(count)]))  7.54 us
    ppermute x2, waiting for transfers between devices, shifted(): lax.ppermute(value, axis, [(i, (i + distance) % count) for i in range(cou...  3.44 us
    pallas_call x1, Pallas kernels, read_out(): pl.pallas_call(functools.partial(readout_kernel, slabs, chunk), in_specs=...  3.28 us
    ppermute x6, waiting for transfers between devices, from_all(): others.append(lax.ppermute(value, axis, [(i, i ^ k) for i in range(count)]))  2.77 us
    pallas_call x1, Pallas kernels, bands(): pl.pallas_call(band_kernel, in_specs=[VMEM] * 6, out_specs=[VMEM] * 6, ou...  1.77 us
    pallas_call x1, Pallas kernels, pack(): pl.pallas_call(pack_kernel, in_specs=[SMEM] + [VMEM] * 4, out_specs=VMEM,...  1.69 us
  transfers between devices with their start and end apart: 8, of which 3 were waited for; matrix products, arithmetic and copies ran while one was open for 0% of the time, Pallas kernels for 29%

profile of v3, /device:TPU:0, one launch (start us, length us, event | category | flops | bytes accessed | tf_op | source)
XLA Modules:
  0.0 42.4 jit_solution(17813558047780334007)
XLA Ops:
  1.3 1.7 %shard_map.191.refs_0_ = bf16[384,128]{1,0:T(8,128)(2,1)} custom-call(f32[1]{0:T(128)S(6)} %copy.21.step_ref, bf16[64,128]{1,0:T(8,128)(2,1)} %bitcast.8, s32[64,128]{1,0:T(8,128)} %bitcast.4, s32[64,128]{1,0:T(8,128)} %bitcast.6, f32[3,8192]{1,0:T(4,128)} %cot_ref.1), custom_call_target="tpu_custom_call" | custom-call | tf_op jit(solution)/shard_map/pallas_call | solution.py:62
  3.0 5.0 %collective-permute-start.2 = (bf16[384,128]{1,0:T(8,128)(2,1)}, bf16[384,128]{1,0:T(8,128)(2,1)S(1)}, u32[]{:S(2)}, u32[]{:S(2)}) collective-permute-start(bf16[384,128]{1,0:T(8,128)(2,1)} %shard_map.191.refs_0_), channel_id=1, source_target_pairs={{0,12},{4,8},{8,4},{12,0},{1,13},{5,9},{9,5},{13,1},{2,14},{6,10},... | collective-permute-start | bytes 294920 | tf_op jit(solution)/shard_map/ppermute | solution.py:535
  8.0 0.6 %collective-permute-start = (bf16[384,128]{1,0:T(8,128)(2,1)}, bf16[384,128]{1,0:T(8,128)(2,1)S(1)}, u32[]{:S(2)}, u32[]{:S(2)}) collective-permute-start(bf16[384,128]{1,0:T(8,128)(2,1)} %shard_map.191.refs_0_), channel_id=1, source_target_pairs={{0,4},{4,0},{8,12},{12,8},{1,5},{5,1},{9,13},{13,9},{2,6},{6,2},{1... | collective-permute-start | bytes 294920 | tf_op jit(solution)/shard_map/ppermute | solution.py:535
  8.6 0.9 %copy-done = bf16[384,128]{1,0:T(8,128)(2,1)S(1)} copy-done((bf16[384,128]{1,0:T(8,128)(2,1)S(1)}, bf16[384,128]{1,0:T(8,128)(2,1)}, u32[]{:S(2)}) %copy-start) | copy-done | bytes 98328
  9.5 2.4 %shard_map.192.refs_0_ = f32[512,256]{1,0:T(8,128)S(1)} custom-call(bf16[384,128]{1,0:T(8,128)(2,1)S(1)} %copy-done), custom_call_target="tpu_custom_call" | custom-call | flops 2147483648 | bytes 1048576 | tf_op jit(solution)/shard_map/pallas_call | solution.py:137
  11.9 2.8 %collective-permute-done.refs_1_ = bf16[384,128]{1,0:T(8,128)(2,1)S(1)} collective-permute-done((bf16[384,128]{1,0:T(8,128)(2,1)}, bf16[384,128]{1,0:T(8,128)(2,1)S(1)}, u32[]{:S(2)}, u32[]{:S(2)}) %collective-permute-start) | collective-permute-done | bytes 98336 | tf_op jit(solution)/shard_map/ppermute | solution.py:535
  14.6 2.4 %shard_map.193.refs_0_ = f32[512,256]{1,0:T(8,128)S(1)} custom-call(f32[512,256]{1,0:T(8,128)S(1)} %shard_map.192.refs_0_, bf16[384,128]{1,0:T(8,128)(2,1)S(1)} %collective-permute-done.refs_1_), custom_call_target="tpu_custom_call" | custom-call | flops 2147483648 | bytes 1048576 | tf_op jit(solution)/shard_map/pallas_call | solution.py:137
  17.0 2.4 %shard_map.194.refs_0_ = f32[512,256]{1,0:T(8,128)S(1)} custom-call(f32[512,256]{1,0:T(8,128)S(1)} %shard_map.193.refs_0_, bf16[384,128]{1,0:T(8,128)(2,1)S(1)} %collective-permute-done.1.refs_1_), custom_call_target="tpu_custom_call" | custom-call | flops 2147483648 | bytes 1048576 | tf_op jit(solution)/shard_map/pallas_call | solution.py:137
  19.4 0.0 copy-start.11
  19.4 0.0 copy-start.13
  19.5 2.4 %shard_map.195 = (bf16[256,256]{1,0:T(8,128)(2,1)S(1)}, bf16[256,256]{1,0:T(8,128)(2,1)S(1)}) custom-call(f32[512,256]{1,0:T(8,128)S(1)} %shard_map.194.refs_0_, bf16[384,128]{1,0:T(8,128)(2,1)S(1)} %collective-permute-done.2.refs_1_), custom_call_target="tpu_custom_call" | custom-call | flops 2147483648 | bytes 1048576 | tf_op jit(solution)/shard_map/pallas_call | solution.py:137
  21.9 0.2 collective-permute-start.3
  22.0 0.4 collective-permute-start.4
  22.4 0.1 copy-done.9
  22.5 1.8 %shard_map.196 = (bf16[112,144]{1,0:T(8,128)(2,1)S(1)}, bf16[96,1008]{1,0:T(8,128)(2,1)S(1)}, bf16[96,240]{1,0:T(8,128)(2,1)S(1)}, bf16[48,240]{1,0:T(8,128)(2,1...) custom-call(bf16[8,27]{1,0:T(8,128)(2,1)S(1)} %copy-done.9, bf16[8,216]{1,0:T(8,128)(2,1)S(1)} %copy-done.8, ...), custom_call_target="tpu_custom_call" | custom-call | flops 800000000 | bytes 4000000 | tf_op jit(solution)/shard_map/pallas_call | solution.py:242
  24.3 0.0 copy-start.5
  24.3 0.5 %collective-permute-done.3.after_ref = bf16[256,256]{1,0:T(8,128)(2,1)S(1)} collective-permute-done((bf16[256,256]{1,0:T(8,128)(2,1)S(1)}, bf16[256,256]{1,0:T(8,128)(2,1)S(1)}, u32[]{:S(2)}, u32[]{:S(2)}) %collective-permute-start.3) | collective-permute-done | bytes 131104 | tf_op jit(solution)/shard_map/ppermute | solution.py:525
  24.8 2.9 %collective-permute-done.4.before_ref = bf16[256,256]{1,0:T(8,128)(2,1)S(1)} collective-permute-done((bf16[256,256]{1,0:T(8,128)(2,1)S(1)}, bf16[256,256]{1,0:T(8,128)(2,1)S(1)}, u32[]{:S(2)}, u32[]{:S(2)}) %collective-permute-start.4) | collective-permute-done | bytes 131104 | tf_op jit(solution)/shard_map/ppermute | solution.py:525
  27.8 8.8 %shard_map.197 = (bf16[512,256]{1,0:T(8,128)(2,1)S(1)}, f32[24,256]{1,0:T(8,128)S(1)}) custom-call(bf16[256,256]{1,0:T(8,128)(2,1)S(1)} %get-tuple-element.25.low_ref, bf16[256,256]{1,0:T(8,128)(2,1)S(1)} %get-tuple-element.26.high_ref, bf16[256,256]{1,0:T(8,128)(2,1)S(1)} %collective-permute-done.3.after_ref, ...), custom_call_target="tpu_custom_call" | custom-call | tf_op jit(solution)/shard_map/pallas_call | solution.py:435
  36.6 0.1 collective-permute-start.7
  36.7 1.5 %collective-permute-start.6 = (f32[24,256]{1,0:T(8,128)S(1)}, f32[24,256]{1,0:T(8,128)S(1)}, u32[]{:S(2)}, u32[]{:S(2)}) collective-permute-start(f32[24,256]{1,0:T(8,128)S(1)} %get-tuple-element.39.refs_0_), channel_id=1, source_target_pairs={{0,2},{1,3},{2,0},{3,1},{4,6},{5,7},{6,4},{7,5},{8,10},{9,11},{10,... | collective-permute-start | bytes 73736 | tf_op jit(solution)/shard_map/ppermute | solution.py:535
  38.2 0.3 collective-permute-start.5
  38.5 3.3 %shard_map.198 = (f32[3,8192]{1,0:T(4,128)}, bf16[64,128]{1,0:T(8,128)(2,1)}) custom-call(f32[1]{0:T(128)S(6)} %copy.21.step_ref, s32[64,128]{1,0:T(8,128)S(1)} %bitcast.5, s32[64,128]{1,0:T(8,128)S(1)} %bitcast.7, f32[3,8192]{1,0:T(4,128)S(1)} %copy-done.7, bf16[512,256]{1,0:T(8,128)(2,1)S(1)} %get-tuple-element.36.mesh_ref), custom_call_target="tpu_custom_call" | custom-call | flops 2147483648 | bytes 1000000 | tf_op jit(solution)/shard_map/pallas_call | solution.py:484
  41.8 0.6 %shard_map.199 = (f32[8,27]{1,0:T(8,128)}, f32[8,216]{1,0:T(8,128)}, f32[3,216]{1,0:T(4,128)}) custom-call(f32[24,256]{1,0:T(8,128)S(1)} %get-tuple-element.39.refs_0_, f32[24,256]{1,0:T(8,128)S(1)} %collective-permute-done.5.refs_1_, f32[24,256]{1,0:T(8,128)S(1)} %collective-permute-done.6.refs_2_, f32[24,256]{1,0:T(8,128)S(1)} %collective-permute-done.7.refs_3_), custom_call_target="tpu_custom_call" | custom-call | tf_op jit(solution)/shard_map/pallas_call | solution.py:514
  (29 shorter events, 0.1 us)
Async XLA Ops:
  3.0 16.5 %collective-permute-start.2 = (bf16[384,128]{1,0:T(8,128)(2,1)}, bf16[384,128]{1,0:T(8,128)(2,1)S(1)}, u32[]{:S(2)}, u32[]{:S(2)}) collective-permute-start(bf16[384,128]{1,0:T(8,128)(2,1)} %shard_map.191.refs_0_), channel_id=1, source_target_pairs={{0,12},{4,8},{8,4},{12,0},{1,13},{5,9},{9,5},{13,1},{2,14},{6,10},... | collective-permute-start | bytes 294920 | tf_op jit(solution)/shard_map/ppermute | solution.py:535
  8.0 9.0 %collective-permute-start.1 = (bf16[384,128]{1,0:T(8,128)(2,1)}, bf16[384,128]{1,0:T(8,128)(2,1)S(1)}, u32[]{:S(2)}, u32[]{:S(2)}) collective-permute-start(bf16[384,128]{1,0:T(8,128)(2,1)} %shard_map.191.refs_0_), channel_id=1, source_target_pairs={{0,8},{4,12},{8,0},{12,4},{1,9},{5,13},{9,1},{13,5},{2,10},{6,14},... | collective-permute-start | bytes 294920 | tf_op jit(solution)/shard_map/ppermute | solution.py:535
  8.0 6.6 %collective-permute-start = (bf16[384,128]{1,0:T(8,128)(2,1)}, bf16[384,128]{1,0:T(8,128)(2,1)S(1)}, u32[]{:S(2)}, u32[]{:S(2)}) collective-permute-start(bf16[384,128]{1,0:T(8,128)(2,1)} %shard_map.191.refs_0_), channel_id=1, source_target_pairs={{0,4},{4,0},{8,12},{12,8},{1,5},{5,1},{9,13},{13,9},{2,6},{6,2},{1... | collective-permute-start | bytes 294920 | tf_op jit(solution)/shard_map/ppermute | solution.py:535
  8.6 0.9 %copy-start = (bf16[384,128]{1,0:T(8,128)(2,1)S(1)}, bf16[384,128]{1,0:T(8,128)(2,1)}, u32[]{:S(2)}) copy-start(bf16[384,128]{1,0:T(8,128)(2,1)} %shard_map.191.refs_0_) | copy-start | bytes 294916
  19.4 3.0 %copy-start.8 = (bf16[8,216]{1,0:T(8,128)(2,1)S(1)}, bf16[8,216]{1,0:T(8,128)(2,1)}, u32[]{:S(2)}) copy-start(bf16[8,216]{1,0:T(8,128)(2,1)} %middle_ref) | copy-start | bytes 10372
  19.4 3.0 %copy-start.11 = (s32[8,1008]{1,0:T(8,128)S(1)}, s32[8,1008]{1,0:T(8,128)}, u32[]{:S(2)}) copy-start(s32[8,1008]{1,0:T(8,128)} %constant.15.clone.c2_ref) | copy-start | bytes 96772
  19.4 3.0 %copy-start.12 = (s32[8,864]{1,0:T(8,128)S(1)}, s32[8,864]{1,0:T(8,128)}, u32[]{:S(2)}) copy-start(s32[8,864]{1,0:T(8,128)} %constant.16.clone.c3_ref) | copy-start | bytes 82948
  19.4 3.0 %copy-start.13 = (s32[8,144]{1,0:T(8,128)S(1)}, s32[8,144]{1,0:T(8,128)}, u32[]{:S(2)}) copy-start(s32[8,144]{1,0:T(8,128)} %constant.14.clone.c1_ref) | copy-start | bytes 13828
  19.5 3.0 %copy-start.10 = (bf16[3,216]{1,0:T(4,128)(2,1)S(1)}, bf16[3,216]{1,0:T(4,128)(2,1)}, u32[]{:S(2)}) copy-start(bf16[3,216]{1,0:T(4,128)(2,1)} %last_ref) | copy-start | bytes 3892
  21.8 0.7 %copy-start.9 = (bf16[8,27]{1,0:T(8,128)(2,1)S(1)}, bf16[8,27]{1,0:T(8,128)(2,1)}, u32[]{:S(2)}) copy-start(bf16[8,27]{1,0:T(8,128)(2,1)} %first_ref) | copy-start | bytes 1300
  21.9 3.0 %collective-permute-start.3 = (bf16[256,256]{1,0:T(8,128)(2,1)S(1)}, bf16[256,256]{1,0:T(8,128)(2,1)S(1)}, u32[]{:S(2)}, u32[]{:S(2)}) collective-permute-start(bf16[256,256]{1,0:T(8,128)(2,1)S(1)} %get-tuple-element.25.low_ref), channel_id=1, source_target_pairs={{0,3},{1,0},{2,1},{3,2},{4,7},{5,4},{6,5},{7,6},{8,11},{9,8},{10,9... | collective-permute-start | bytes 393224 | tf_op jit(solution)/shard_map/ppermute | solution.py:525
  22.0 5.7 %collective-permute-start.4 = (bf16[256,256]{1,0:T(8,128)(2,1)S(1)}, bf16[256,256]{1,0:T(8,128)(2,1)S(1)}, u32[]{:S(2)}, u32[]{:S(2)}) collective-permute-start(bf16[256,256]{1,0:T(8,128)(2,1)S(1)} %get-tuple-element.26.high_ref), channel_id=1, source_target_pairs={{0,1},{1,2},{2,3},{3,0},{4,5},{5,6},{6,7},{7,4},{8,9},{9,10},{10,1... | collective-permute-start | bytes 393224 | tf_op jit(solution)/shard_map/ppermute | solution.py:525
  22.5 5.2 %copy-start.3 = (bf16[64,64]{1,0:T(8,128)(2,1)S(1)}, bf16[64,64]{1,0:T(8,128)(2,1)}, u32[]{:S(2)}) copy-start(bf16[64,64]{1,0:T(8,128)(2,1)} %constant.20.clone.order_ref) | copy-start | bytes 24580
  22.5 5.2 %copy-start.4 = (s32[8,336]{1,0:T(8,128)S(1)}, s32[8,336]{1,0:T(8,128)}, u32[]{:S(2)}) copy-start(s32[8,336]{1,0:T(8,128)} %constant.18.clone.c2_ref) | copy-start | bytes 32260
  22.5 5.2 %copy-start.6 = (s32[8,48]{1,0:T(8,128)S(1)}, s32[8,48]{1,0:T(8,128)}, u32[]{:S(2)}) copy-start(s32[8,48]{1,0:T(8,128)} %constant.17.clone.c1_ref) | copy-start | bytes 4612
  24.3 3.5 %copy-start.5 = (s32[8,240]{1,0:T(8,128)S(1)}, s32[8,240]{1,0:T(8,128)}, u32[]{:S(2)}) copy-start(s32[8,240]{1,0:T(8,128)} %constant.19.clone.c3_ref) | copy-start | bytes 23044
  27.8 10.8 %copy-start.1 = (s32[8192,1]{0,1:T(1,128)S(1)}, s32[8192,1]{0,1:T(1,128)}, u32[]{:S(2)}) copy-start(s32[8192,1]{0,1:T(1,128)} %param.18) | copy-start | bytes 98308
  27.8 10.7 %copy-start.2 = (s32[8192]{0:T(1024)S(1)}, s32[8192]{0:T(1024)}, u32[]{:S(2)}) copy-start(s32[8192]{0:T(1024)} %param.19) | copy-start | bytes 98308
  27.8 10.7 %copy-start.7 = (f32[3,8192]{1,0:T(4,128)S(1)}, f32[3,8192]{1,0:T(4,128)}, u32[]{:S(2)}) copy-start(f32[3,8192]{1,0:T(4,128)} %velocity_ref.1) | copy-start | bytes 294916
  36.6 5.2 %collective-permute-start.7 = (f32[24,256]{1,0:T(8,128)S(1)}, f32[24,256]{1,0:T(8,128)S(1)}, u32[]{:S(2)}, u32[]{:S(2)}) collective-permute-start(f32[24,256]{1,0:T(8,128)S(1)} %get-tuple-element.39.refs_0_), channel_id=1, source_target_pairs={{0,3},{1,2},{2,1},{3,0},{4,7},{5,6},{6,5},{7,4},{8,11},{9,10},{10,... | collective-permute-start | bytes 73736 | tf_op jit(solution)/shard_map/ppermute | solution.py:535
  36.7 5.1 %collective-permute-start.6 = (f32[24,256]{1,0:T(8,128)S(1)}, f32[24,256]{1,0:T(8,128)S(1)}, u32[]{:S(2)}, u32[]{:S(2)}) collective-permute-start(f32[24,256]{1,0:T(8,128)S(1)} %get-tuple-element.39.refs_0_), channel_id=1, source_target_pairs={{0,2},{1,3},{2,0},{3,1},{4,6},{5,7},{6,4},{7,5},{8,10},{9,11},{10,... | collective-permute-start | bytes 73736 | tf_op jit(solution)/shard_map/ppermute | solution.py:535
  38.2 3.6 %collective-permute-start.5 = (f32[24,256]{1,0:T(8,128)S(1)}, f32[24,256]{1,0:T(8,128)S(1)}, u32[]{:S(2)}, u32[]{:S(2)}) collective-permute-start(f32[24,256]{1,0:T(8,128)S(1)} %get-tuple-element.39.refs_0_), channel_id=1, source_target_pairs={{0,1},{1,0},{2,3},{3,2},{4,5},{5,4},{6,7},{7,6},{8,9},{9,8},{10,11... | collective-permute-start | bytes 73736 | tf_op jit(solution)/shard_map/ppermute | solution.py:535

commit v4 on v3

--- a/solution.py
+++ b/solution.py
@@ -40,7 +40,8 @@
     return pltpu.CompilerParams(vmem_limit_bytes=size)
 
 
-def pack_kernel(step_ref, mass_ref, slab_ref, cell_ref, cot_ref, out_ref, rows):
+def pack_kernel(step_ref, mass_ref, slab_ref, cell_ref, cot_ref, *rest):
+    outs, rows = rest[:-1], rest[-1]
     tiles = mass_ref.shape[0]
     cell, slab = cell_ref[...], slab_ref[...]
     z, y = cell >> 11, (cell >> 8) & 7
@@ -49,21 +50,29 @@
         for t in range(tiles):
             row = component * tiles + t
             rows[row : row + 1, :] = cot_ref[component : component + 1, t * 128 : (t + 1) * 128]
-    out_ref[0:tiles, :] = mass_ref[...]
-    out_ref[tiles : 4 * tiles, :] = (step_ref[0] * rows[...]).astype(BF16)
-    out_ref[4 * tiles : 5 * tiles, :] = code.astype(F32).astype(BF16)
-    out_ref[5 * tiles : 6 * tiles, :] = (cell & (XL - 1)).astype(F32).astype(BF16)
-    if out_ref.shape[0] > 6 * tiles:
-        out_ref[6 * tiles : 7 * tiles, :] = (slab >> 3).astype(F32).astype(BF16)
+    parts = [
+        mass_ref[...],
+        (step_ref[0] * rows[...]).astype(BF16),
+        code.astype(F32).astype(BF16),
+        (cell & (XL - 1)).astype(F32).astype(BF16),
+        (slab >> 3).astype(F32).astype(BF16),
+    ]
+    for out_ref in outs:
+        first = 0
+        for part in parts:
+            if first < out_ref.shape[0]:
+                out_ref[first : first + part.shape[0], :] = part
+            first += part.shape[0]
 
 
 def pack(step_size, masses, target, cells, cotangent, slabs):
     tiles = masses.shape[0]
+    shape = jax.ShapeDtypeStruct(((6 if slabs <= 8 else 7) * tiles, 128), BF16)
     return pl.pallas_call(
         pack_kernel,
         in_specs=[SMEM] + [VMEM] * 4,
-        out_specs=VMEM,
-        out_shape=jax.ShapeDtypeStruct(((6 if slabs <= 8 else 7) * tiles, 128), BF16),
+        out_specs=[VMEM] * slabs,
+        out_shape=[shape] * slabs,
         scratch_shapes=[pltpu.VMEM((3 * tiles, 128), F32)],
         compiler_params=limit(60 * MIB),
     )(step_size, masses, target, cells, cotangent)
@@ -84,14 +93,15 @@
         store[16 * group : 16 * group + 16, :] = jnp.where(same, one, zero)
 
 
-def paint_kernel(slabs, chunk, tiles, started, final, *refs):
+def paint_kernel(slabs, chunk, tiles, started, final, count, *refs):
     before, refs = (refs[0], refs[1:]) if started else (None, refs)
-    message, refs = refs[0], refs[1:]
+    messages, refs = refs[:count], refs[count:]
     outs, (hot, lane_hot, total) = refs[:-3], refs[-3:]
     step = chunk // 128
     sixteen = row_iota((16, chunk), 0)
     zero = jnp.zeros((16, chunk), BF16)
-    for turn in range(tiles // step):
+    for number in range(count * (tiles // step)):
+        message, turn = messages[number // (tiles // step)], number % (tiles // step)
         here, here_lane = hot.at[turn % 2], lane_hot.at[turn % 2]
 
         def spread(field):
@@ -112,7 +122,7 @@
                         first = ((half * FIELDS + field) * slabs + slab) * 16
                         here[first : first + 16, :] = jnp.where(same, values[field], zero)
         part = dot_nt(here[...], here_lane[...])
-        if turn > 0:
+        if number > 0:
             total[...] += part
         elif started:
             total[...] = before[...] + part
@@ -126,16 +136,18 @@
         outs[0][...] = total[...]
 
 
-def paint(before, message, tiles, slabs, final):
+def paint(before, messages, tiles, slabs, final):
     chunk = 128 * math.gcd(tiles, 16)
     height = 2 * FIELDS * slabs * 16
     scratch = 2 * chunk * (height + XL) * 2 + height * XL * 4
     shapes = [jax.ShapeDtypeStruct((height, XL), F32)]
     if final:
         shapes = [jax.ShapeDtypeStruct((height // 2, XL), BF16)] * 2
-    given = [message] if before is None else [before, message]
+    given = messages if before is None else [before] + messages
     return pl.pallas_call(
-        functools.partial(paint_kernel, slabs, chunk, tiles, before is not None, final),
+        functools.partial(
+            paint_kernel, slabs, chunk, tiles, before is not None, final, len(messages)
+        ),
         in_specs=[VMEM] * len(given),
         out_specs=[VMEM] * len(shapes),
         out_shape=shapes,
@@ -144,9 +156,9 @@
             pltpu.VMEM((2, XL, chunk), BF16),
             pltpu.VMEM((height, XL), F32),
         ],
-        compiler_params=limit(scratch + height * XL * 12 + 8 * MIB),
+        compiler_params=limit(scratch + height * XL * 24 + 12 * MIB),
         cost_estimate=pl.CostEstimate(
-            flops=2 * height * XL * tiles * 128, bytes_accessed=MIB, transcendentals=0
+            flops=2 * height * XL * tiles * 128 * len(messages), bytes_accessed=MIB, transcendentals=0
         ),
     )(*given)
 
@@ -322,35 +334,29 @@
         return self.ref[row : row + count, :]
 
 
-def products(delta, count, source, depth):
-    total = None
-    for plane in range(0, depth, 4):
-        left, right = [
-            jnp.concatenate([rows(plane + k) for k in range(4)], axis=1)
-            for rows in (
-                lambda p: jnp.concatenate([delta.shifted(p, e, count) for e in (2, 1, 0)], axis=0),
-                lambda p: jnp.concatenate(
-                    [source.shifted(p + a, 1, source.rows) for a in (-1, 0, 1)], axis=0
-                ),
-            )
-        ]
-        if source.rows < count:
-            term = dot_nt(left, right)
-        else:
-            term = dot_nt(right, left)
-        total = term if total is None else total + term
-    return total if source.rows < count else total.T
-
-
-def stacked(weight, store, depth):
-    rows = weight.shape[0] // 3
-    parts = [dot(weight, store.plane(plane)) for plane in range(depth)]
-    return [
-        parts[(plane - 1) % depth][0:rows]
-        + parts[plane][rows : 2 * rows]
-        + parts[(plane + 1) % depth][2 * rows :]
-        for plane in range(depth)
+def product(delta, count, source, plane):
+    planes = range(plane, plane + 4)
+    left = [
+        jnp.concatenate([delta.shifted(p, e, count) for e in (2, 1, 0)], axis=0) for p in planes
     ]
+    right = [
+        jnp.concatenate([source.shifted(p + a, 1, source.rows) for a in (-1, 0, 1)], axis=0)
+        for p in planes
+    ]
+    return dot_nt(jnp.concatenate(left, axis=1), jnp.concatenate(right, axis=1))
+
+
+class Plan:
+    def __init__(self):
+        self.stages = {}
+
+    def add(self, stage, key, after, step):
+        self.stages.setdefault(stage, []).append((key, after, step))
+
+    def in_turn(self):
+        for steps in self.stages.values():
+            for _, _, step in steps:
+                step()
 
 
 def net_kernel(
@@ -366,7 +372,18 @@
     d2 = Store(b_ref if shared else more[0], depth, 12 * channels)
     d1 = Store(a_ref if shared else more[1], depth, 10 * channels)
     order = order_ref[...]
-    for slab in range(slabs):
+    grads_ref[...] = jnp.zeros_like(grads_ref)
+    inner = 10 * channels
+    plan, kept, sums = Plan(), {}, {}
+
+    def near(stage, plane):
+        return [(stage, (plane + a) % depth) for a in (-1, 0, 1)]
+
+    def place(plane, field):
+        first = (plane // ZL * FIELDS + field) * ROWS + plane % ZL * YL
+        return slice(first, first + YL)
+
+    def load(slab):
         for c in range(FIELDS):
             first = (c * slabs + slab) * 16
             pieces = [ref[first : first + 16, :] for ref in (low_ref, high_ref, after_ref, before_ref)]
@@ -377,43 +394,90 @@
                     s0.put(slab * ZL + z, value)
                 else:
                     sg.put(slab * ZL + z, value, (c - 1) * POS)
-    grads_ref[...] = jnp.zeros_like(grads_ref)
-    inner, outer = 10 * channels, 12 * channels
-    b1 = b1_ref[...]
-    for plane in range(depth):
-        pre = dot(b1, s0.window(plane))
+
+    def first_layer(plane):
+        pre = dot(b1_ref[...], s0.window(plane))
         sigma = jax.nn.sigmoid(pre)
         s1.put(plane, pre * sigma)
         slope1[plane] = slope(pre[0:inner], sigma[0:inner])
-    b2 = b2_ref[...]
-    for plane in range(depth):
-        pre = dot(b2, s1.window(plane))
+
+    def second_layer(plane):
+        pre = dot(b2_ref[...], s1.window(plane))
         sigma = jax.nn.sigmoid(pre)
         s2.put(plane, pre[0:inner] * sigma[0:inner])
         slope2[plane] = slope(pre, sigma)
 
-    def place(plane, field):
-        first = (plane // ZL * FIELDS + field) * ROWS + plane % ZL * YL
-        return slice(first, first + YL)
-
-    for plane, force in enumerate(stacked(b3_ref[...], s2, depth)):
+    def stacked(stage, weight_ref, store, plane):
+        kept[stage, plane] = dot(weight_ref[...], store.plane(plane))
+
+    def unstacked(stage, plane):
+        rows = kept[stage, plane].shape[0] // 3
+        return functools.reduce(
+            jnp.add,
+            [kept[key][a * rows : (a + 1) * rows] for a, key in enumerate(near(stage, plane))],
+        )
+
+    def force(plane):
+        value = unstacked("force parts", plane)
         for c in range(3):
-            fields[place(plane, c), :] = force[c * YL : (c + 1) * YL, :]
-    full = products(sg, 3 * POS, s2, depth)
-    grads_ref[16:24, 0 : 27 * channels] = weight_sum(full, c3_ref[...], channels, False, 3)
-    t3 = t3_ref[...]
-    for plane in range(depth):
-        d2.put(plane, dot(t3, sg.window(plane)) * slope2[plane])
-    full = products(d2, YL * channels, s1, depth)
-    grads_ref[8:16, 0 : 27 * channels] = weight_sum(full, c2_ref[...], channels, True, channels)
-    t2 = t2_ref[...]
-    for plane in range(depth):
-        d1.put(plane, dot(t2, d2.window(plane)) * slope1[plane])
-    full = products(d1, YL * channels, s0, depth)
-    grads_ref[0:8, 0:27] = weight_sum(full, c1_ref[...], 1, True, channels)
-    for plane, pull in enumerate(stacked(t1_ref[...], d1, depth)):
-        fields[place(plane, 3), :] = pull[0:YL, :]
+            fields[place(plane, c), :] = value[c * YL : (c + 1) * YL, :]
+
+    def pull(plane):
+        fields[place(plane, 3), :] = unstacked("pull parts", plane)[0:YL, :]
+
+    def second_delta(plane):
+        d2.put(plane, dot(t3_ref[...], sg.window(plane)) * slope2[plane])
+
+    def first_delta(plane):
+        d1.put(plane, dot(t2_ref[...], d2.window(plane)) * slope1[plane])
+
+    def add_product(name, delta, count, source, plane):
+        term = product(delta, count, source, plane)
+        sums[name] = sums[name] + term if name in sums else term
+
+    def bind(step, *given):
+        return functools.partial(step, *given)
+
+    for slab in range(slabs):
+        plan.add("load", slab, [], bind(load, slab))
+    for p in range(depth):
+        slabs_near = [("load", q // ZL) for _, q in near("", p)]
+        plan.add("first", p, slabs_near, bind(first_layer, p))
+    for p in range(depth):
+        plan.add("second", p, near("first", p), bind(second_layer, p))
+    for p in range(depth):
+        plan.add("force parts", p, [("second", p)], bind(stacked, "force parts", b3_ref, s2, p))
+    for p in range(depth):
+        plan.add("force", p, near("force parts", p), bind(force, p))
+    groups = range(0, depth, 4)
+    for p in groups:
+        after = [("second", q % depth) for q in range(p - 1, p + 5)]
+        plan.add("last sum", p, after, bind(add_product, "last", sg, 3 * POS, s2, p))
+    for p in range(depth):
+        plan.add("second delta", p, [("second", p)], bind(second_delta, p))
+    for p in groups:
+        after = [("second delta", q) for q in range(p, p + 4)]
+        plan.add("middle sum", p, after, bind(add_product, "middle", d2, YL * channels, s1, p))
+    for p in range(depth):
+        plan.add("first delta", p, near("second delta", p), bind(first_delta, p))
+    for p in groups:
+        after = [("first delta", q) for q in range(p, p + 4)]
+        plan.add("first sum", p, after, bind(add_product, "first", d1, YL * channels, s0, p))
+    for p in range(depth):
+        plan.add("pull parts", p, [("first delta", p)], bind(stacked, "pull parts", t1_ref, d1, p))
+    for p in range(depth):
+        plan.add("pull", p, near("pull parts", p), bind(pull, p))
+    plan.in_turn()
     mesh_ref[...] = fields[...].astype(BF16)
+    for first, name, table_ref, ins, mixed in (
+        (0, "first", c1_ref, 1, True),
+        (8, "middle", c2_ref, channels, True),
+        (16, "last", c3_ref, channels, False),
+    ):
+        outs = channels if mixed else 3
+        grads_ref[first : first + 8, 0 : 27 * ins] = weight_sum(
+            sums[name], table_ref[...], ins, mixed, outs
+        )
 
 
 def network(halves, band_list, channels, slabs):
@@ -461,8 +525,9 @@
         fill_lane_hot(here, spread_rows(lanes, 16, turn * tiles, tiles).astype(BF16), chunk)
         code_tile = spread_rows(code, 8, turn * tiles, tiles)
         sums = [jnp.zeros((8, chunk), F32) for _ in range(FIELDS)]
+        everything = dot(mesh_ref[...], here[...])
         for k in range(slabs):
-            rows = dot(mesh_ref[k * height : (k + 1) * height, :], here[...])
+            rows = everything[k * height : (k + 1) * height, :]
             for group in range(ROWS // 8):
                 same = code_tile == eight + (k * ROWS + group * 8)
                 for c in range(FIELDS):
@@ -493,7 +558,7 @@
             pltpu.VMEM((2, XL, chunk), BF16),
             pltpu.VMEM((count // 128, 128), F32),
         ],
-        compiler_params=limit(24 * MIB),
+        compiler_params=limit((16 + 4 * slabs) * MIB),
         cost_estimate=pl.CostEstimate(
             flops=slabs * 2 * FIELDS * ROWS * XL * count, bytes_accessed=1_000_000, transcendentals=0
         ),
@@ -527,13 +592,17 @@
 
 def from_all(value, axis):
     count = lax.axis_size(axis)
+    values = value if isinstance(value, (list, tuple)) else [value] * count
     others = []
-    for k in range(1, count):
+    order = list(range(1, count))
+    if count > 3:
+        order = order[1:2] + order[0:1] + order[2:]
+    for n, k in enumerate(order, 1):
         if count & (count - 1):
-            others.append(shifted(value, axis, -k))
+            others.append(shifted(values[n], axis, -k))
         else:
-            others.append(lax.ppermute(value, axis, [(i, i ^ k) for i in range(count)]))
-    return [value] + others
+            others.append(lax.ppermute(values[n], axis, [(i, i ^ k) for i in range(count)]))
+    return [values[0]] + others
 
 
 def local(masses, velocity, dest_slab, dest_cell, w_first, w_middle, w_last, step_size, cotangent):
@@ -542,13 +611,12 @@
     count = masses.shape[0]
     dense = (count // 128, 128)
     target, cells = dest_slab.reshape(dense), dest_cell.reshape(dense)
-    message = pack(step_size, masses.reshape(dense), target, cells, cotangent, slabs)
-    messages = from_all(message, "slab")
+    packed = pack(step_size, masses.reshape(dense), target, cells, cotangent, slabs)
+    messages = from_all(packed, "slab")
     painted = None
-    for number, message in enumerate(messages):
-        painted = paint(painted, message, dense[0], slabs, number == slabs - 1)
-        painted = painted[0] if number < slabs - 1 else painted
-    low, high = painted
+    for message in messages[:-2]:
+        painted = paint(painted, [message], dense[0], slabs, False)[0]
+    low, high = paint(painted, messages[-2:], dense[0], slabs, True)
     low, w_first, w_middle, w_last = lax.optimization_barrier((low, w_first, w_middle, w_last))
     before, after = shifted(high, column, 1), shifted(low, column, -1)
     band_list = bands(w_first, w_middle, w_last)

time: 42.6 us -> 39.4 us (0.925)
  Pallas kernels: 25.6 us -> 23.4 us
  waiting for transfers between devices: 6.21 us -> 4.92 us
    pallas_call x1, Pallas kernels: 8.78 us -> 6.86 us  [network(): pl.pallas_call(functools.partial(net_kernel, slabs, channels, shared), in...]
    ppermute x6, waiting for transfers between devices: 2.77 us -> 1.31 us  [from_all(): lax.ppermute(values[n], axis, [(i, i ^ k) for i in range(count)])]
    pallas_call x4 -> x3, Pallas kernels: 9.46 us -> 9.25 us  [paint(): pl.pallas_call(functools.partial(paint_kernel, slabs, chunk, tiles, befor...]
  transfers between devices with their start and end apart: 8 -> 8, of which waited for: 3 -> 3; matrix products, arithmetic and copies ran while one was open for 0% -> 0% of each run, Pallas kernels for 29% -> 24%
where the time goes in v4:
time: 39.4 us; the launch traced here: 39.2 us
  Pallas kernels  23.4 us (59%)
  starting transfers between devices  8.37 us (21%)
  waiting for transfers between devices  4.92 us (12%)
  between operations  1.46 us (4%)
  local copies, waits for them, and re-layouts  1.05 us (3%)
    pallas_call x3, Pallas kernels, paint(): pl.pallas_call(functools.partial(paint_kernel, slabs, chunk, tiles, befor...  9.25 us
    ppermute x6, starting transfers between devices, from_all(): lax.ppermute(values[n], axis, [(i, i ^ k) for i in range(count)])  7.81 us
    pallas_call x1, Pallas kernels, network(): pl.pallas_call(functools.partial(net_kernel, slabs, channels, shared), in...  6.86 us
    ppermute x2, waiting for transfers between devices, shifted(): lax.ppermute(value, axis, [(i, (i + distance) % count) for i in range(cou...  3.61 us
    pallas_call x1, Pallas kernels, read_out(): pl.pallas_call(functools.partial(readout_kernel, slabs, chunk), in_specs=...  3.07 us
    pallas_call x1, Pallas kernels, pack(): pl.pallas_call(pack_kernel, in_specs=[SMEM] + [VMEM] * 4, out_specs=[VMEM...  1.8 us
    pallas_call x1, Pallas kernels, bands(): pl.pallas_call(band_kernel, in_specs=[VMEM] * 6, out_specs=[VMEM] * 6, ou...  1.77 us
    ppermute x6, waiting for transfers between devices, from_all(): lax.ppermute(values[n], axis, [(i, i ^ k) for i in range(count)])  1.31 us
  transfers between devices with their start and end apart: 8, of which 3 were waited for; matrix products, arithmetic and copies ran while one was open for 0% of the time, Pallas kernels for 24%

profile of v4, /device:TPU:0, one launch (start us, length us, event | category | flops | bytes accessed | tf_op | source)
XLA Modules:
  0.0 39.2 jit_solution(3802023874287171657)
XLA Ops:
  1.3 1.8 %shard_map.191 = (bf16[384,128]{1,0:T(8,128)(2,1)}, bf16[384,128]{1,0:T(8,128)(2,1)}, bf16[384,128]{1,0:T(8,128)(2,1)}, bf16[384,128]{1,0:T(8,128)(2,1)}) custom-call(f32[1]{0:T(128)S(6)} %copy.21.step_ref, bf16[64,128]{1,0:T(8,128)(2,1)} %bitcast.8, s32[64,128]{1,0:T(8,128)} %bitcast.4, s32[64,128]{1,0:T(8,128)} %bitcast.6, f32[3,8192]{1,0:T(4,128)} %cot_ref.1), custom_call_target="tpu_custom_call" | custom-call | tf_op jit(solution)/shard_map/pallas_call | solution.py:71
  3.1 4.0 %collective-permute-start = (bf16[384,128]{1,0:T(8,128)(2,1)}, bf16[384,128]{1,0:T(8,128)(2,1)S(1)}, u32[]{:S(2)}, u32[]{:S(2)}) collective-permute-start(bf16[384,128]{1,0:T(8,128)(2,1)} %get-tuple-element.29), channel_id=1, source_target_pairs={{0,8},{4,12},{8,0},{12,4},{1,9},{5,13},{9,1},{13,5},{2,10},{6,14},... | collective-permute-start | bytes 294920 | tf_op jit(solution)/shard_map/ppermute | solution.py:604
  7.1 1.6 %collective-permute-start.1 = (bf16[384,128]{1,0:T(8,128)(2,1)}, bf16[384,128]{1,0:T(8,128)(2,1)S(1)}, u32[]{:S(2)}, u32[]{:S(2)}) collective-permute-start(bf16[384,128]{1,0:T(8,128)(2,1)} %get-tuple-element.30), channel_id=1, source_target_pairs={{0,4},{4,0},{8,12},{12,8},{1,5},{5,1},{9,13},{13,9},{2,6},{6,2},{1... | collective-permute-start | bytes 294920 | tf_op jit(solution)/shard_map/ppermute | solution.py:604
  8.7 0.9 %copy-done.7 = bf16[384,128]{1,0:T(8,128)(2,1)S(1)} copy-done((bf16[384,128]{1,0:T(8,128)(2,1)S(1)}, bf16[384,128]{1,0:T(8,128)(2,1)}, u32[]{:S(2)}) %copy-start.7) | copy-done | bytes 98328
  9.6 2.4 %shard_map.192.refs_0_ = f32[512,256]{1,0:T(8,128)S(1)} custom-call(bf16[384,128]{1,0:T(8,128)(2,1)S(1)} %copy-done.7), custom_call_target="tpu_custom_call" | custom-call | flops 2147483648 | bytes 1048576 | tf_op jit(solution)/shard_map/pallas_call | solution.py:147
  12.0 1.3 %collective-permute-done.refs_1_ = bf16[384,128]{1,0:T(8,128)(2,1)S(1)} collective-permute-done((bf16[384,128]{1,0:T(8,128)(2,1)}, bf16[384,128]{1,0:T(8,128)(2,1)S(1)}, u32[]{:S(2)}, u32[]{:S(2)}) %collective-permute-start) | collective-permute-done | bytes 98336 | tf_op jit(solution)/shard_map/ppermute | solution.py:604
  13.3 2.4 %shard_map.193.refs_0_ = f32[512,256]{1,0:T(8,128)S(1)} custom-call(f32[512,256]{1,0:T(8,128)S(1)} %shard_map.192.refs_0_, bf16[384,128]{1,0:T(8,128)(2,1)S(1)} %collective-permute-done.refs_1_), custom_call_target="tpu_custom_call" | custom-call | flops 2147483648 | bytes 1048576 | tf_op jit(solution)/shard_map/pallas_call | solution.py:147
  15.6 0.0 copy-start.11
  15.7 0.0 copy-start.12
  15.7 0.0 copy-start.13
  15.7 4.5 %shard_map.194 = (bf16[256,256]{1,0:T(8,128)(2,1)S(1)}, bf16[256,256]{1,0:T(8,128)(2,1)S(1)}) custom-call(f32[512,256]{1,0:T(8,128)S(1)} %shard_map.193.refs_0_, bf16[384,128]{1,0:T(8,128)(2,1)S(1)} %collective-permute-done.1.refs_1_, bf16[384,128]{1,0:T(8,128)(2,1)S(1)} %collective-permute-done.2.refs_2_), custom_call_target="tpu_custom_call" | custom-call | flops 4294967296 | bytes 1048576 | tf_op jit(solution)/shard_map/pallas_call | solution.py:147
  20.3 0.1 collective-permute-start.3
  20.3 0.5 %collective-permute-start.4 = (bf16[256,256]{1,0:T(8,128)(2,1)S(1)}, bf16[256,256]{1,0:T(8,128)(2,1)S(1)}, u32[]{:S(2)}, u32[]{:S(2)}) collective-permute-start(bf16[256,256]{1,0:T(8,128)(2,1)S(1)} %get-tuple-element.34.high_ref), channel_id=1, source_target_pairs={{0,1},{1,2},{2,3},{3,0},{4,5},{5,6},{6,7},{7,4},{8,9},{9,10},{10,1... | collective-permute-start | bytes 393224 | tf_op jit(solution)/shard_map/ppermute | solution.py:590
  20.8 0.1 copy-done.9
  20.9 1.8 %shard_map.195 = (bf16[112,144]{1,0:T(8,128)(2,1)S(1)}, bf16[96,1008]{1,0:T(8,128)(2,1)S(1)}, bf16[96,240]{1,0:T(8,128)(2,1)S(1)}, bf16[48,240]{1,0:T(8,128)(2,1...) custom-call(bf16[8,27]{1,0:T(8,128)(2,1)S(1)} %copy-done.9, bf16[8,216]{1,0:T(8,128)(2,1)S(1)} %copy-done.8, ...), custom_call_target="tpu_custom_call" | custom-call | flops 800000000 | bytes 4000000 | tf_op jit(solution)/shard_map/pallas_call | solution.py:254
  22.7 0.0 copy-start.4
  22.7 0.1 collective-permute-done.3.after_ref
  22.8 3.5 %collective-permute-done.4.before_ref = bf16[256,256]{1,0:T(8,128)(2,1)S(1)} collective-permute-done((bf16[256,256]{1,0:T(8,128)(2,1)S(1)}, bf16[256,256]{1,0:T(8,128)(2,1)S(1)}, u32[]{:S(2)}, u32[]{:S(2)}) %collective-permute-start.4) | collective-permute-done | bytes 131104 | tf_op jit(solution)/shard_map/ppermute | solution.py:590
  26.4 6.9 %shard_map.196 = (bf16[512,256]{1,0:T(8,128)(2,1)S(1)}, f32[24,256]{1,0:T(8,128)S(1)}) custom-call(bf16[256,256]{1,0:T(8,128)(2,1)S(1)} %get-tuple-element.33.low_ref, bf16[256,256]{1,0:T(8,128)(2,1)S(1)} %get-tuple-element.34.high_ref, bf16[256,256]{1,0:T(8,128)(2,1)S(1)} %collective-permute-done.3.after_ref, ...), custom_call_target="tpu_custom_call" | custom-call | tf_op jit(solution)/shard_map/pallas_call | solution.py:499
  33.3 0.1 collective-permute-start.7
  33.3 0.5 %collective-permute-start.6 = (f32[24,256]{1,0:T(8,128)S(1)}, f32[24,256]{1,0:T(8,128)S(1)}, u32[]{:S(2)}, u32[]{:S(2)}) collective-permute-start(f32[24,256]{1,0:T(8,128)S(1)} %get-tuple-element.47.refs_0_), channel_id=1, source_target_pairs={{0,1},{1,0},{2,3},{3,2},{4,5},{5,4},{6,7},{7,6},{8,9},{9,8},{10,11... | collective-permute-start | bytes 73736 | tf_op jit(solution)/shard_map/ppermute | solution.py:604
  33.8 1.7 %collective-permute-start.5 = (f32[24,256]{1,0:T(8,128)S(1)}, f32[24,256]{1,0:T(8,128)S(1)}, u32[]{:S(2)}, u32[]{:S(2)}) collective-permute-start(f32[24,256]{1,0:T(8,128)S(1)} %get-tuple-element.47.refs_0_), channel_id=1, source_target_pairs={{0,2},{1,3},{2,0},{3,1},{4,6},{5,7},{6,4},{7,5},{8,10},{9,11},{10,... | collective-permute-start | bytes 73736 | tf_op jit(solution)/shard_map/ppermute | solution.py:604
  35.5 3.1 %shard_map.197 = (f32[3,8192]{1,0:T(4,128)}, bf16[64,128]{1,0:T(8,128)(2,1)}) custom-call(f32[1]{0:T(128)S(6)} %copy.21.step_ref, s32[64,128]{1,0:T(8,128)S(1)} %bitcast.5, s32[64,128]{1,0:T(8,128)S(1)} %bitcast.7, f32[3,8192]{1,0:T(4,128)S(1)} %copy-done.6, bf16[512,256]{1,0:T(8,128)(2,1)S(1)} %get-tuple-element.44.mesh_ref), custom_call_target="tpu_custom_call" | custom-call | flops 2147483648 | bytes 1000000 | tf_op jit(solution)/shard_map/pallas_call | solution.py:549
  38.6 0.6 %shard_map.198 = (f32[8,27]{1,0:T(8,128)}, f32[8,216]{1,0:T(8,128)}, f32[3,216]{1,0:T(4,128)}) custom-call(f32[24,256]{1,0:T(8,128)S(1)} %get-tuple-element.47.refs_0_, f32[24,256]{1,0:T(8,128)S(1)} %collective-permute-done.5.refs_1_, f32[24,256]{1,0:T(8,128)S(1)} %collective-permute-done.6.refs_2_, f32[24,256]{1,0:T(8,128)S(1)} %collective-permute-done.7.refs_3_), custom_call_target="tpu_custom_call" | custom-call | tf_op jit(solution)/shard_map/pallas_call | solution.py:579
  (28 shorter events, 0.1 us)
Async XLA Ops:
  3.1 10.2 %collective-permute-start = (bf16[384,128]{1,0:T(8,128)(2,1)}, bf16[384,128]{1,0:T(8,128)(2,1)S(1)}, u32[]{:S(2)}, u32[]{:S(2)}) collective-permute-start(bf16[384,128]{1,0:T(8,128)(2,1)} %get-tuple-element.29), channel_id=1, source_target_pairs={{0,8},{4,12},{8,0},{12,4},{1,9},{5,13},{9,1},{13,5},{2,10},{6,14},... | collective-permute-start | bytes 294920 | tf_op jit(solution)/shard_map/ppermute | solution.py:604
  7.1 8.6 %collective-permute-start.1 = (bf16[384,128]{1,0:T(8,128)(2,1)}, bf16[384,128]{1,0:T(8,128)(2,1)S(1)}, u32[]{:S(2)}, u32[]{:S(2)}) collective-permute-start(bf16[384,128]{1,0:T(8,128)(2,1)} %get-tuple-element.30), channel_id=1, source_target_pairs={{0,4},{4,0},{8,12},{12,8},{1,5},{5,1},{9,13},{13,9},{2,6},{6,2},{1... | collective-permute-start | bytes 294920 | tf_op jit(solution)/shard_map/ppermute | solution.py:604
  8.7 7.0 %collective-permute-start.2 = (bf16[384,128]{1,0:T(8,128)(2,1)}, bf16[384,128]{1,0:T(8,128)(2,1)S(1)}, u32[]{:S(2)}, u32[]{:S(2)}) collective-permute-start(bf16[384,128]{1,0:T(8,128)(2,1)} %get-tuple-element.31), channel_id=1, source_target_pairs={{0,12},{4,8},{8,4},{12,0},{1,13},{5,9},{9,5},{13,1},{2,14},{6,10},... | collective-permute-start | bytes 294920 | tf_op jit(solution)/shard_map/ppermute | solution.py:604
  8.7 0.9 %copy-start.7 = (bf16[384,128]{1,0:T(8,128)(2,1)S(1)}, bf16[384,128]{1,0:T(8,128)(2,1)}, u32[]{:S(2)}) copy-start(bf16[384,128]{1,0:T(8,128)(2,1)} %get-tuple-element.28.refs_0_) | copy-start | bytes 294916
  15.6 5.2 %copy-start.8 = (bf16[8,216]{1,0:T(8,128)(2,1)S(1)}, bf16[8,216]{1,0:T(8,128)(2,1)}, u32[]{:S(2)}) copy-start(bf16[8,216]{1,0:T(8,128)(2,1)} %middle_ref) | copy-start | bytes 10372
  15.6 5.2 %copy-start.11 = (s32[8,1008]{1,0:T(8,128)S(1)}, s32[8,1008]{1,0:T(8,128)}, u32[]{:S(2)}) copy-start(s32[8,1008]{1,0:T(8,128)} %constant.15.clone.c2_ref) | copy-start | bytes 96772
  15.7 5.2 %copy-start.12 = (s32[8,864]{1,0:T(8,128)S(1)}, s32[8,864]{1,0:T(8,128)}, u32[]{:S(2)}) copy-start(s32[8,864]{1,0:T(8,128)} %constant.16.clone.c3_ref) | copy-start | bytes 82948
  15.7 5.2 %copy-start.13 = (s32[8,144]{1,0:T(8,128)S(1)}, s32[8,144]{1,0:T(8,128)}, u32[]{:S(2)}) copy-start(s32[8,144]{1,0:T(8,128)} %constant.14.clone.c1_ref) | copy-start | bytes 13828
  15.7 5.1 %copy-start.10 = (bf16[3,216]{1,0:T(4,128)(2,1)S(1)}, bf16[3,216]{1,0:T(4,128)(2,1)}, u32[]{:S(2)}) copy-start(bf16[3,216]{1,0:T(4,128)(2,1)} %last_ref) | copy-start | bytes 3892
  20.2 0.7 %copy-start.9 = (bf16[8,27]{1,0:T(8,128)(2,1)S(1)}, bf16[8,27]{1,0:T(8,128)(2,1)}, u32[]{:S(2)}) copy-start(bf16[8,27]{1,0:T(8,128)(2,1)} %first_ref) | copy-start | bytes 1300
  20.3 2.6 %collective-permute-start.3 = (bf16[256,256]{1,0:T(8,128)(2,1)S(1)}, bf16[256,256]{1,0:T(8,128)(2,1)S(1)}, u32[]{:S(2)}, u32[]{:S(2)}) collective-permute-start(bf16[256,256]{1,0:T(8,128)(2,1)S(1)} %get-tuple-element.33.low_ref), channel_id=1, source_target_pairs={{0,3},{1,0},{2,1},{3,2},{4,7},{5,4},{6,5},{7,6},{8,11},{9,8},{10,9... | collective-permute-start | bytes 393224 | tf_op jit(solution)/shard_map/ppermute | solution.py:590
  20.3 6.0 %collective-permute-start.4 = (bf16[256,256]{1,0:T(8,128)(2,1)S(1)}, bf16[256,256]{1,0:T(8,128)(2,1)S(1)}, u32[]{:S(2)}, u32[]{:S(2)}) collective-permute-start(bf16[256,256]{1,0:T(8,128)(2,1)S(1)} %get-tuple-element.34.high_ref), channel_id=1, source_target_pairs={{0,1},{1,2},{2,3},{3,0},{4,5},{5,6},{6,7},{7,4},{8,9},{9,10},{10,1... | collective-permute-start | bytes 393224 | tf_op jit(solution)/shard_map/ppermute | solution.py:590
  20.9 5.4 %copy-start.2 = (bf16[64,64]{1,0:T(8,128)(2,1)S(1)}, bf16[64,64]{1,0:T(8,128)(2,1)}, u32[]{:S(2)}) copy-start(bf16[64,64]{1,0:T(8,128)(2,1)} %constant.20.clone.order_ref) | copy-start | bytes 24580
  20.9 5.4 %copy-start.3 = (s32[8,336]{1,0:T(8,128)S(1)}, s32[8,336]{1,0:T(8,128)}, u32[]{:S(2)}) copy-start(s32[8,336]{1,0:T(8,128)} %constant.18.clone.c2_ref) | copy-start | bytes 32260
  20.9 5.4 %copy-start.5 = (s32[8,48]{1,0:T(8,128)S(1)}, s32[8,48]{1,0:T(8,128)}, u32[]{:S(2)}) copy-start(s32[8,48]{1,0:T(8,128)} %constant.17.clone.c1_ref) | copy-start | bytes 4612
  22.7 3.6 %copy-start.4 = (s32[8,240]{1,0:T(8,128)S(1)}, s32[8,240]{1,0:T(8,128)}, u32[]{:S(2)}) copy-start(s32[8,240]{1,0:T(8,128)} %constant.19.clone.c3_ref) | copy-start | bytes 23044
  26.3 9.1 %copy-start = (s32[8192,1]{0,1:T(1,128)S(1)}, s32[8192,1]{0,1:T(1,128)}, u32[]{:S(2)}) copy-start(s32[8192,1]{0,1:T(1,128)} %param.18) | copy-start | bytes 98308
  26.4 9.1 %copy-start.1 = (s32[8192]{0:T(1024)S(1)}, s32[8192]{0:T(1024)}, u32[]{:S(2)}) copy-start(s32[8192]{0:T(1024)} %param.19) | copy-start | bytes 98308
  26.4 9.1 %copy-start.6 = (f32[3,8192]{1,0:T(4,128)S(1)}, f32[3,8192]{1,0:T(4,128)}, u32[]{:S(2)}) copy-start(f32[3,8192]{1,0:T(4,128)} %velocity_ref.1) | copy-start | bytes 294916
  33.3 5.3 %collective-permute-start.7 = (f32[24,256]{1,0:T(8,128)S(1)}, f32[24,256]{1,0:T(8,128)S(1)}, u32[]{:S(2)}, u32[]{:S(2)}) collective-permute-start(f32[24,256]{1,0:T(8,128)S(1)} %get-tuple-element.47.refs_0_), channel_id=1, source_target_pairs={{0,3},{1,2},{2,1},{3,0},{4,7},{5,6},{6,5},{7,4},{8,11},{9,10},{10,... | collective-permute-start | bytes 73736 | tf_op jit(solution)/shard_map/ppermute | solution.py:604
  33.3 5.2 %collective-permute-start.6 = (f32[24,256]{1,0:T(8,128)S(1)}, f32[24,256]{1,0:T(8,128)S(1)}, u32[]{:S(2)}, u32[]{:S(2)}) collective-permute-start(f32[24,256]{1,0:T(8,128)S(1)} %get-tuple-element.47.refs_0_), channel_id=1, source_target_pairs={{0,1},{1,0},{2,3},{3,2},{4,5},{5,4},{6,7},{7,6},{8,9},{9,8},{10,11... | collective-permute-start | bytes 73736 | tf_op jit(solution)/shard_map/ppermute | solution.py:604
  33.8 4.7 %collective-permute-start.5 = (f32[24,256]{1,0:T(8,128)S(1)}, f32[24,256]{1,0:T(8,128)S(1)}, u32[]{:S(2)}, u32[]{:S(2)}) collective-permute-start(f32[24,256]{1,0:T(8,128)S(1)} %get-tuple-element.47.refs_0_), channel_id=1, source_target_pairs={{0,2},{1,3},{2,0},{3,1},{4,6},{5,7},{6,4},{7,5},{8,10},{9,11},{10,... | collective-permute-start | bytes 73736 | tf_op jit(solution)/shard_map/ppermute | solution.py:604

commit v5 on v4

--- a/solution.py
+++ b/solution.py
@@ -93,7 +93,7 @@
         store[16 * group : 16 * group + 16, :] = jnp.where(same, one, zero)
 
 
-def paint_kernel(slabs, chunk, tiles, started, final, count, *refs):
+def paint_kernel(slabs, chunk, tiles, started, halves, count, *refs):
     before, refs = (refs[0], refs[1:]) if started else (None, refs)
     messages, refs = refs[:count], refs[count:]
     outs, (hot, lane_hot, total) = refs[:-3], refs[-3:]
@@ -115,38 +115,33 @@
             code_tile = code if slabs <= 8 else jnp.where(spread(6) == eight // 8, code, -1.0)
             code_tile = code_tile.astype(BF16)
             for slab in range(eight, min(eight + 8, slabs)):
-                for half in range(2):
+                for number_of, half in enumerate(halves):
                     place = ((slab - eight) * 2 + half) * 16
                     same = code_tile == (sixteen + place).astype(F32).astype(BF16)
                     for field in range(FIELDS):
-                        first = ((half * FIELDS + field) * slabs + slab) * 16
+                        first = ((number_of * FIELDS + field) * slabs + slab) * 16
                         here[first : first + 16, :] = jnp.where(same, values[field], zero)
         part = dot_nt(here[...], here_lane[...])
         if number > 0:
             total[...] += part
         elif started:
-            total[...] = before[...] + part
+            skip = before.shape[0] - total.shape[0] if halves[0] else 0
+            total[...] = before[skip : skip + total.shape[0], :] + part
         else:
             total[...] = part
-    if final:
-        middle = total.shape[0] // 2
-        outs[0][...] = total[:middle, :].astype(BF16)
-        outs[1][...] = total[middle:, :].astype(BF16)
-    else:
-        outs[0][...] = total[...]
-
-
-def paint(before, messages, tiles, slabs, final):
+    outs[0][...] = total[...].astype(outs[0].dtype)
+
+
+def paint(before, messages, tiles, slabs, half=None):
     chunk = 128 * math.gcd(tiles, 16)
-    height = 2 * FIELDS * slabs * 16
+    halves = (0, 1) if half is None else (half,)
+    height = len(halves) * FIELDS * slabs * 16
     scratch = 2 * chunk * (height + XL) * 2 + height * XL * 4
-    shapes = [jax.ShapeDtypeStruct((height, XL), F32)]
-    if final:
-        shapes = [jax.ShapeDtypeStruct((height // 2, XL), BF16)] * 2
+    shapes = [jax.ShapeDtypeStruct((height, XL), F32 if half is None else BF16)]
     given = messages if before is None else [before] + messages
     return pl.pallas_call(
         functools.partial(
-            paint_kernel, slabs, chunk, tiles, before is not None, final, len(messages)
+            paint_kernel, slabs, chunk, tiles, before is not None, halves, len(messages)
         ),
         in_specs=[VMEM] * len(given),
         out_specs=[VMEM] * len(shapes),
@@ -160,7 +155,7 @@
         cost_estimate=pl.CostEstimate(
             flops=2 * height * XL * tiles * 128 * len(messages), bytes_accessed=MIB, transcendentals=0
         ),
-    )(*given)
+    )(*given)[0]
 
 
 def y_of(place):
@@ -614,11 +609,13 @@
     packed = pack(step_size, masses.reshape(dense), target, cells, cotangent, slabs)
     messages = from_all(packed, "slab")
     painted = None
-    for message in messages[:-2]:
-        painted = paint(painted, [message], dense[0], slabs, False)[0]
-    low, high = paint(painted, messages[-2:], dense[0], slabs, True)
+    for message in messages[:-1]:
+        painted = paint(painted, [message], dense[0], slabs)
+    high = paint(painted, messages[-1:], dense[0], slabs, 1)
+    before = shifted(high, column, 1)
+    low = paint(painted, messages[-1:], dense[0], slabs, 0)
     low, w_first, w_middle, w_last = lax.optimization_barrier((low, w_first, w_middle, w_last))
-    before, after = shifted(high, column, 1), shifted(low, column, -1)
+    after = shifted(low, column, -1)
     band_list = bands(w_first, w_middle, w_last)
     mesh, grads = network((low, high, after, before), band_list, w_middle.shape[0], slabs)
     all_grads = from_all(grads, column)

time: 39.4 us -> 38.8 us (0.985)
  waiting for transfers between devices: 4.92 us -> 3.76 us
  Pallas kernels: 23.4 us -> 23.8 us
    ppermute x2, waiting for transfers between devices: 3.61 us -> 2.14 us  [shifted(): lax.ppermute(value, axis, [(i, (i + distance) % count) for i in range(cou...]
    pallas_call x3 -> x5, Pallas kernels: 9.25 us -> 9.67 us  [paint(): pl.pallas_call(functools.partial(paint_kernel, slabs, chunk, tiles, befor...]
  transfers between devices with their start and end apart: 8 -> 8, of which waited for: 3 -> 3; matrix products, arithmetic and copies ran while one was open for 0% -> 0% of each run, Pallas kernels for 24% -> 34%
where the time goes in v5:
time: 38.8 us; the launch traced here: 38.6 us
  Pallas kernels  23.8 us (61%)
  starting transfers between devices  8.59 us (22%)
  waiting for transfers between devices  3.76 us (10%)
  between operations  1.51 us (4%)
  local copies, waits for them, and re-layouts  0.98 us (3%)
    pallas_call x5, Pallas kernels, paint(): pl.pallas_call(functools.partial(paint_kernel, slabs, chunk, tiles, befor...  9.67 us
    ppermute x6, starting transfers between devices, from_all(): lax.ppermute(values[n], axis, [(i, i ^ k) for i in range(count)])  7.81 us
    pallas_call x1, Pallas kernels, network(): pl.pallas_call(functools.partial(net_kernel, slabs, channels, shared), in...  6.86 us
    pallas_call x1, Pallas kernels, read_out(): pl.pallas_call(functools.partial(readout_kernel, slabs, chunk), in_specs=...  3.07 us
    ppermute x2, waiting for transfers between devices, shifted(): lax.ppermute(value, axis, [(i, (i + distance) % count) for i in range(cou...  2.14 us
    pallas_call x1, Pallas kernels, pack(): pl.pallas_call(pack_kernel, in_specs=[SMEM] + [VMEM] * 4, out_specs=[VMEM...  1.8 us
    pallas_call x1, Pallas kernels, bands(): pl.pallas_call(band_kernel, in_specs=[VMEM] * 6, out_specs=[VMEM] * 6, ou...  1.77 us
    ppermute x6, waiting for transfers between devices, from_all(): lax.ppermute(values[n], axis, [(i, i ^ k) for i in range(count)])  1.62 us
  transfers between devices with their start and end apart: 8, of which 3 were waited for; matrix products, arithmetic and copies ran while one was open for 0% of the time, Pallas kernels for 34%

profile of v5, /device:TPU:0, one launch (start us, length us, event | category | flops | bytes accessed | tf_op | source)
XLA Modules:
  0.0 38.6 jit_solution(297645584303323641)
XLA Ops:
  1.3 1.8 %shard_map.191 = (bf16[384,128]{1,0:T(8,128)(2,1)}, bf16[384,128]{1,0:T(8,128)(2,1)}, bf16[384,128]{1,0:T(8,128)(2,1)}, bf16[384,128]{1,0:T(8,128)(2,1)}) custom-call(f32[1]{0:T(128)S(6)} %copy.21.step_ref, bf16[64,128]{1,0:T(8,128)(2,1)} %bitcast.8, s32[64,128]{1,0:T(8,128)} %bitcast.4, s32[64,128]{1,0:T(8,128)} %bitcast.6, f32[3,8192]{1,0:T(4,128)} %cot_ref.1), custom_call_target="tpu_custom_call" | custom-call | tf_op jit(solution)/shard_map/pallas_call | solution.py:71
  3.1 4.0 %collective-permute-start = (bf16[384,128]{1,0:T(8,128)(2,1)}, bf16[384,128]{1,0:T(8,128)(2,1)S(1)}, u32[]{:S(2)}, u32[]{:S(2)}) collective-permute-start(bf16[384,128]{1,0:T(8,128)(2,1)} %get-tuple-element.27), channel_id=1, source_target_pairs={{0,8},{4,12},{8,0},{12,4},{1,9},{5,13},{9,1},{13,5},{2,10},{6,14},... | collective-permute-start | bytes 294920 | tf_op jit(solution)/shard_map/ppermute | solution.py:599
  7.1 1.6 %collective-permute-start.1 = (bf16[384,128]{1,0:T(8,128)(2,1)}, bf16[384,128]{1,0:T(8,128)(2,1)S(1)}, u32[]{:S(2)}, u32[]{:S(2)}) collective-permute-start(bf16[384,128]{1,0:T(8,128)(2,1)} %get-tuple-element.28), channel_id=1, source_target_pairs={{0,4},{4,0},{8,12},{12,8},{1,5},{5,1},{9,13},{13,9},{2,6},{6,2},{1... | collective-permute-start | bytes 294920 | tf_op jit(solution)/shard_map/ppermute | solution.py:599
  8.7 0.9 %copy-done.7 = bf16[384,128]{1,0:T(8,128)(2,1)S(1)} copy-done((bf16[384,128]{1,0:T(8,128)(2,1)S(1)}, bf16[384,128]{1,0:T(8,128)(2,1)}, u32[]{:S(2)}) %copy-start.7) | copy-done | bytes 98328
  9.6 2.4 %shard_map.192.refs_0_ = f32[512,256]{1,0:T(8,128)S(1)} custom-call(bf16[384,128]{1,0:T(8,128)(2,1)S(1)} %copy-done.7), custom_call_target="tpu_custom_call" | custom-call | flops 2147483648 | bytes 1048576 | tf_op jit(solution)/shard_map/pallas_call | solution.py:142
  12.0 1.3 %collective-permute-done.refs_1_ = bf16[384,128]{1,0:T(8,128)(2,1)S(1)} collective-permute-done((bf16[384,128]{1,0:T(8,128)(2,1)}, bf16[384,128]{1,0:T(8,128)(2,1)S(1)}, u32[]{:S(2)}, u32[]{:S(2)}) %collective-permute-start) | collective-permute-done | bytes 98336 | tf_op jit(solution)/shard_map/ppermute | solution.py:599
  13.3 2.4 %shard_map.193.refs_0_ = f32[512,256]{1,0:T(8,128)S(1)} custom-call(f32[512,256]{1,0:T(8,128)S(1)} %shard_map.192.refs_0_, bf16[384,128]{1,0:T(8,128)(2,1)S(1)} %collective-permute-done.refs_1_), custom_call_target="tpu_custom_call" | custom-call | flops 2147483648 | bytes 1048576 | tf_op jit(solution)/shard_map/pallas_call | solution.py:142
  15.6 2.4 %shard_map.194.refs_0_ = f32[512,256]{1,0:T(8,128)S(1)} custom-call(f32[512,256]{1,0:T(8,128)S(1)} %shard_map.193.refs_0_, bf16[384,128]{1,0:T(8,128)(2,1)S(1)} %collective-permute-done.1.refs_1_), custom_call_target="tpu_custom_call" | custom-call | flops 2147483648 | bytes 1048576 | tf_op jit(solution)/shard_map/pallas_call | solution.py:142
  18.0 1.3 %shard_map.195.low_ref = bf16[256,256]{1,0:T(8,128)(2,1)S(1)} custom-call(f32[512,256]{1,0:T(8,128)S(1)} %shard_map.194.refs_0_, bf16[384,128]{1,0:T(8,128)(2,1)S(1)} %collective-permute-done.2.refs_1_), custom_call_target="tpu_custom_call" | custom-call | flops 1073741824 | bytes 1048576 | tf_op jit(solution)/shard_map/pallas_call | solution.py:142
  19.4 0.0 copy-start.11
  19.4 0.0 copy-start.12
  19.4 0.0 copy-start.13
  19.4 0.1 collective-permute-start.3
  19.5 1.3 %shard_map.196.high_ref = bf16[256,256]{1,0:T(8,128)(2,1)S(1)} custom-call(f32[512,256]{1,0:T(8,128)S(1)} %shard_map.194.refs_0_, bf16[384,128]{1,0:T(8,128)(2,1)S(1)} %collective-permute-done.2.refs_1_), custom_call_target="tpu_custom_call" | custom-call | flops 1073741824 | bytes 1048576 | tf_op jit(solution)/shard_map/pallas_call | solution.py:142
  20.8 0.7 %collective-permute-start.4 = (bf16[256,256]{1,0:T(8,128)(2,1)S(1)}, bf16[256,256]{1,0:T(8,128)(2,1)S(1)}, u32[]{:S(2)}, u32[]{:S(2)}) collective-permute-start(bf16[256,256]{1,0:T(8,128)(2,1)S(1)} %shard_map.196.high_ref), channel_id=1, source_target_pairs={{0,1},{1,2},{2,3},{3,0},{4,5},{5,6},{6,7},{7,4},{8,9},{9,10},{10,1... | collective-permute-start | bytes 393224 | tf_op jit(solution)/shard_map/ppermute | solution.py:585
  21.5 1.8 %shard_map.197 = (bf16[112,144]{1,0:T(8,128)(2,1)S(1)}, bf16[96,1008]{1,0:T(8,128)(2,1)S(1)}, bf16[96,240]{1,0:T(8,128)(2,1)S(1)}, bf16[48,240]{1,0:T(8,128)(2,1...) custom-call(bf16[8,27]{1,0:T(8,128)(2,1)S(1)} %copy-done.9, bf16[8,216]{1,0:T(8,128)(2,1)S(1)} %copy-done.8, ...), custom_call_target="tpu_custom_call" | custom-call | flops 800000000 | bytes 4000000 | tf_op jit(solution)/shard_map/pallas_call | solution.py:249
  23.3 2.1 %collective-permute-done.4.before_ref = bf16[256,256]{1,0:T(8,128)(2,1)S(1)} collective-permute-done((bf16[256,256]{1,0:T(8,128)(2,1)S(1)}, bf16[256,256]{1,0:T(8,128)(2,1)S(1)}, u32[]{:S(2)}, u32[]{:S(2)}) %collective-permute-start.4) | collective-permute-done | bytes 131104 | tf_op jit(solution)/shard_map/ppermute | solution.py:585
  25.5 6.9 %shard_map.198 = (bf16[512,256]{1,0:T(8,128)(2,1)S(1)}, f32[24,256]{1,0:T(8,128)S(1)}) custom-call(bf16[256,256]{1,0:T(8,128)(2,1)S(1)} %shard_map.195.low_ref, bf16[256,256]{1,0:T(8,128)(2,1)S(1)} %shard_map.196.high_ref, bf16[256,256]{1,0:T(8,128)(2,1)S(1)} %collective-permute-done.3.after_ref, bf16[256,256]{1,0:T(8,128)(2,1)S(1)} %collective-permute-done.4.before_ref, ...), custom_call_target="tpu_custom_call" | custom-call | tf_op jit(solution)/shard_map/pallas_call | solution.py:494
  32.4 0.1 collective-permute-start.7
  32.5 1.7 %collective-permute-start.6 = (f32[24,256]{1,0:T(8,128)S(1)}, f32[24,256]{1,0:T(8,128)S(1)}, u32[]{:S(2)}, u32[]{:S(2)}) collective-permute-start(f32[24,256]{1,0:T(8,128)S(1)} %get-tuple-element.43.refs_0_), channel_id=1, source_target_pairs={{0,1},{1,0},{2,3},{3,2},{4,5},{5,4},{6,7},{7,6},{8,9},{9,8},{10,11... | collective-permute-start | bytes 73736 | tf_op jit(solution)/shard_map/ppermute | solution.py:599
  34.2 0.4 %collective-permute-start.5 = (f32[24,256]{1,0:T(8,128)S(1)}, f32[24,256]{1,0:T(8,128)S(1)}, u32[]{:S(2)}, u32[]{:S(2)}) collective-permute-start(f32[24,256]{1,0:T(8,128)S(1)} %get-tuple-element.43.refs_0_), channel_id=1, source_target_pairs={{0,2},{1,3},{2,0},{3,1},{4,6},{5,7},{6,4},{7,5},{8,10},{9,11},{10,... | collective-permute-start | bytes 73736 | tf_op jit(solution)/shard_map/ppermute | solution.py:599
  34.6 3.1 %shard_map.199 = (f32[3,8192]{1,0:T(4,128)}, bf16[64,128]{1,0:T(8,128)(2,1)}) custom-call(f32[1]{0:T(128)S(6)} %copy.21.step_ref, s32[64,128]{1,0:T(8,128)S(1)} %bitcast.5, s32[64,128]{1,0:T(8,128)S(1)} %bitcast.7, f32[3,8192]{1,0:T(4,128)S(1)} %copy-done.6, bf16[512,256]{1,0:T(8,128)(2,1)S(1)} %get-tuple-element.40.mesh_ref), custom_call_target="tpu_custom_call" | custom-call | flops 2147483648 | bytes 1000000 | tf_op jit(solution)/shard_map/pallas_call | solution.py:544
  37.7 0.3 collective-permute-done.5.refs_1_
  38.0 0.6 %shard_map.200 = (f32[8,27]{1,0:T(8,128)}, f32[8,216]{1,0:T(8,128)}, f32[3,216]{1,0:T(4,128)}) custom-call(f32[24,256]{1,0:T(8,128)S(1)} %get-tuple-element.43.refs_0_, f32[24,256]{1,0:T(8,128)S(1)} %collective-permute-done.5.refs_1_, f32[24,256]{1,0:T(8,128)S(1)} %collective-permute-done.6.refs_2_, f32[24,256]{1,0:T(8,128)S(1)} %collective-permute-done.7.refs_3_), custom_call_target="tpu_custom_call" | custom-call | tf_op jit(solution)/shard_map/pallas_call | solution.py:574
  (30 shorter events, 0.1 us)
Async XLA Ops:
  3.1 10.2 %collective-permute-start = (bf16[384,128]{1,0:T(8,128)(2,1)}, bf16[384,128]{1,0:T(8,128)(2,1)S(1)}, u32[]{:S(2)}, u32[]{:S(2)}) collective-permute-start(bf16[384,128]{1,0:T(8,128)(2,1)} %get-tuple-element.27), channel_id=1, source_target_pairs={{0,8},{4,12},{8,0},{12,4},{1,9},{5,13},{9,1},{13,5},{2,10},{6,14},... | collective-permute-start | bytes 294920 | tf_op jit(solution)/shard_map/ppermute | solution.py:599
  7.1 8.5 %collective-permute-start.1 = (bf16[384,128]{1,0:T(8,128)(2,1)}, bf16[384,128]{1,0:T(8,128)(2,1)S(1)}, u32[]{:S(2)}, u32[]{:S(2)}) collective-permute-start(bf16[384,128]{1,0:T(8,128)(2,1)} %get-tuple-element.28), channel_id=1, source_target_pairs={{0,4},{4,0},{8,12},{12,8},{1,5},{5,1},{9,13},{13,9},{2,6},{6,2},{1... | collective-permute-start | bytes 294920 | tf_op jit(solution)/shard_map/ppermute | solution.py:599
  8.7 9.3 %collective-permute-start.2 = (bf16[384,128]{1,0:T(8,128)(2,1)}, bf16[384,128]{1,0:T(8,128)(2,1)S(1)}, u32[]{:S(2)}, u32[]{:S(2)}) collective-permute-start(bf16[384,128]{1,0:T(8,128)(2,1)} %get-tuple-element.29), channel_id=1, source_target_pairs={{0,12},{4,8},{8,4},{12,0},{1,13},{5,9},{9,5},{13,1},{2,14},{6,10},... | collective-permute-start | bytes 294920 | tf_op jit(solution)/shard_map/ppermute | solution.py:599
  8.7 0.9 %copy-start.7 = (bf16[384,128]{1,0:T(8,128)(2,1)S(1)}, bf16[384,128]{1,0:T(8,128)(2,1)}, u32[]{:S(2)}) copy-start(bf16[384,128]{1,0:T(8,128)(2,1)} %get-tuple-element.26.refs_0_) | copy-start | bytes 294916
  19.3 2.2 %copy-start.8 = (bf16[8,216]{1,0:T(8,128)(2,1)S(1)}, bf16[8,216]{1,0:T(8,128)(2,1)}, u32[]{:S(2)}) copy-start(bf16[8,216]{1,0:T(8,128)(2,1)} %middle_ref) | copy-start | bytes 10372
  19.3 2.1 %copy-start.9 = (bf16[8,27]{1,0:T(8,128)(2,1)S(1)}, bf16[8,27]{1,0:T(8,128)(2,1)}, u32[]{:S(2)}) copy-start(bf16[8,27]{1,0:T(8,128)(2,1)} %first_ref) | copy-start | bytes 1300
  19.3 2.1 %copy-start.10 = (bf16[3,216]{1,0:T(4,128)(2,1)S(1)}, bf16[3,216]{1,0:T(4,128)(2,1)}, u32[]{:S(2)}) copy-start(bf16[3,216]{1,0:T(4,128)(2,1)} %last_ref) | copy-start | bytes 3892
  19.4 2.1 %copy-start.11 = (s32[8,1008]{1,0:T(8,128)S(1)}, s32[8,1008]{1,0:T(8,128)}, u32[]{:S(2)}) copy-start(s32[8,1008]{1,0:T(8,128)} %constant.15.clone.c2_ref) | copy-start | bytes 96772
  19.4 2.1 %copy-start.12 = (s32[8,864]{1,0:T(8,128)S(1)}, s32[8,864]{1,0:T(8,128)}, u32[]{:S(2)}) copy-start(s32[8,864]{1,0:T(8,128)} %constant.16.clone.c3_ref) | copy-start | bytes 82948
  19.4 2.1 %copy-start.13 = (s32[8,144]{1,0:T(8,128)S(1)}, s32[8,144]{1,0:T(8,128)}, u32[]{:S(2)}) copy-start(s32[8,144]{1,0:T(8,128)} %constant.14.clone.c1_ref) | copy-start | bytes 13828
  19.4 3.9 %collective-permute-start.3 = (bf16[256,256]{1,0:T(8,128)(2,1)S(1)}, bf16[256,256]{1,0:T(8,128)(2,1)S(1)}, u32[]{:S(2)}, u32[]{:S(2)}) collective-permute-start(bf16[256,256]{1,0:T(8,128)(2,1)S(1)} %shard_map.195.low_ref), channel_id=1, source_target_pairs={{0,3},{1,0},{2,1},{3,2},{4,7},{5,4},{6,5},{7,6},{8,11},{9,8},{10,9... | collective-permute-start | bytes 393224 | tf_op jit(solution)/shard_map/ppermute | solution.py:585
  20.8 4.7 %collective-permute-start.4 = (bf16[256,256]{1,0:T(8,128)(2,1)S(1)}, bf16[256,256]{1,0:T(8,128)(2,1)S(1)}, u32[]{:S(2)}, u32[]{:S(2)}) collective-permute-start(bf16[256,256]{1,0:T(8,128)(2,1)S(1)} %shard_map.196.high_ref), channel_id=1, source_target_pairs={{0,1},{1,2},{2,3},{3,0},{4,5},{5,6},{6,7},{7,4},{8,9},{9,10},{10,1... | collective-permute-start | bytes 393224 | tf_op jit(solution)/shard_map/ppermute | solution.py:585
  21.5 4.0 %copy-start.2 = (bf16[64,64]{1,0:T(8,128)(2,1)S(1)}, bf16[64,64]{1,0:T(8,128)(2,1)}, u32[]{:S(2)}) copy-start(bf16[64,64]{1,0:T(8,128)(2,1)} %constant.20.clone.order_ref) | copy-start | bytes 24580
  21.5 4.0 %copy-start.3 = (s32[8,336]{1,0:T(8,128)S(1)}, s32[8,336]{1,0:T(8,128)}, u32[]{:S(2)}) copy-start(s32[8,336]{1,0:T(8,128)} %constant.18.clone.c2_ref) | copy-start | bytes 32260
  21.5 4.0 %copy-start.5 = (s32[8,48]{1,0:T(8,128)S(1)}, s32[8,48]{1,0:T(8,128)}, u32[]{:S(2)}) copy-start(s32[8,48]{1,0:T(8,128)} %constant.17.clone.c1_ref) | copy-start | bytes 4612
  23.3 2.2 %copy-start.4 = (s32[8,240]{1,0:T(8,128)S(1)}, s32[8,240]{1,0:T(8,128)}, u32[]{:S(2)}) copy-start(s32[8,240]{1,0:T(8,128)} %constant.19.clone.c3_ref) | copy-start | bytes 23044
  25.5 9.1 %copy-start = (s32[8192,1]{0,1:T(1,128)S(1)}, s32[8192,1]{0,1:T(1,128)}, u32[]{:S(2)}) copy-start(s32[8192,1]{0,1:T(1,128)} %param.18) | copy-start | bytes 98308
  25.5 9.1 %copy-start.1 = (s32[8192]{0:T(1024)S(1)}, s32[8192]{0:T(1024)}, u32[]{:S(2)}) copy-start(s32[8192]{0:T(1024)} %param.19) | copy-start | bytes 98308
  25.5 9.1 %copy-start.6 = (f32[3,8192]{1,0:T(4,128)S(1)}, f32[3,8192]{1,0:T(4,128)}, u32[]{:S(2)}) copy-start(f32[3,8192]{1,0:T(4,128)} %velocity_ref.1) | copy-start | bytes 294916
  32.4 5.3 %collective-permute-start.7 = (f32[24,256]{1,0:T(8,128)S(1)}, f32[24,256]{1,0:T(8,128)S(1)}, u32[]{:S(2)}, u32[]{:S(2)}) collective-permute-start(f32[24,256]{1,0:T(8,128)S(1)} %get-tuple-element.43.refs_0_), channel_id=1, source_target_pairs={{0,3},{1,2},{2,1},{3,0},{4,7},{5,6},{6,5},{7,4},{8,11},{9,10},{10,... | collective-permute-start | bytes 73736 | tf_op jit(solution)/shard_map/ppermute | solution.py:599
  32.5 5.2 %collective-permute-start.6 = (f32[24,256]{1,0:T(8,128)S(1)}, f32[24,256]{1,0:T(8,128)S(1)}, u32[]{:S(2)}, u32[]{:S(2)}) collective-permute-start(f32[24,256]{1,0:T(8,128)S(1)} %get-tuple-element.43.refs_0_), channel_id=1, source_target_pairs={{0,1},{1,0},{2,3},{3,2},{4,5},{5,4},{6,7},{7,6},{8,9},{9,8},{10,11... | collective-permute-start | bytes 73736 | tf_op jit(solution)/shard_map/ppermute | solution.py:599
  34.2 3.8 %collective-permute-start.5 = (f32[24,256]{1,0:T(8,128)S(1)}, f32[24,256]{1,0:T(8,128)S(1)}, u32[]{:S(2)}, u32[]{:S(2)}) collective-permute-start(f32[24,256]{1,0:T(8,128)S(1)} %get-tuple-element.43.refs_0_), channel_id=1, source_target_pairs={{0,2},{1,3},{2,0},{3,1},{4,6},{5,7},{6,4},{7,5},{8,10},{9,11},{10,... | collective-permute-start | bytes 73736 | tf_op jit(solution)/shard_map/ppermute | solution.py:599

commit v6 on v5

--- a/solution.py
+++ b/solution.py
@@ -50,13 +50,13 @@
         for t in range(tiles):
             row = component * tiles + t
             rows[row : row + 1, :] = cot_ref[component : component + 1, t * 128 : (t + 1) * 128]
-    parts = [
-        mass_ref[...],
-        (step_ref[0] * rows[...]).astype(BF16),
-        code.astype(F32).astype(BF16),
-        (cell & (XL - 1)).astype(F32).astype(BF16),
-        (slab >> 3).astype(F32).astype(BF16),
-    ]
+    parts = [mass_ref[...], (step_ref[0] * rows[...]).astype(BF16)]
+    lane = cell & (XL - 1)
+    if outs[0].shape[0] == 5 * tiles:
+        value = (128 + (lane & 127)).astype(F32) * jnp.exp2((code - 64).astype(F32))
+        parts.append(jnp.where(lane > 127, -value, value).astype(BF16))
+    else:
+        parts += [part.astype(F32).astype(BF16) for part in (code, lane, slab >> 3)]
     for out_ref in outs:
         first = 0
         for part in parts:
@@ -65,9 +65,13 @@
             first += part.shape[0]
 
 
+def message_rows(slabs):
+    return 5 if slabs <= 4 else 6 if slabs <= 8 else 7
+
+
 def pack(step_size, masses, target, cells, cotangent, slabs):
     tiles = masses.shape[0]
-    shape = jax.ShapeDtypeStruct(((6 if slabs <= 8 else 7) * tiles, 128), BF16)
+    shape = jax.ShapeDtypeStruct((message_rows(slabs) * tiles, 128), BF16)
     return pl.pallas_call(
         pack_kernel,
         in_specs=[SMEM] + [VMEM] * 4,
@@ -91,6 +95,16 @@
     for group in range(XL // 16):
         same = lane == (sixteen + 16 * group).astype(F32).astype(BF16)
         store[16 * group : 16 * group + 16, :] = jnp.where(same, one, zero)
+
+
+def cell_parts(message, tiles, slabs):
+    value = message[4 * tiles : 5 * tiles, :].astype(F32)
+    if message_rows(slabs) > 5:
+        return value, message[5 * tiles : 6 * tiles, :].astype(F32)
+    size = jnp.abs(value)
+    power = jnp.floor(jnp.log2(size) + 0.002)
+    mantissa = jnp.floor(size * jnp.exp2(-power) * 128.0 + 0.5)
+    return power + 57.0, jnp.where(value < 0.0, mantissa, mantissa - 128.0)
 
 
 def paint_kernel(slabs, chunk, tiles, started, halves, count, *refs):
@@ -108,9 +122,12 @@
             rows = message[field * tiles : (field + 1) * tiles, :].astype(F32)
             return spread_rows(rows, 16, turn * step, step)
 
-        fill_lane_hot(here_lane, spread(5).astype(BF16), chunk)
+        if turn == 0:
+            codes, lanes = cell_parts(message, tiles, slabs)
+        lane = spread_rows(lanes, 16, turn * step, step).astype(BF16)
+        fill_lane_hot(here_lane, lane, chunk)
         values = [spread(field).astype(BF16) for field in range(FIELDS)]
-        code = spread(4)
+        code = spread_rows(codes, 16, turn * step, step)
         for eight in range(0, slabs, 8):
             code_tile = code if slabs <= 8 else jnp.where(spread(6) == eight // 8, code, -1.0)
             code_tile = code_tile.astype(BF16)

time: 38.8 us -> 37.6 us (0.969)
  waiting for transfers between devices: 3.76 us -> 2.49 us
    ppermute x6, waiting for transfers between devices: 1.62 us -> 0.1 us  [from_all(): lax.ppermute(values[n], axis, [(i, i ^ k) for i in range(count)])]
  transfers between devices with their start and end apart: 8 -> 8, of which waited for: 3 -> 2; matrix products, arithmetic and copies ran while one was open for 0% -> 0% of each run, Pallas kernels for 34% -> 36%
where the time goes in v6:
time: 37.6 us; the launch traced here: 37.4 us
  Pallas kernels  23.8 us (63%)
  starting transfers between devices  8.61 us (23%)
  waiting for transfers between devices  2.49 us (7%)
  between operations  1.51 us (4%)
  local copies, waits for them, and re-layouts  0.97 us (3%)
    pallas_call x5, Pallas kernels, paint(): pl.pallas_call(functools.partial(paint_kernel, slabs, chunk, tiles, befor...  9.74 us
    ppermute x6, starting transfers between devices, from_all(): lax.ppermute(values[n], axis, [(i, i ^ k) for i in range(count)])  7.81 us
    pallas_call x1, Pallas kernels, network(): pl.pallas_call(functools.partial(net_kernel, slabs, channels, shared), in...  6.86 us
    pallas_call x1, Pallas kernels, read_out(): pl.pallas_call(functools.partial(readout_kernel, slabs, chunk), in_specs=...  3.07 us
    ppermute x2, waiting for transfers between devices, shifted(): lax.ppermute(value, axis, [(i, (i + distance) % count) for i in range(cou...  2.39 us
    pallas_call x1, Pallas kernels, pack(): pl.pallas_call(pack_kernel, in_specs=[SMEM] + [VMEM] * 4, out_specs=[VMEM...  1.79 us
    pallas_call x1, Pallas kernels, bands(): pl.pallas_call(band_kernel, in_specs=[VMEM] * 6, out_specs=[VMEM] * 6, ou...  1.77 us
    unnamed x28, local copies, waits for them, and re-layouts  0.97 us
  transfers between devices with their start and end apart: 8, of which 2 were waited for; matrix products, arithmetic and copies ran while one was open for 0% of the time, Pallas kernels for 36%

profile of v6, /device:TPU:0, one launch (start us, length us, event | category | flops | bytes accessed | tf_op | source)
XLA Modules:
  0.0 37.4 jit_solution(18444691123712344173)
XLA Ops:
  1.3 1.8 %shard_map.191 = (bf16[320,128]{1,0:T(8,128)(2,1)}, bf16[320,128]{1,0:T(8,128)(2,1)}, bf16[320,128]{1,0:T(8,128)(2,1)}, bf16[320,128]{1,0:T(8,128)(2,1)}) custom-call(f32[1]{0:T(128)S(6)} %copy.21.step_ref, bf16[64,128]{1,0:T(8,128)(2,1)} %bitcast.8, s32[64,128]{1,0:T(8,128)} %bitcast.4, s32[64,128]{1,0:T(8,128)} %bitcast.6, f32[3,8192]{1,0:T(4,128)} %cot_ref.1), custom_call_target="tpu_custom_call" | custom-call | tf_op jit(solution)/shard_map/pallas_call | solution.py:75
  3.1 4.0 %collective-permute-start = (bf16[320,128]{1,0:T(8,128)(2,1)}, bf16[320,128]{1,0:T(8,128)(2,1)S(1)}, u32[]{:S(2)}, u32[]{:S(2)}) collective-permute-start(bf16[320,128]{1,0:T(8,128)(2,1)} %get-tuple-element.27), channel_id=1, source_target_pairs={{0,8},{4,12},{8,0},{12,4},{1,9},{5,13},{9,1},{13,5},{2,10},{6,14},... | collective-permute-start | bytes 245768 | tf_op jit(solution)/shard_map/ppermute | solution.py:616
  7.1 1.6 %collective-permute-start.1 = (bf16[320,128]{1,0:T(8,128)(2,1)}, bf16[320,128]{1,0:T(8,128)(2,1)S(1)}, u32[]{:S(2)}, u32[]{:S(2)}) collective-permute-start(bf16[320,128]{1,0:T(8,128)(2,1)} %get-tuple-element.28), channel_id=1, source_target_pairs={{0,4},{4,0},{8,12},{12,8},{1,5},{5,1},{9,13},{13,9},{2,6},{6,2},{1... | collective-permute-start | bytes 245768 | tf_op jit(solution)/shard_map/ppermute | solution.py:616
  8.7 0.9 %copy-done.7 = bf16[320,128]{1,0:T(8,128)(2,1)S(1)} copy-done((bf16[320,128]{1,0:T(8,128)(2,1)S(1)}, bf16[320,128]{1,0:T(8,128)(2,1)}, u32[]{:S(2)}) %copy-start.7) | copy-done | bytes 81944
  9.6 2.4 %shard_map.192.refs_0_ = f32[512,256]{1,0:T(8,128)S(1)} custom-call(bf16[320,128]{1,0:T(8,128)(2,1)S(1)} %copy-done.7), custom_call_target="tpu_custom_call" | custom-call | flops 2147483648 | bytes 1048576 | tf_op jit(solution)/shard_map/pallas_call | solution.py:159
  12.0 2.4 %shard_map.193.refs_0_ = f32[512,256]{1,0:T(8,128)S(1)} custom-call(f32[512,256]{1,0:T(8,128)S(1)} %shard_map.192.refs_0_, bf16[320,128]{1,0:T(8,128)(2,1)S(1)} %collective-permute-done.refs_1_), custom_call_target="tpu_custom_call" | custom-call | flops 2147483648 | bytes 1048576 | tf_op jit(solution)/shard_map/pallas_call | solution.py:159
  14.4 2.4 %shard_map.194.refs_0_ = f32[512,256]{1,0:T(8,128)S(1)} custom-call(f32[512,256]{1,0:T(8,128)S(1)} %shard_map.193.refs_0_, bf16[320,128]{1,0:T(8,128)(2,1)S(1)} %collective-permute-done.1.refs_1_), custom_call_target="tpu_custom_call" | custom-call | flops 2147483648 | bytes 1048576 | tf_op jit(solution)/shard_map/pallas_call | solution.py:159
  16.8 1.3 %shard_map.195.low_ref = bf16[256,256]{1,0:T(8,128)(2,1)S(1)} custom-call(f32[512,256]{1,0:T(8,128)S(1)} %shard_map.194.refs_0_, bf16[320,128]{1,0:T(8,128)(2,1)S(1)} %collective-permute-done.2.refs_1_), custom_call_target="tpu_custom_call" | custom-call | flops 1073741824 | bytes 1048576 | tf_op jit(solution)/shard_map/pallas_call | solution.py:159
  18.1 0.0 copy-start.11
  18.1 0.0 copy-start.12
  18.1 0.0 copy-start.13
  18.2 0.4 %collective-permute-start.3 = (bf16[256,256]{1,0:T(8,128)(2,1)S(1)}, bf16[256,256]{1,0:T(8,128)(2,1)S(1)}, u32[]{:S(2)}, u32[]{:S(2)}) collective-permute-start(bf16[256,256]{1,0:T(8,128)(2,1)S(1)} %shard_map.195.low_ref), channel_id=1, source_target_pairs={{0,3},{1,0},{2,1},{3,2},{4,7},{5,4},{6,5},{7,6},{8,11},{9,8},{10,9... | collective-permute-start | bytes 393224 | tf_op jit(solution)/shard_map/ppermute | solution.py:602
  18.6 1.3 %shard_map.196.high_ref = bf16[256,256]{1,0:T(8,128)(2,1)S(1)} custom-call(f32[512,256]{1,0:T(8,128)S(1)} %shard_map.194.refs_0_, bf16[320,128]{1,0:T(8,128)(2,1)S(1)} %collective-permute-done.2.refs_1_), custom_call_target="tpu_custom_call" | custom-call | flops 1073741824 | bytes 1048576 | tf_op jit(solution)/shard_map/pallas_call | solution.py:159
  19.9 0.4 collective-permute-start.4
  20.3 0.0 copy-start.2
  20.3 1.8 %shard_map.197 = (bf16[112,144]{1,0:T(8,128)(2,1)S(1)}, bf16[96,1008]{1,0:T(8,128)(2,1)S(1)}, bf16[96,240]{1,0:T(8,128)(2,1)S(1)}, bf16[48,240]{1,0:T(8,128)(2,1...) custom-call(bf16[8,27]{1,0:T(8,128)(2,1)S(1)} %copy-done.9, bf16[8,216]{1,0:T(8,128)(2,1)S(1)} %copy-done.8, ...), custom_call_target="tpu_custom_call" | custom-call | flops 800000000 | bytes 4000000 | tf_op jit(solution)/shard_map/pallas_call | solution.py:266
  22.1 2.4 %collective-permute-done.4.before_ref = bf16[256,256]{1,0:T(8,128)(2,1)S(1)} collective-permute-done((bf16[256,256]{1,0:T(8,128)(2,1)S(1)}, bf16[256,256]{1,0:T(8,128)(2,1)S(1)}, u32[]{:S(2)}, u32[]{:S(2)}) %collective-permute-start.4) | collective-permute-done | bytes 131104 | tf_op jit(solution)/shard_map/ppermute | solution.py:602
  24.6 6.9 %shard_map.198 = (bf16[512,256]{1,0:T(8,128)(2,1)S(1)}, f32[24,256]{1,0:T(8,128)S(1)}) custom-call(bf16[256,256]{1,0:T(8,128)(2,1)S(1)} %shard_map.195.low_ref, bf16[256,256]{1,0:T(8,128)(2,1)S(1)} %shard_map.196.high_ref, bf16[256,256]{1,0:T(8,128)(2,1)S(1)} %collective-permute-done.3.after_ref, bf16[256,256]{1,0:T(8,128)(2,1)S(1)} %collective-permute-done.4.before_ref, ...), custom_call_target="tpu_custom_call" | custom-call | tf_op jit(solution)/shard_map/pallas_call | solution.py:511
  31.4 0.1 collective-permute-start.7
  31.5 1.5 %collective-permute-start.6 = (f32[24,256]{1,0:T(8,128)S(1)}, f32[24,256]{1,0:T(8,128)S(1)}, u32[]{:S(2)}, u32[]{:S(2)}) collective-permute-start(f32[24,256]{1,0:T(8,128)S(1)} %get-tuple-element.43.refs_0_), channel_id=1, source_target_pairs={{0,1},{1,0},{2,3},{3,2},{4,5},{5,4},{6,7},{7,6},{8,9},{9,8},{10,11... | collective-permute-start | bytes 73736 | tf_op jit(solution)/shard_map/ppermute | solution.py:616
  33.0 0.7 %collective-permute-start.5 = (f32[24,256]{1,0:T(8,128)S(1)}, f32[24,256]{1,0:T(8,128)S(1)}, u32[]{:S(2)}, u32[]{:S(2)}) collective-permute-start(f32[24,256]{1,0:T(8,128)S(1)} %get-tuple-element.43.refs_0_), channel_id=1, source_target_pairs={{0,2},{1,3},{2,0},{3,1},{4,6},{5,7},{6,4},{7,5},{8,10},{9,11},{10,... | collective-permute-start | bytes 73736 | tf_op jit(solution)/shard_map/ppermute | solution.py:616
  33.6 3.1 %shard_map.199 = (f32[3,8192]{1,0:T(4,128)}, bf16[64,128]{1,0:T(8,128)(2,1)}) custom-call(f32[1]{0:T(128)S(6)} %copy.21.step_ref, s32[64,128]{1,0:T(8,128)S(1)} %bitcast.5, s32[64,128]{1,0:T(8,128)S(1)} %bitcast.7, f32[3,8192]{1,0:T(4,128)S(1)} %copy-done.6, bf16[512,256]{1,0:T(8,128)(2,1)S(1)} %get-tuple-element.40.mesh_ref), custom_call_target="tpu_custom_call" | custom-call | flops 2147483648 | bytes 1000000 | tf_op jit(solution)/shard_map/pallas_call | solution.py:561
  36.7 0.1 collective-permute-done.5.refs_1_
  36.8 0.6 %shard_map.200 = (f32[8,27]{1,0:T(8,128)}, f32[8,216]{1,0:T(8,128)}, f32[3,216]{1,0:T(4,128)}) custom-call(f32[24,256]{1,0:T(8,128)S(1)} %get-tuple-element.43.refs_0_, f32[24,256]{1,0:T(8,128)S(1)} %collective-permute-done.5.refs_1_, f32[24,256]{1,0:T(8,128)S(1)} %collective-permute-done.6.refs_2_, f32[24,256]{1,0:T(8,128)S(1)} %collective-permute-done.7.refs_3_), custom_call_target="tpu_custom_call" | custom-call | tf_op jit(solution)/shard_map/pallas_call | solution.py:591
  (30 shorter events, 0.1 us)
Async XLA Ops:
  3.1 8.9 %collective-permute-start = (bf16[320,128]{1,0:T(8,128)(2,1)}, bf16[320,128]{1,0:T(8,128)(2,1)S(1)}, u32[]{:S(2)}, u32[]{:S(2)}) collective-permute-start(bf16[320,128]{1,0:T(8,128)(2,1)} %get-tuple-element.27), channel_id=1, source_target_pairs={{0,8},{4,12},{8,0},{12,4},{1,9},{5,13},{9,1},{13,5},{2,10},{6,14},... | collective-permute-start | bytes 245768 | tf_op jit(solution)/shard_map/ppermute | solution.py:616
  7.1 7.3 %collective-permute-start.1 = (bf16[320,128]{1,0:T(8,128)(2,1)}, bf16[320,128]{1,0:T(8,128)(2,1)S(1)}, u32[]{:S(2)}, u32[]{:S(2)}) collective-permute-start(bf16[320,128]{1,0:T(8,128)(2,1)} %get-tuple-element.28), channel_id=1, source_target_pairs={{0,4},{4,0},{8,12},{12,8},{1,5},{5,1},{9,13},{13,9},{2,6},{6,2},{1... | collective-permute-start | bytes 245768 | tf_op jit(solution)/shard_map/ppermute | solution.py:616
  8.7 8.1 %collective-permute-start.2 = (bf16[320,128]{1,0:T(8,128)(2,1)}, bf16[320,128]{1,0:T(8,128)(2,1)S(1)}, u32[]{:S(2)}, u32[]{:S(2)}) collective-permute-start(bf16[320,128]{1,0:T(8,128)(2,1)} %get-tuple-element.29), channel_id=1, source_target_pairs={{0,12},{4,8},{8,4},{12,0},{1,13},{5,9},{9,5},{13,1},{2,14},{6,10},... | collective-permute-start | bytes 245768 | tf_op jit(solution)/shard_map/ppermute | solution.py:616
  8.7 0.9 %copy-start.7 = (bf16[320,128]{1,0:T(8,128)(2,1)S(1)}, bf16[320,128]{1,0:T(8,128)(2,1)}, u32[]{:S(2)}) copy-start(bf16[320,128]{1,0:T(8,128)(2,1)} %get-tuple-element.26.refs_0_) | copy-start | bytes 245764
  18.1 2.2 %copy-start.8 = (bf16[8,216]{1,0:T(8,128)(2,1)S(1)}, bf16[8,216]{1,0:T(8,128)(2,1)}, u32[]{:S(2)}) copy-start(bf16[8,216]{1,0:T(8,128)(2,1)} %middle_ref) | copy-start | bytes 10372
  18.1 2.2 %copy-start.9 = (bf16[8,27]{1,0:T(8,128)(2,1)S(1)}, bf16[8,27]{1,0:T(8,128)(2,1)}, u32[]{:S(2)}) copy-start(bf16[8,27]{1,0:T(8,128)(2,1)} %first_ref) | copy-start | bytes 1300
  18.1 2.2 %copy-start.10 = (bf16[3,216]{1,0:T(4,128)(2,1)S(1)}, bf16[3,216]{1,0:T(4,128)(2,1)}, u32[]{:S(2)}) copy-start(bf16[3,216]{1,0:T(4,128)(2,1)} %last_ref) | copy-start | bytes 3892
  18.1 2.1 %copy-start.11 = (s32[8,1008]{1,0:T(8,128)S(1)}, s32[8,1008]{1,0:T(8,128)}, u32[]{:S(2)}) copy-start(s32[8,1008]{1,0:T(8,128)} %constant.15.clone.c2_ref) | copy-start | bytes 96772
  18.1 2.1 %copy-start.12 = (s32[8,864]{1,0:T(8,128)S(1)}, s32[8,864]{1,0:T(8,128)}, u32[]{:S(2)}) copy-start(s32[8,864]{1,0:T(8,128)} %constant.16.clone.c3_ref) | copy-start | bytes 82948
  18.1 2.1 %copy-start.13 = (s32[8,144]{1,0:T(8,128)S(1)}, s32[8,144]{1,0:T(8,128)}, u32[]{:S(2)}) copy-start(s32[8,144]{1,0:T(8,128)} %constant.14.clone.c1_ref) | copy-start | bytes 13828
  18.2 4.0 %collective-permute-start.3 = (bf16[256,256]{1,0:T(8,128)(2,1)S(1)}, bf16[256,256]{1,0:T(8,128)(2,1)S(1)}, u32[]{:S(2)}, u32[]{:S(2)}) collective-permute-start(bf16[256,256]{1,0:T(8,128)(2,1)S(1)} %shard_map.195.low_ref), channel_id=1, source_target_pairs={{0,3},{1,0},{2,1},{3,2},{4,7},{5,4},{6,5},{7,6},{8,11},{9,8},{10,9... | collective-permute-start | bytes 393224 | tf_op jit(solution)/shard_map/ppermute | solution.py:602
  19.9 4.6 %collective-permute-start.4 = (bf16[256,256]{1,0:T(8,128)(2,1)S(1)}, bf16[256,256]{1,0:T(8,128)(2,1)S(1)}, u32[]{:S(2)}, u32[]{:S(2)}) collective-permute-start(bf16[256,256]{1,0:T(8,128)(2,1)S(1)} %shard_map.196.high_ref), channel_id=1, source_target_pairs={{0,1},{1,2},{2,3},{3,0},{4,5},{5,6},{6,7},{7,4},{8,9},{9,10},{10,1... | collective-permute-start | bytes 393224 | tf_op jit(solution)/shard_map/ppermute | solution.py:602
  20.3 4.2 %copy-start.2 = (bf16[64,64]{1,0:T(8,128)(2,1)S(1)}, bf16[64,64]{1,0:T(8,128)(2,1)}, u32[]{:S(2)}) copy-start(bf16[64,64]{1,0:T(8,128)(2,1)} %constant.20.clone.order_ref) | copy-start | bytes 24580
  20.3 4.2 %copy-start.3 = (s32[8,336]{1,0:T(8,128)S(1)}, s32[8,336]{1,0:T(8,128)}, u32[]{:S(2)}) copy-start(s32[8,336]{1,0:T(8,128)} %constant.18.clone.c2_ref) | copy-start | bytes 32260
  20.3 4.2 %copy-start.5 = (s32[8,48]{1,0:T(8,128)S(1)}, s32[8,48]{1,0:T(8,128)}, u32[]{:S(2)}) copy-start(s32[8,48]{1,0:T(8,128)} %constant.17.clone.c1_ref) | copy-start | bytes 4612
  22.1 2.4 %copy-start.4 = (s32[8,240]{1,0:T(8,128)S(1)}, s32[8,240]{1,0:T(8,128)}, u32[]{:S(2)}) copy-start(s32[8,240]{1,0:T(8,128)} %constant.19.clone.c3_ref) | copy-start | bytes 23044
  24.5 9.1 %copy-start = (s32[8192,1]{0,1:T(1,128)S(1)}, s32[8192,1]{0,1:T(1,128)}, u32[]{:S(2)}) copy-start(s32[8192,1]{0,1:T(1,128)} %param.18) | copy-start | bytes 98308
  24.5 9.1 %copy-start.1 = (s32[8192]{0:T(1024)S(1)}, s32[8192]{0:T(1024)}, u32[]{:S(2)}) copy-start(s32[8192]{0:T(1024)} %param.19) | copy-start | bytes 98308
  24.6 9.1 %copy-start.6 = (f32[3,8192]{1,0:T(4,128)S(1)}, f32[3,8192]{1,0:T(4,128)}, u32[]{:S(2)}) copy-start(f32[3,8192]{1,0:T(4,128)} %velocity_ref.1) | copy-start | bytes 294916
  31.4 5.3 %collective-permute-start.7 = (f32[24,256]{1,0:T(8,128)S(1)}, f32[24,256]{1,0:T(8,128)S(1)}, u32[]{:S(2)}, u32[]{:S(2)}) collective-permute-start(f32[24,256]{1,0:T(8,128)S(1)} %get-tuple-element.43.refs_0_), channel_id=1, source_target_pairs={{0,3},{1,2},{2,1},{3,0},{4,7},{5,6},{6,5},{7,4},{8,11},{9,10},{10,... | collective-permute-start | bytes 73736 | tf_op jit(solution)/shard_map/ppermute | solution.py:616
  31.5 5.2 %collective-permute-start.6 = (f32[24,256]{1,0:T(8,128)S(1)}, f32[24,256]{1,0:T(8,128)S(1)}, u32[]{:S(2)}, u32[]{:S(2)}) collective-permute-start(f32[24,256]{1,0:T(8,128)S(1)} %get-tuple-element.43.refs_0_), channel_id=1, source_target_pairs={{0,1},{1,0},{2,3},{3,2},{4,5},{5,4},{6,7},{7,6},{8,9},{9,8},{10,11... | collective-permute-start | bytes 73736 | tf_op jit(solution)/shard_map/ppermute | solution.py:616
  33.0 3.8 %collective-permute-start.5 = (f32[24,256]{1,0:T(8,128)S(1)}, f32[24,256]{1,0:T(8,128)S(1)}, u32[]{:S(2)}, u32[]{:S(2)}) collective-permute-start(f32[24,256]{1,0:T(8,128)S(1)} %get-tuple-element.43.refs_0_), channel_id=1, source_target_pairs={{0,2},{1,3},{2,0},{3,1},{4,6},{5,7},{6,4},{7,5},{8,10},{9,11},{10,... | collective-permute-start | bytes 73736 | tf_op jit(solution)/shard_map/ppermute | solution.py:616
